TPU v7x, 32 devices: a whole 2x2x4 slice. The times are simulated.
32 devices in a mesh: ref: 8 (over y, x, core), img: 4 (over z).
Axes of the slice: x: 2, y: 2, z: 4, core: 2. Of those that a mesh axis runs over, the one named last changes fastest.
Arguments:
- images: bfloat16 [4096, 4096], P(('img', 'ref')), may hold values from -6 to 6
- exponents: int32 [4096], P('img'), may hold values from 0 to 8
- references: bfloat16 [6144, 4096], P('ref'), may hold values from -8 to 8
- partners: int32 [6144], P('ref'), may hold values from 0 to 6143, as said below
Outputs:
- symmetric_sums: float32 [6144, 4096], P('ref', 'img')
Inputs may be any that keep to these rules, and one draw needn't show every extreme that they name: partners is an involution without fixed points; partners[r] lies in the block of 768 references that starts 6144 / 2 references after or before the start of r's block.
All inputs are finite; a program needn't handle non-finite values.
Results may differ from a plain program's by a relative error of at most 0.0033.
Values may be sent and summed in bfloat16 or wider, within the bound.
No kernel may reach another device: no remote copies, remote signals or barrier semaphores. Data moves between devices by JAX's collectives and lax.ppermute only.
A program may use at most 64 MiB of HBM per device.

v0:
```python
import jax
import jax.numpy as jnp
from jax import lax
from jax.sharding import PartitionSpec as P

F32 = jnp.float32
BF16 = jnp.bfloat16
ROW_CHUNKS = (8, 7, 5, 4)
FORWARD_LOW = 10


def swap(block, axis, bit):
    count = lax.axis_size(axis)
    return lax.ppermute(block, axis, [(i, i ^ bit) for i in range(count)])


def after(array, *others):
    return lax.optimization_barrier((array, *others))[0]


def halves(part, axis, bit):
    n = lax.axis_size(axis)
    side = lax.axis_index(axis) // bit % 2
    blocks = n // bit
    width = part.shape[1] // blocks

    def of_side(s):
        cut = [lax.dynamic_slice_in_dim(part, (2 * j + s) * width, width, axis=1) for j in range(blocks // 2)]
        return jnp.concatenate(cut, axis=1)

    return of_side(side), of_side(1 - side).astype(BF16)


def body(images, exponents, references, partners):
    rows, width = references.shape
    half = rows // 2
    count = lax.axis_size("ref")
    me = lax.axis_index("ref")
    img_rows = images.shape[0]
    total_images = img_rows * count * lax.axis_size("img")
    top = count // 2
    upper = me // top

    pieces = {0: [images]}
    for k in reversed(range(2, count, 2)):
        if k & (k - 1) == 0:
            pieces[k] = [swap(images, "ref", k)]
    pieces[1] = [swap(images, "ref", 1)]

    own_order = jnp.arange(rows, dtype=jnp.int32)
    place = jnp.where(upper == 0, own_order, partners % rows)
    place = (place + upper * half) % rows
    one_hot = (own_order[:, None] == place[None, :]).astype(BF16)
    refs = jnp.dot(one_hot, references, preferred_element_type=F32).astype(BF16)
    norms = jnp.sum(jnp.square(refs.astype(F32)), axis=1) / width
    inv_root = 1.0 / jnp.sqrt(F32(width))
    offsets = exponents.reshape(count, img_rows)[me ^ jnp.arange(count)].astype(F32) * 0.25

    apart = top // 2
    blocks = count // 2
    end = blocks - 1
    weights, sent = {}, {}

    def images_of(ms):
        return jnp.concatenate([part for m in ms for k in (2 * m, 2 * m + 1) for part in pieces[k]], axis=0)

    def score(m):
        scores = lax.dot_general(refs, images_of([m]), (((1,), (1,)), ((), ())), preferred_element_type=F32) * inv_root
        scores = scores - 0.5 * norms[:, None] - offsets[2 * m : 2 * m + 2].reshape(1, 2 * img_rows)
        weights[m] = jnp.exp(scores).astype(BF16)

    unit = half // sum(ROW_CHUNKS)
    ends = [0]
    for size in ROW_CHUNKS:
        ends.append(ends[-1] + size * unit)
    chunks = [slice(*pair) for pair in zip(ends, ends[1:])]

    early = ends[1]
    parted = [m for m in range(blocks) if m != apart]

    def send(m, start, stop, *before):
        part = weights[m][half + start : half + stop]
        sent.setdefault(m ^ apart, []).append(swap(after(part, *before) if before else part, "ref", top))

    def mean(m, at):
        theirs = sent[m][0][at]
        if m in parted and at.start >= early:
            theirs = sent[m][1][at.start - early : at.stop - early]
        return (0.5 * weights[m][at].astype(F32) + 0.5 * theirs.astype(F32)).astype(BF16)

    score(0)
    singles = [k for k in reversed(range(2, count, 2)) if k & (k - 1) == 0]
    for k in singles:
        pieces[k] = [after(pieces[k][0], weights[0], *(pieces[2 * k + 1] if k != singles[0] else []))]
        pieces[k + 1] = [swap(pieces[k][0], "ref", 1)]
    cut = img_rows * FORWARD_LOW // 16
    for k in range(2, count, 2):
        if k not in singles:
            low, high = k & -k, 1 << (k.bit_length() - 1)
            whole = [jnp.concatenate(pieces[k ^ bit], axis=0) for bit in (low, high)]
            pieces[k] = [swap(whole[0][:cut], "ref", low), swap(whole[1][cut:], "ref", high)]
        if k + 1 not in pieces and k != 2 * end:
            pieces[k + 1] = [swap(part, "ref", 1) for part in pieces[k]]
    send(0, 0, half, *pieces[3])
    for m in reversed(range(1, end)):
        score(m)
        if m != 1:
            send(m, 0, early, *(pieces[3] if m == apart else []))
    pieces[2 * end] = [after(part, *weights.values()) for part in pieces[2 * end]]
    pieces[2 * end + 1] = [swap(part, "ref", 1) for part in pieces[2 * end]]
    send(1, 0, early, pieces[2 * end + 1][-1])
    score(end)
    sent = {m: [after(part, weights[end]) for part in parts] for m, parts in sent.items()}
    send(end, 0, early)

    order = range(blocks)
    every_image = images_of(order)
    scale = 1.0 / jnp.sqrt(F32(total_images))
    def onward(pair, block, bit, before):
        total = pair[0] + after(block, *before).astype(F32)
        return halves(total, "img", bit) if bit < lax.axis_size("img") else (total, total.astype(BF16))

    first, came, pairs = [], [], []
    for c, at in enumerate(chunks):
        w = jnp.concatenate([mean(m, at) for m in order], axis=1)
        w = after(w, *[give for keep, give in first[-1:] + (pairs[-1:] if 1 < c < len(chunks) - 1 else [])])
        first.append(halves(jnp.dot(w, every_image, preferred_element_type=F32) * scale, "img", 1))
        came.append(swap(first[c][1], "img", 1))
        if c == 0:
            for m in parted:
                send(m ^ apart, early, half, first[0][1])
        if c:
            pairs.append(onward(first[c - 1], came[c - 1], 2, [give for keep, give in pairs[-1:]]))
    pairs.append(onward(first[-1], came[-1], 2, [pairs[-1][1]]))
    bit = 2
    while bit < lax.axis_size("img"):
        came = [swap(give, "img", bit) for keep, give in pairs]
        bit *= 2
        after_it = []
        for pair, block in zip(pairs, came):
            after_it.append(onward(pair, block, bit, [give for keep, give in after_it[-1:] + pairs[-1:]]))
        pairs = after_it
    done = [keep for keep, give in pairs]
    gone = [give for keep, give in pairs]
    other = [swap(block, "ref", top).astype(F32) for block in gone]
    return jnp.concatenate(done + other, axis=0).at[place].get(mode="promise_in_bounds")


def solution(mesh):
    in_specs = (P(("img", "ref"), None), P("img"), P("ref", None), P("ref"))
    out_specs = P("ref", "img")
    return jax.shard_map(body, mesh=mesh, in_specs=in_specs, out_specs=out_specs, check_vma=False)
```

profile of v0, /device:TPU:0, one launch (start us, length us, event | category | flops | bytes accessed | tf_op | source)
XLA Modules:
  0.0 125.5 jit_solution(3249685470686858638)
XLA Ops:
  0.0 3.0 %collective-permute-start.1 = (bf16[128,4096]{1,0:T(8,128)(2,1)}, bf16[128,4096]{1,0:T(8,128)(2,1)S(1)}, u32[]{:S(2)}, u32[]{:S(2)}) collective-permute-start(bf16[128,4096]{1,0:T(8,128)(2,1)} %param.4), channel_id=1, source_target_pairs={{0,16},{4,20},{8,24},{12,28},{16,0},{20,4},{24,8},{28,12},{1,17},{... | collective-permute-start | bytes 3145736 | tf_op jit(solution)/shard_map/ppermute | solution.py:14
  5.2 9.9 %multiply_reduce_fusion = (f32[768]{0:T(1024)S(1)}, bf16[768,4096]{1,0:T(8,128)(2,1)}) fusion(bf16[768,4096]{1,0:T(8,128)(2,1)} %param.6, s32[768]{0:T(1024)S(1)} %get-tuple-element.52), kind=kOutput, calls=%fused_computation.2 | convolution fusion | flops 4845009920 | bytes 12589056 | tf_op jit(solution)/shard_map/dot_general | solution.py:54
  15.8 5.0 %fusion.74 = bf16[768,256]{1,0:T(8,128)(2,1)S(1)} fusion(bf16[768,4096]{1,0:T(8,128)(2,1)} %get-tuple-element.82, bf16[128,4096]{1,0:T(8,128)(2,1)} %collective-permute-done, bf16[128,4096]{1,0:T(8,128)(2,1)S(1)} %copy-done.1, f32[256]{0:T(256)S(1)} %get-tuple-element.80, f32[768]{0:T(1024)S(1)} %broadcast_multiply_fusion), kind=kOutput, calls=%fused_computation.47 | convolution fusion | flops 1615593472 | bytes 8785920 | tf_op jit(solution)/shard_map/dot_general | solution.py:68
  20.8 5.6 %collective-permute-done.1 = bf16[128,4096]{1,0:T(8,128)(2,1)S(1)} collective-permute-done((bf16[128,4096]{1,0:T(8,128)(2,1)}, bf16[128,4096]{1,0:T(8,128)(2,1)S(1)}, u32[]{:S(2)}, u32[]{:S(2)}) %collective-permute-start.1) | collective-permute-done | bytes 1048608 | tf_op jit(solution)/shard_map/ppermute | solution.py:14
  26.5 1.8 %collective-permute-start.6 = (bf16[80,4096]{1,0:T(8,128)(2,1)S(1)}, bf16[80,4096]{1,0:T(8,128)(2,1)S(1)}, u32[]{:S(2)}, u32[]{:S(2)}) collective-permute-start(bf16[80,4096]{1,0:T(8,128)(2,1)S(1)} %slice.130), channel_id=1, source_target_pairs={{0,8},{4,12},{8,0},{12,4},{16,24},{20,28},{24,16},{28,20},{1,9},{5... | collective-permute-start | bytes 1966088 | tf_op jit(solution)/shard_map/ppermute | solution.py:14
  29.9 2.0 %fusion.71 = bf16[768,256]{1,0:T(8,128)(2,1)S(1)} fusion(bf16[768,4096]{1,0:T(8,128)(2,1)S(1)} %bitcast.26, bf16[128,4096]{1,0:T(8,128)(2,1)S(1)} %collective-permute-done.2, bf16[128,4096]{1,0:T(8,128)(2,1)S(1)} %collective-permute-done.1, f32[256]{0:T(256)S(1)} %get-tuple-element.79, f32[768]{0:T(1024)S(1)} %broadcast_multiply_fusion), kind=kOutput, calls=%fused_computation.46 | convolution fusion | flops 1615593472 | bytes 8785920 | tf_op jit(solution)/shard_map/dot_general | solution.py:68
  32.1 1.6 %collective-permute-start.7 = (bf16[48,4096]{1,0:T(8,128)(2,1)S(1)}, bf16[48,4096]{1,0:T(8,128)(2,1)S(1)}, u32[]{:S(2)}, u32[]{:S(2)}) collective-permute-start(bf16[48,4096]{1,0:T(8,128)(2,1)S(1)} %slice.132), channel_id=1, source_target_pairs={{0,16},{4,20},{8,24},{12,28},{16,0},{20,4},{24,8},{28,12},{1,17},{... | collective-permute-start | bytes 1179656 | tf_op jit(solution)/shard_map/ppermute | solution.py:14
  33.7 2.0 %fusion.68 = bf16[768,256]{1,0:T(8,128)(2,1)S(1)} fusion(bf16[768,4096]{1,0:T(8,128)(2,1)S(1)} %bitcast.26, bf16[128,4096]{1,0:T(8,128)(2,1)S(1)} %collective-permute-done.4, bf16[128,4096]{1,0:T(8,128)(2,1)S(1)} %collective-permute-done.3, f32[256]{0:T(256)S(1)} %get-tuple-element.78, f32[768]{0:T(1024)S(1)} %broadcast_multiply_fusion), kind=kOutput, calls=%fused_computation.45 | convolution fusion | flops 1615593472 | bytes 8785920 | tf_op jit(solution)/shard_map/dot_general | solution.py:68
  36.3 1.5 %collective-permute-start.11 = (bf16[384,256]{1,0:T(8,128)(2,1)S(1)}, bf16[384,256]{1,0:T(8,128)(2,1)S(1)}, u32[]{:S(2)}, u32[]{:S(2)}) collective-permute-start(bf16[384,256]{1,0:T(8,128)(2,1)S(1)} %slice.177), channel_id=1, source_target_pairs={{0,16},{4,20},{8,24},{12,28},{16,0},{20,4},{24,8},{28,12},{1,17},{... | collective-permute-start | bytes 589832 | tf_op jit(solution)/shard_map/ppermute | solution.py:14
  37.8 6.3 %collective-permute-done.7 = bf16[48,4096]{1,0:T(8,128)(2,1)S(1)} collective-permute-done((bf16[48,4096]{1,0:T(8,128)(2,1)S(1)}, bf16[48,4096]{1,0:T(8,128)(2,1)S(1)}, u32[]{:S(2)}, u32[]{:S(2)}) %collective-permute-start.7) | collective-permute-done | bytes 393248 | tf_op jit(solution)/shard_map/ppermute | solution.py:14
  45.8 1.5 %collective-permute-start.12 = (bf16[128,256]{1,0:T(8,128)(2,1)S(1)}, bf16[128,256]{1,0:T(8,128)(2,1)S(1)}, u32[]{:S(2)}, u32[]{:S(2)}) collective-permute-start(bf16[128,256]{1,0:T(8,128)(2,1)S(1)} %slice.179), channel_id=1, source_target_pairs={{0,16},{4,20},{8,24},{12,28},{16,0},{20,4},{24,8},{28,12},{1,17},{... | collective-permute-start | bytes 196616 | tf_op jit(solution)/shard_map/ppermute | solution.py:14
  47.3 1.8 %fusion.77 = bf16[768,256]{1,0:T(8,128)(2,1)S(1)} fusion(bf16[768,4096]{1,0:T(8,128)(2,1)S(1)} %bitcast.26, bf16[48,4096]{1,0:T(8,128)(2,1)S(1)} %collective-permute-done.9, bf16[80,4096]{1,0:T(8,128)(2,1)S(1)} %collective-permute-done.8, bf16[48,4096]{1,0:T(8,128)(2,1)S(1)} %collective-permute-done.7, bf16[80,4096]{1,0:T(8,128)(2,1)S(1)} %collective-permute-done.6, ...), kind=kOutput, calls=%fused_computation.48 | convolution fusion | flops 1619787776 | bytes 8785920 | tf_op jit(solution)/shard_map/dot_general | solution.py:68
  50.5 1.6 %collective-permute-start.10 = (bf16[128,256]{1,0:T(8,128)(2,1)S(1)}, bf16[128,256]{1,0:T(8,128)(2,1)S(1)}, u32[]{:S(2)}, u32[]{:S(2)}) collective-permute-start(bf16[128,256]{1,0:T(8,128)(2,1)S(1)} %slice.175), channel_id=1, source_target_pairs={{0,16},{4,20},{8,24},{12,28},{16,0},{20,4},{24,8},{28,12},{1,17},{... | collective-permute-start | bytes 196616 | tf_op jit(solution)/shard_map/ppermute | solution.py:14
  52.3 2.6 %collective-permute-done.10 = bf16[128,256]{1,0:T(8,128)(2,1)S(1)} collective-permute-done((bf16[128,256]{1,0:T(8,128)(2,1)S(1)}, bf16[128,256]{1,0:T(8,128)(2,1)S(1)}, u32[]{:S(2)}, u32[]{:S(2)}) %collective-permute-start.10) | collective-permute-done | bytes 65568 | tf_op jit(solution)/shard_map/ppermute | solution.py:14
  56.4 1.6 %collective-permute-start.13 = (bf16[128,2048]{1,0:T(8,128)(2,1)S(1)}, bf16[128,2048]{1,0:T(8,128)(2,1)S(1)}, u32[]{:S(2)}, u32[]{:S(2)}) collective-permute-start(bf16[128,2048]{1,0:T(8,128)(2,1)S(1)} %pad_maximum_fusion), channel_id=1, source_target_pairs={{0,1},{1,0},{2,3},{3,2},{4,5},{5,4},{6,7},{7,6},{8,9},{9,8},{10,11... | collective-permute-start | bytes 1572872 | tf_op jit(solution)/shard_map/ppermute | solution.py:14
  58.0 1.5 %collective-permute-start.15 = (bf16[256,256]{1,0:T(8,128)(2,1)S(1)}, bf16[256,256]{1,0:T(8,128)(2,1)S(1)}, u32[]{:S(2)}, u32[]{:S(2)}) collective-permute-start(bf16[256,256]{1,0:T(8,128)(2,1)S(1)} %slice.181), channel_id=1, source_target_pairs={{0,16},{4,20},{8,24},{12,28},{16,0},{20,4},{24,8},{28,12},{1,17},{... | collective-permute-start | bytes 393224 | tf_op jit(solution)/shard_map/ppermute | solution.py:14
  61.7 2.8 %collective-permute-done.15 = bf16[256,256]{1,0:T(8,128)(2,1)S(1)} collective-permute-done((bf16[256,256]{1,0:T(8,128)(2,1)S(1)}, bf16[256,256]{1,0:T(8,128)(2,1)S(1)}, u32[]{:S(2)}, u32[]{:S(2)}) %collective-permute-start.15) | collective-permute-done | bytes 131104 | tf_op jit(solution)/shard_map/ppermute | solution.py:14
  70.1 2.7 %collective-permute-start.14 = (bf16[128,1024]{1,0:T(8,128)(2,1)S(1)}, bf16[128,1024]{1,0:T(8,128)(2,1)S(1)}, u32[]{:S(2)}, u32[]{:S(2)}) collective-permute-start(bf16[128,1024]{1,0:T(8,128)(2,1)S(1)} %dynamic-slice_convert_fusion), channel_id=1, source_target_pairs={{0,2},{1,3},{2,0},{3,1},{4,6},{5,7},{6,4},{7,5},{8,10},{9,11},{10,... | collective-permute-start | bytes 786440 | tf_op jit(solution)/shard_map/ppermute | solution.py:14
  72.7 1.6 %convolution_multiply_fusion.2 = f32[80,4096]{1,0:T(8,128)S(1)} fusion(bf16[80,1024]{1,0:T(8,128)(2,1)S(1)} %pad_maximum_fusion.6, bf16[1024,4096]{1,0:T(8,128)(2,1)S(1)} %constant_dynamic-update-slice_fusion), kind=kOutput, calls=%fused_computation.6 | convolution fusion | flops 671416320 | bytes 9863168 | tf_op jit(solution)/shard_map/dot_general | solution.py:127
  74.4 1.6 %collective-permute-start.19 = (bf16[80,2048]{1,0:T(8,128)(2,1)S(1)}, bf16[80,2048]{1,0:T(8,128)(2,1)S(1)}, u32[]{:S(2)}, u32[]{:S(2)}) collective-permute-start(bf16[80,2048]{1,0:T(8,128)(2,1)S(1)} %pad_maximum_fusion.2), channel_id=1, source_target_pairs={{0,1},{1,0},{2,3},{3,2},{4,5},{5,4},{6,7},{7,6},{8,9},{9,8},{10,11... | collective-permute-start | bytes 983048 | tf_op jit(solution)/shard_map/ppermute | solution.py:14
  76.0 1.6 %convolution_multiply_fusion.3 = f32[64,4096]{1,0:T(8,128)S(1)} fusion(bf16[64,1024]{1,0:T(8,128)(2,1)S(1)} %pad_maximum_fusion.7, bf16[1024,4096]{1,0:T(8,128)(2,1)S(1)} %constant_dynamic-update-slice_fusion), kind=kOutput, calls=%fused_computation.7 | convolution fusion | flops 537133056 | bytes 9568256 | tf_op jit(solution)/shard_map/dot_general | solution.py:127
  78.3 8.1 %collective-permute-done.20 = bf16[112,2048]{1,0:T(8,128)(2,1)S(1)} collective-permute-done((bf16[112,2048]{1,0:T(8,128)(2,1)S(1)}, bf16[112,2048]{1,0:T(8,128)(2,1)S(1)}, u32[]{:S(2)}, u32[]{:S(2)}) %collective-permute-start.20) | collective-permute-done | bytes 458784 | tf_op jit(solution)/shard_map/ppermute | solution.py:14
  86.5 1.6 %collective-permute-start.21 = (bf16[112,1024]{1,0:T(8,128)(2,1)S(1)}, bf16[112,1024]{1,0:T(8,128)(2,1)S(1)}, u32[]{:S(2)}, u32[]{:S(2)}) collective-permute-start(bf16[112,1024]{1,0:T(8,128)(2,1)S(1)} %dynamic-slice_convert_fusion.3), channel_id=1, source_target_pairs={{0,2},{1,3},{2,0},{3,1},{4,6},{5,7},{6,4},{7,5},{8,10},{9,11},{10,... | collective-permute-start | bytes 688136 | tf_op jit(solution)/shard_map/ppermute | solution.py:14
  88.1 10.2 %collective-permute-done.19 = bf16[80,2048]{1,0:T(8,128)(2,1)S(1)} collective-permute-done((bf16[80,2048]{1,0:T(8,128)(2,1)S(1)}, bf16[80,2048]{1,0:T(8,128)(2,1)S(1)}, u32[]{:S(2)}, u32[]{:S(2)}) %collective-permute-start.19) | collective-permute-done | bytes 327712 | tf_op jit(solution)/shard_map/ppermute | solution.py:14
  98.5 1.5 %collective-permute-start.22 = (bf16[80,1024]{1,0:T(8,128)(2,1)S(1)}, bf16[80,1024]{1,0:T(8,128)(2,1)S(1)}, u32[]{:S(2)}, u32[]{:S(2)}) collective-permute-start(bf16[80,1024]{1,0:T(8,128)(2,1)S(1)} %dynamic-slice_convert_fusion.6), channel_id=1, source_target_pairs={{0,2},{1,3},{2,0},{3,1},{4,6},{5,7},{6,4},{7,5},{8,10},{9,11},{10,... | collective-permute-start | bytes 491528 | tf_op jit(solution)/shard_map/ppermute | solution.py:14
  100.0 3.6 %collective-permute-done.18 = bf16[64,2048]{1,0:T(8,128)(2,1)S(1)} collective-permute-done((bf16[64,2048]{1,0:T(8,128)(2,1)S(1)}, bf16[64,2048]{1,0:T(8,128)(2,1)S(1)}, u32[]{:S(2)}, u32[]{:S(2)}) %collective-permute-start.18) | collective-permute-done | bytes 262176 | tf_op jit(solution)/shard_map/ppermute | solution.py:14
  104.5 1.6 %collective-permute-start.24 = (bf16[128,1024]{1,0:T(8,128)(2,1)S(1)}, bf16[128,1024]{1,0:T(8,128)(2,1)S(1)}, u32[]{:S(2)}, u32[]{:S(2)}) collective-permute-start(bf16[128,1024]{1,0:T(8,128)(2,1)S(1)} %get-tuple-element.61), channel_id=1, source_target_pairs={{0,16},{4,20},{8,24},{12,28},{16,0},{20,4},{24,8},{28,12},{1,17},{... | collective-permute-start | bytes 786440 | tf_op jit(solution)/shard_map/ppermute | solution.py:14
  106.7 6.6 %collective-permute-done.22 = bf16[80,1024]{1,0:T(8,128)(2,1)S(1)} collective-permute-done((bf16[80,1024]{1,0:T(8,128)(2,1)S(1)}, bf16[80,1024]{1,0:T(8,128)(2,1)S(1)}, u32[]{:S(2)}, u32[]{:S(2)}) %collective-permute-start.22) | collective-permute-done | bytes 163872 | tf_op jit(solution)/shard_map/ppermute | solution.py:14
  113.4 1.6 %collective-permute-start.26 = (bf16[80,1024]{1,0:T(8,128)(2,1)S(1)}, bf16[80,1024]{1,0:T(8,128)(2,1)S(1)}, u32[]{:S(2)}, u32[]{:S(2)}) collective-permute-start(bf16[80,1024]{1,0:T(8,128)(2,1)S(1)} %get-tuple-element.73), channel_id=1, source_target_pairs={{0,16},{4,20},{8,24},{12,28},{16,0},{20,4},{24,8},{28,12},{1,17},{... | collective-permute-start | bytes 491528 | tf_op jit(solution)/shard_map/ppermute | solution.py:14
  116.4 2.2 %collective-permute-done.25 = bf16[112,1024]{1,0:T(8,128)(2,1)S(1)} collective-permute-done((bf16[112,1024]{1,0:T(8,128)(2,1)S(1)}, bf16[112,1024]{1,0:T(8,128)(2,1)S(1)}, u32[]{:S(2)}, u32[]{:S(2)}) %collective-permute-start.25) | collective-permute-done | bytes 229408 | tf_op jit(solution)/shard_map/ppermute | solution.py:14
  118.6 1.8 %collective-permute-done.26 = bf16[80,1024]{1,0:T(8,128)(2,1)S(1)} collective-permute-done((bf16[80,1024]{1,0:T(8,128)(2,1)S(1)}, bf16[80,1024]{1,0:T(8,128)(2,1)S(1)}, u32[]{:S(2)}, u32[]{:S(2)}) %collective-permute-start.26) | collective-permute-done | bytes 163872 | tf_op jit(solution)/shard_map/ppermute | solution.py:14
  121.8 3.6 %gather_fusion.1 = f32[768,1024]{1,0:T(8,128)} fusion(f32[768,1024]{1,0:T(8,128)S(1)} %convert_dynamic-update-slice_fusion.3, s32[1024]{0:T(1024)S(1)} %pad_clamp_fusion), kind=kCustom, calls=%fused_computation.1 | custom fusion | bytes 6294528 | tf_op jit(solution)/shard_map/gather | solution.py:146
  (117 shorter events, 22.8 us)
Async XLA Ops:
  0.0 15.1 %copy-start = (s32[1024]{0:T(1024)S(1)}, s32[1024]{0:T(1024)}, u32[]{:S(2)}) copy-start(s32[1024]{0:T(1024)} %param.5) | copy-start | bytes 12292
  0.0 26.3 %collective-permute-start.1 = (bf16[128,4096]{1,0:T(8,128)(2,1)}, bf16[128,4096]{1,0:T(8,128)(2,1)S(1)}, u32[]{:S(2)}, u32[]{:S(2)}) collective-permute-start(bf16[128,4096]{1,0:T(8,128)(2,1)} %param.4), channel_id=1, source_target_pairs={{0,16},{4,20},{8,24},{12,28},{16,0},{20,4},{24,8},{28,12},{1,17},{... | collective-permute-start | bytes 3145736 | tf_op jit(solution)/shard_map/ppermute | solution.py:14
  3.0 12.7 %collective-permute-start = (bf16[128,4096]{1,0:T(8,128)(2,1)}, bf16[128,4096]{1,0:T(8,128)(2,1)}, u32[]{:S(2)}, u32[]{:S(2)}) collective-permute-start(bf16[128,4096]{1,0:T(8,128)(2,1)} %param.4), channel_id=1, source_target_pairs={{0,4},{4,0},{8,12},{12,8},{16,20},{20,16},{24,28},{28,24},{1,5},{5... | collective-permute-start | bytes 3145736 | tf_op jit(solution)/shard_map/ppermute | solution.py:14
  3.0 26.6 %collective-permute-start.3 = (bf16[128,4096]{1,0:T(8,128)(2,1)}, bf16[128,4096]{1,0:T(8,128)(2,1)S(1)}, u32[]{:S(2)}, u32[]{:S(2)}) collective-permute-start(bf16[128,4096]{1,0:T(8,128)(2,1)} %param.4), channel_id=1, source_target_pairs={{0,8},{4,12},{8,0},{12,4},{16,24},{20,28},{24,16},{28,20},{1,9},{5... | collective-permute-start | bytes 3145736 | tf_op jit(solution)/shard_map/ppermute | solution.py:14
  5.2 10.6 %copy-start.1 = (bf16[128,4096]{1,0:T(8,128)(2,1)S(1)}, bf16[128,4096]{1,0:T(8,128)(2,1)}, u32[]{:S(2)}) copy-start(bf16[128,4096]{1,0:T(8,128)(2,1)} %param.4) | copy-start | bytes 3145732
  15.7 14.2 %slice-start = ((s8[6291456]{0:T(1024)(128)(4,1)}), s8[4194304]{0:T(1024)(128)(4,1)S(1)}, s32[]{:S(2)}) async-start(s8[6291456]{0:T(1024)(128)(4,1)} %bitcast.25), calls=%async_computation | async-start | bytes 8388608
  15.7 14.2 %slice-start.1 = ((s8[6291456]{0:T(1024)(128)(4,1)}), s8[2097152]{0:T(1024)(128)(4,1)S(1)}, s32[]{:S(2)}) async-start(s8[6291456]{0:T(1024)(128)(4,1)} %bitcast.25), calls=%async_computation.1 | async-start | bytes 4194304
  26.3 3.3 %collective-permute-start.2 = (bf16[128,4096]{1,0:T(8,128)(2,1)S(1)}, bf16[128,4096]{1,0:T(8,128)(2,1)S(1)}, u32[]{:S(2)}, u32[]{:S(2)}) collective-permute-start(bf16[128,4096]{1,0:T(8,128)(2,1)S(1)} %collective-permute-done.1), channel_id=1, source_target_pairs={{0,4},{4,0},{8,12},{12,8},{16,20},{20,16},{24,28},{28,24},{1,5},{5... | collective-permute-start | bytes 3145736 | tf_op jit(solution)/shard_map/ppermute | solution.py:14
  26.5 17.6 %collective-permute-start.6 = (bf16[80,4096]{1,0:T(8,128)(2,1)S(1)}, bf16[80,4096]{1,0:T(8,128)(2,1)S(1)}, u32[]{:S(2)}, u32[]{:S(2)}) collective-permute-start(bf16[80,4096]{1,0:T(8,128)(2,1)S(1)} %slice.130), channel_id=1, source_target_pairs={{0,8},{4,12},{8,0},{12,4},{16,24},{20,28},{24,16},{28,20},{1,9},{5... | collective-permute-start | bytes 1966088 | tf_op jit(solution)/shard_map/ppermute | solution.py:14
  29.6 4.1 %collective-permute-start.4 = (bf16[128,4096]{1,0:T(8,128)(2,1)S(1)}, bf16[128,4096]{1,0:T(8,128)(2,1)S(1)}, u32[]{:S(2)}, u32[]{:S(2)}) collective-permute-start(bf16[128,4096]{1,0:T(8,128)(2,1)S(1)} %collective-permute-done.3), channel_id=1, source_target_pairs={{0,4},{4,0},{8,12},{12,8},{16,20},{20,16},{24,28},{28,24},{1,5},{5... | collective-permute-start | bytes 3145736 | tf_op jit(solution)/shard_map/ppermute | solution.py:14
  32.1 12.0 %collective-permute-start.7 = (bf16[48,4096]{1,0:T(8,128)(2,1)S(1)}, bf16[48,4096]{1,0:T(8,128)(2,1)S(1)}, u32[]{:S(2)}, u32[]{:S(2)}) collective-permute-start(bf16[48,4096]{1,0:T(8,128)(2,1)S(1)} %slice.132), channel_id=1, source_target_pairs={{0,16},{4,20},{8,24},{12,28},{16,0},{20,4},{24,8},{28,12},{1,17},{... | collective-permute-start | bytes 1179656 | tf_op jit(solution)/shard_map/ppermute | solution.py:14
  35.7 14.8 %collective-permute-start.5 = (bf16[128,256]{1,0:T(8,128)(2,1)S(1)}, bf16[128,256]{1,0:T(8,128)(2,1)S(1)}, u32[]{:S(2)}, u32[]{:S(2)}) collective-permute-start(bf16[128,256]{1,0:T(8,128)(2,1)S(1)} %slice.173), channel_id=1, source_target_pairs={{0,16},{4,20},{8,24},{12,28},{16,0},{20,4},{24,8},{28,12},{1,17},{... | collective-permute-start | bytes 196616 | tf_op jit(solution)/shard_map/ppermute | solution.py:14
  36.3 13.3 %collective-permute-start.11 = (bf16[384,256]{1,0:T(8,128)(2,1)S(1)}, bf16[384,256]{1,0:T(8,128)(2,1)S(1)}, u32[]{:S(2)}, u32[]{:S(2)}) collective-permute-start(bf16[384,256]{1,0:T(8,128)(2,1)S(1)} %slice.177), channel_id=1, source_target_pairs={{0,16},{4,20},{8,24},{12,28},{16,0},{20,4},{24,8},{28,12},{1,17},{... | collective-permute-start | bytes 589832 | tf_op jit(solution)/shard_map/ppermute | solution.py:14
  44.1 1.7 %collective-permute-start.9 = (bf16[48,4096]{1,0:T(8,128)(2,1)S(1)}, bf16[48,4096]{1,0:T(8,128)(2,1)S(1)}, u32[]{:S(2)}, u32[]{:S(2)}) collective-permute-start(bf16[48,4096]{1,0:T(8,128)(2,1)S(1)} %collective-permute-done.7), channel_id=1, source_target_pairs={{0,4},{4,0},{8,12},{12,8},{16,20},{20,16},{24,28},{28,24},{1,5},{5... | collective-permute-start | bytes 1179656 | tf_op jit(solution)/shard_map/ppermute | solution.py:14
  44.1 3.2 %collective-permute-start.8 = (bf16[80,4096]{1,0:T(8,128)(2,1)S(1)}, bf16[80,4096]{1,0:T(8,128)(2,1)S(1)}, u32[]{:S(2)}, u32[]{:S(2)}) collective-permute-start(bf16[80,4096]{1,0:T(8,128)(2,1)S(1)} %collective-permute-done.6), channel_id=1, source_target_pairs={{0,4},{4,0},{8,12},{12,8},{16,20},{20,16},{24,28},{28,24},{1,5},{5... | collective-permute-start | bytes 1966088 | tf_op jit(solution)/shard_map/ppermute | solution.py:14
  45.8 4.7 %collective-permute-start.12 = (bf16[128,256]{1,0:T(8,128)(2,1)S(1)}, bf16[128,256]{1,0:T(8,128)(2,1)S(1)}, u32[]{:S(2)}, u32[]{:S(2)}) collective-permute-start(bf16[128,256]{1,0:T(8,128)(2,1)S(1)} %slice.179), channel_id=1, source_target_pairs={{0,16},{4,20},{8,24},{12,28},{16,0},{20,4},{24,8},{28,12},{1,17},{... | collective-permute-start | bytes 196616 | tf_op jit(solution)/shard_map/ppermute | solution.py:14
  50.5 4.3 %collective-permute-start.10 = (bf16[128,256]{1,0:T(8,128)(2,1)S(1)}, bf16[128,256]{1,0:T(8,128)(2,1)S(1)}, u32[]{:S(2)}, u32[]{:S(2)}) collective-permute-start(bf16[128,256]{1,0:T(8,128)(2,1)S(1)} %slice.175), channel_id=1, source_target_pairs={{0,16},{4,20},{8,24},{12,28},{16,0},{20,4},{24,8},{28,12},{1,17},{... | collective-permute-start | bytes 196616 | tf_op jit(solution)/shard_map/ppermute | solution.py:14
  56.4 13.5 %collective-permute-start.13 = (bf16[128,2048]{1,0:T(8,128)(2,1)S(1)}, bf16[128,2048]{1,0:T(8,128)(2,1)S(1)}, u32[]{:S(2)}, u32[]{:S(2)}) collective-permute-start(bf16[128,2048]{1,0:T(8,128)(2,1)S(1)} %pad_maximum_fusion), channel_id=1, source_target_pairs={{0,1},{1,0},{2,3},{3,2},{4,5},{5,4},{6,7},{7,6},{8,9},{9,8},{10,11... | collective-permute-start | bytes 1572872 | tf_op jit(solution)/shard_map/ppermute | solution.py:14
  58.0 6.4 %collective-permute-start.15 = (bf16[256,256]{1,0:T(8,128)(2,1)S(1)}, bf16[256,256]{1,0:T(8,128)(2,1)S(1)}, u32[]{:S(2)}, u32[]{:S(2)}) collective-permute-start(bf16[256,256]{1,0:T(8,128)(2,1)S(1)} %slice.181), channel_id=1, source_target_pairs={{0,16},{4,20},{8,24},{12,28},{16,0},{20,4},{24,8},{28,12},{1,17},{... | collective-permute-start | bytes 393224 | tf_op jit(solution)/shard_map/ppermute | solution.py:14
  59.5 6.3 %collective-permute-start.16 = (bf16[256,256]{1,0:T(8,128)(2,1)S(1)}, bf16[256,256]{1,0:T(8,128)(2,1)S(1)}, u32[]{:S(2)}, u32[]{:S(2)}) collective-permute-start(bf16[256,256]{1,0:T(8,128)(2,1)S(1)} %slice.184), channel_id=1, source_target_pairs={{0,16},{4,20},{8,24},{12,28},{16,0},{20,4},{24,8},{28,12},{1,17},{... | collective-permute-start | bytes 393224 | tf_op jit(solution)/shard_map/ppermute | solution.py:14
  60.1 7.2 %collective-permute-start.17 = (bf16[256,256]{1,0:T(8,128)(2,1)S(1)}, bf16[256,256]{1,0:T(8,128)(2,1)S(1)}, u32[]{:S(2)}, u32[]{:S(2)}) collective-permute-start(bf16[256,256]{1,0:T(8,128)(2,1)S(1)} %slice.188), channel_id=1, source_target_pairs={{0,16},{4,20},{8,24},{12,28},{16,0},{20,4},{24,8},{28,12},{1,17},{... | collective-permute-start | bytes 393224 | tf_op jit(solution)/shard_map/ppermute | solution.py:14
  68.9 17.5 %collective-permute-start.20 = (bf16[112,2048]{1,0:T(8,128)(2,1)S(1)}, bf16[112,2048]{1,0:T(8,128)(2,1)S(1)}, u32[]{:S(2)}, u32[]{:S(2)}) collective-permute-start(bf16[112,2048]{1,0:T(8,128)(2,1)S(1)} %pad_maximum_fusion.1), channel_id=1, source_target_pairs={{0,1},{1,0},{2,3},{3,2},{4,5},{5,4},{6,7},{7,6},{8,9},{9,8},{10,11... | collective-permute-start | bytes 1376264 | tf_op jit(solution)/shard_map/ppermute | solution.py:14
  70.1 34.3 %collective-permute-start.14 = (bf16[128,1024]{1,0:T(8,128)(2,1)S(1)}, bf16[128,1024]{1,0:T(8,128)(2,1)S(1)}, u32[]{:S(2)}, u32[]{:S(2)}) collective-permute-start(bf16[128,1024]{1,0:T(8,128)(2,1)S(1)} %dynamic-slice_convert_fusion), channel_id=1, source_target_pairs={{0,2},{1,3},{2,0},{3,1},{4,6},{5,7},{6,4},{7,5},{8,10},{9,11},{10,... | collective-permute-start | bytes 786440 | tf_op jit(solution)/shard_map/ppermute | solution.py:14
  74.4 24.0 %collective-permute-start.19 = (bf16[80,2048]{1,0:T(8,128)(2,1)S(1)}, bf16[80,2048]{1,0:T(8,128)(2,1)S(1)}, u32[]{:S(2)}, u32[]{:S(2)}) collective-permute-start(bf16[80,2048]{1,0:T(8,128)(2,1)S(1)} %pad_maximum_fusion.2), channel_id=1, source_target_pairs={{0,1},{1,0},{2,3},{3,2},{4,5},{5,4},{6,7},{7,6},{8,9},{9,8},{10,11... | collective-permute-start | bytes 983048 | tf_op jit(solution)/shard_map/ppermute | solution.py:14
  77.7 26.0 %collective-permute-start.18 = (bf16[64,2048]{1,0:T(8,128)(2,1)S(1)}, bf16[64,2048]{1,0:T(8,128)(2,1)S(1)}, u32[]{:S(2)}, u32[]{:S(2)}) collective-permute-start(bf16[64,2048]{1,0:T(8,128)(2,1)S(1)} %pad_maximum_fusion.4), channel_id=1, source_target_pairs={{0,1},{1,0},{2,3},{3,2},{4,5},{5,4},{6,7},{7,6},{8,9},{9,8},{10,11... | collective-permute-start | bytes 786440 | tf_op jit(solution)/shard_map/ppermute | solution.py:14
  86.5 19.6 %collective-permute-start.21 = (bf16[112,1024]{1,0:T(8,128)(2,1)S(1)}, bf16[112,1024]{1,0:T(8,128)(2,1)S(1)}, u32[]{:S(2)}, u32[]{:S(2)}) collective-permute-start(bf16[112,1024]{1,0:T(8,128)(2,1)S(1)} %dynamic-slice_convert_fusion.3), channel_id=1, source_target_pairs={{0,2},{1,3},{2,0},{3,1},{4,6},{5,7},{6,4},{7,5},{8,10},{9,11},{10,... | collective-permute-start | bytes 688136 | tf_op jit(solution)/shard_map/ppermute | solution.py:14
  98.5 14.9 %collective-permute-start.22 = (bf16[80,1024]{1,0:T(8,128)(2,1)S(1)}, bf16[80,1024]{1,0:T(8,128)(2,1)S(1)}, u32[]{:S(2)}, u32[]{:S(2)}) collective-permute-start(bf16[80,1024]{1,0:T(8,128)(2,1)S(1)} %dynamic-slice_convert_fusion.6), channel_id=1, source_target_pairs={{0,2},{1,3},{2,0},{3,1},{4,6},{5,7},{6,4},{7,5},{8,10},{9,11},{10,... | collective-permute-start | bytes 491528 | tf_op jit(solution)/shard_map/ppermute | solution.py:14
  103.7 11.2 %collective-permute-start.23 = (bf16[64,1024]{1,0:T(8,128)(2,1)S(1)}, bf16[64,1024]{1,0:T(8,128)(2,1)S(1)}, u32[]{:S(2)}, u32[]{:S(2)}) collective-permute-start(bf16[64,1024]{1,0:T(8,128)(2,1)S(1)} %dynamic-slice_convert_fusion.9), channel_id=1, source_target_pairs={{0,2},{1,3},{2,0},{3,1},{4,6},{5,7},{6,4},{7,5},{8,10},{9,11},{10,... | collective-permute-start | bytes 393224 | tf_op jit(solution)/shard_map/ppermute | solution.py:14
  104.5 11.8 %collective-permute-start.24 = (bf16[128,1024]{1,0:T(8,128)(2,1)S(1)}, bf16[128,1024]{1,0:T(8,128)(2,1)S(1)}, u32[]{:S(2)}, u32[]{:S(2)}) collective-permute-start(bf16[128,1024]{1,0:T(8,128)(2,1)S(1)} %get-tuple-element.61), channel_id=1, source_target_pairs={{0,16},{4,20},{8,24},{12,28},{16,0},{20,4},{24,8},{28,12},{1,17},{... | collective-permute-start | bytes 786440 | tf_op jit(solution)/shard_map/ppermute | solution.py:14
  106.2 12.4 %collective-permute-start.25 = (bf16[112,1024]{1,0:T(8,128)(2,1)S(1)}, bf16[112,1024]{1,0:T(8,128)(2,1)S(1)}, u32[]{:S(2)}, u32[]{:S(2)}) collective-permute-start(bf16[112,1024]{1,0:T(8,128)(2,1)S(1)} %get-tuple-element.67), channel_id=1, source_target_pairs={{0,16},{4,20},{8,24},{12,28},{16,0},{20,4},{24,8},{28,12},{1,17},{... | collective-permute-start | bytes 688136 | tf_op jit(solution)/shard_map/ppermute | solution.py:14
  113.4 7.0 %collective-permute-start.26 = (bf16[80,1024]{1,0:T(8,128)(2,1)S(1)}, bf16[80,1024]{1,0:T(8,128)(2,1)S(1)}, u32[]{:S(2)}, u32[]{:S(2)}) collective-permute-start(bf16[80,1024]{1,0:T(8,128)(2,1)S(1)} %get-tuple-element.73), channel_id=1, source_target_pairs={{0,16},{4,20},{8,24},{12,28},{16,0},{20,4},{24,8},{28,12},{1,17},{... | collective-permute-start | bytes 491528 | tf_op jit(solution)/shard_map/ppermute | solution.py:14
  115.0 6.8 %collective-permute-start.27 = (bf16[64,1024]{1,0:T(8,128)(2,1)S(1)}, bf16[64,1024]{1,0:T(8,128)(2,1)S(1)}, u32[]{:S(2)}, u32[]{:S(2)}) collective-permute-start(bf16[64,1024]{1,0:T(8,128)(2,1)S(1)} %get-tuple-element.75), channel_id=1, source_target_pairs={{0,16},{4,20},{8,24},{12,28},{16,0},{20,4},{24,8},{28,12},{1,17},{... | collective-permute-start | bytes 393224 | tf_op jit(solution)/shard_map/ppermute | solution.py:14
where the time goes:
time: 126 us; the launch traced here: 125 us
  waiting for transfers between devices  56 us (44%)
  starting transfers between devices  33.2 us (26%)
  matrix products  26.7 us (21%)
  local copies, waits for them, and re-layouts  6.77 us (5%)
  other arithmetic  2.13 us (2%)
    ppermute x28, waiting for transfers between devices, swap(): return lax.ppermute(block, axis, [(i, i ^ bit) for i in range(count)])  56 us
    ppermute x28, starting transfers between devices, swap(): return lax.ppermute(block, axis, [(i, i ^ bit) for i in range(count)])  33.2 us
    dot_general x4, matrix products, score(): lax.dot_general(refs, images_of([m]), (((1,), (1,)), ((), ())), preferred...  10.9 us
    dot_general x1, matrix products, body(): refs = jnp.dot(one_hot, references, preferred_element_type=F32).astype(BF16)  9.9 us
    dot_general x4, matrix products, body(): jnp.dot(w, every_image, preferred_element_type=F32) * scale  5.87 us
    gather x1, local copies, waits for them, and re-layouts, body(): jnp.concatenate(done + other, axis=0).at[place]  3.61 us
  transfers between devices with their start and end apart: 28, of which 16 were waited for; matrix products, arithmetic and copies ran while one was open for 24% of the time, Pallas kernels for 0%

commit v1 on v0

--- a/solution.py
+++ b/solution.py
@@ -5,7 +5,7 @@
 
 F32 = jnp.float32
 BF16 = jnp.bfloat16
-ROW_CHUNKS = (8, 7, 5, 4)
+ROW_CHUNKS = (8, 6, 5, 3, 2)
 FORWARD_LOW = 10
 
 
@@ -137,8 +137,8 @@
         came = [swap(give, "img", bit) for keep, give in pairs]
         bit *= 2
         after_it = []
-        for pair, block in zip(pairs, came):
-            after_it.append(onward(pair, block, bit, [give for keep, give in after_it[-1:] + pairs[-1:]]))
+        for c, (pair, block) in enumerate(zip(pairs, came)):
+            after_it.append(onward(pair, block, bit, [give for keep, give in after_it[-1:] + pairs[c + 1 : c + 2]]))
         pairs = after_it
     done = [keep for keep, give in pairs]
     gone = [give for keep, give in pairs]

time: 126 us -> 122 us (0.968)
  waiting for transfers between devices: 56 us -> 41.5 us
  starting transfers between devices: 33.2 us -> 42.6 us
  matrix products: 26.7 us -> 28.3 us
    ppermute x28 -> x31, waiting for transfers between devices: 56 us -> 41.5 us  [swap(): return lax.ppermute(block, axis, [(i, i ^ bit) for i in range(count)])]
    ppermute x28 -> x31, starting transfers between devices: 33.2 us -> 42.6 us  [swap(): return lax.ppermute(block, axis, [(i, i ^ bit) for i in range(count)])]
    dot_general x4 -> x5, matrix products: 5.87 us -> 7.5 us  [body(): jnp.dot(w, every_image, preferred_element_type=F32) * scale]
  transfers between devices with their start and end apart: 28 -> 31, of which waited for: 16 -> 16; matrix products, arithmetic and copies ran while one was open for 24% -> 26% of each run, Pallas kernels for 0% -> 0%
where the time goes in v1:
time: 122 us
  starting transfers between devices  42.6 us (35%)
  waiting for transfers between devices  41.5 us (34%)
  matrix products  28.3 us (23%)
  local copies, waits for them, and re-layouts  6.8 us (6%)
  other arithmetic  2.13 us (2%)
    ppermute x31, starting transfers between devices, swap(): return lax.ppermute(block, axis, [(i, i ^ bit) for i in range(count)])  42.6 us
    ppermute x31, waiting for transfers between devices, swap(): return lax.ppermute(block, axis, [(i, i ^ bit) for i in range(count)])  41.5 us
    dot_general x4, matrix products, score(): lax.dot_general(refs, images_of([m]), (((1,), (1,)), ((), ())), preferred...  10.9 us
    dot_general x1, matrix products, body(): refs = jnp.dot(one_hot, references, preferred_element_type=F32).astype(BF16)  9.89 us
    dot_general x5, matrix products, body(): jnp.dot(w, every_image, preferred_element_type=F32) * scale  7.5 us
    gather x1, local copies, waits for them, and re-layouts, body(): jnp.concatenate(done + other, axis=0).at[place]  3.61 us
  transfers between devices with their start and end apart: 31, of which 16 were waited for; matrix products, arithmetic and copies ran while one was open for 26% of the time, Pallas kernels for 0%

profile of v1, /device:TPU:0, one launch (start us, length us, event | category | flops | bytes accessed | tf_op | source)
XLA Modules:
  0.0 122.0 jit_solution(7497714586094204762)
XLA Ops:
  0.0 3.0 %collective-permute-start.1 = (bf16[128,4096]{1,0:T(8,128)(2,1)}, bf16[128,4096]{1,0:T(8,128)(2,1)S(1)}, u32[]{:S(2)}, u32[]{:S(2)}) collective-permute-start(bf16[128,4096]{1,0:T(8,128)(2,1)} %param.4), channel_id=1, source_target_pairs={{0,16},{4,20},{8,24},{12,28},{16,0},{20,4},{24,8},{28,12},{1,17},{... | collective-permute-start | bytes 3145736 | tf_op jit(solution)/shard_map/ppermute | solution.py:14
  5.2 9.9 %multiply_reduce_fusion = (f32[768]{0:T(1024)S(1)}, bf16[768,4096]{1,0:T(8,128)(2,1)}) fusion(bf16[768,4096]{1,0:T(8,128)(2,1)} %param.6, s32[768]{0:T(1024)S(1)} %get-tuple-element.58), kind=kOutput, calls=%fused_computation.2 | convolution fusion | flops 4845009920 | bytes 12589056 | tf_op jit(solution)/shard_map/dot_general | solution.py:54
  15.7 5.0 %fusion.74 = bf16[768,256]{1,0:T(8,128)(2,1)S(1)} fusion(bf16[768,4096]{1,0:T(8,128)(2,1)} %get-tuple-element.94, bf16[128,4096]{1,0:T(8,128)(2,1)} %collective-permute-done, bf16[128,4096]{1,0:T(8,128)(2,1)S(1)} %copy-done.1, f32[256]{0:T(256)S(1)} %get-tuple-element.92, f32[768]{0:T(1024)S(1)} %broadcast_multiply_fusion), kind=kOutput, calls=%fused_computation.48 | convolution fusion | flops 1615593472 | bytes 8785920 | tf_op jit(solution)/shard_map/dot_general | solution.py:68
  20.8 5.6 %collective-permute-done.1 = bf16[128,4096]{1,0:T(8,128)(2,1)S(1)} collective-permute-done((bf16[128,4096]{1,0:T(8,128)(2,1)}, bf16[128,4096]{1,0:T(8,128)(2,1)S(1)}, u32[]{:S(2)}, u32[]{:S(2)}) %collective-permute-start.1) | collective-permute-done | bytes 1048608 | tf_op jit(solution)/shard_map/ppermute | solution.py:14
  26.5 1.8 %collective-permute-start.6 = (bf16[80,4096]{1,0:T(8,128)(2,1)S(1)}, bf16[80,4096]{1,0:T(8,128)(2,1)S(1)}, u32[]{:S(2)}, u32[]{:S(2)}) collective-permute-start(bf16[80,4096]{1,0:T(8,128)(2,1)S(1)} %slice.154), channel_id=1, source_target_pairs={{0,8},{4,12},{8,0},{12,4},{16,24},{20,28},{24,16},{28,20},{1,9},{5... | collective-permute-start | bytes 1966088 | tf_op jit(solution)/shard_map/ppermute | solution.py:14
  29.9 2.0 %fusion.71 = bf16[768,256]{1,0:T(8,128)(2,1)S(1)} fusion(bf16[768,4096]{1,0:T(8,128)(2,1)S(1)} %bitcast.28, bf16[128,4096]{1,0:T(8,128)(2,1)S(1)} %collective-permute-done.2, bf16[128,4096]{1,0:T(8,128)(2,1)S(1)} %collective-permute-done.1, f32[256]{0:T(256)S(1)} %get-tuple-element.91, f32[768]{0:T(1024)S(1)} %broadcast_multiply_fusion), kind=kOutput, calls=%fused_computation.47 | convolution fusion | flops 1615593472 | bytes 8785920 | tf_op jit(solution)/shard_map/dot_general | solution.py:68
  32.1 1.6 %collective-permute-start.7 = (bf16[48,4096]{1,0:T(8,128)(2,1)S(1)}, bf16[48,4096]{1,0:T(8,128)(2,1)S(1)}, u32[]{:S(2)}, u32[]{:S(2)}) collective-permute-start(bf16[48,4096]{1,0:T(8,128)(2,1)S(1)} %slice.156), channel_id=1, source_target_pairs={{0,16},{4,20},{8,24},{12,28},{16,0},{20,4},{24,8},{28,12},{1,17},{... | collective-permute-start | bytes 1179656 | tf_op jit(solution)/shard_map/ppermute | solution.py:14
  33.7 2.0 %fusion.68 = bf16[768,256]{1,0:T(8,128)(2,1)S(1)} fusion(bf16[768,4096]{1,0:T(8,128)(2,1)S(1)} %bitcast.28, bf16[128,4096]{1,0:T(8,128)(2,1)S(1)} %collective-permute-done.4, bf16[128,4096]{1,0:T(8,128)(2,1)S(1)} %collective-permute-done.3, f32[256]{0:T(256)S(1)} %get-tuple-element.90, f32[768]{0:T(1024)S(1)} %broadcast_multiply_fusion), kind=kOutput, calls=%fused_computation.46 | convolution fusion | flops 1615593472 | bytes 8785920 | tf_op jit(solution)/shard_map/dot_general | solution.py:68
  37.8 6.3 %collective-permute-done.7 = bf16[48,4096]{1,0:T(8,128)(2,1)S(1)} collective-permute-done((bf16[48,4096]{1,0:T(8,128)(2,1)S(1)}, bf16[48,4096]{1,0:T(8,128)(2,1)S(1)}, u32[]{:S(2)}, u32[]{:S(2)}) %collective-permute-start.7) | collective-permute-done | bytes 393248 | tf_op jit(solution)/shard_map/ppermute | solution.py:14
  45.8 1.5 %collective-permute-start.12 = (bf16[128,256]{1,0:T(8,128)(2,1)S(1)}, bf16[128,256]{1,0:T(8,128)(2,1)S(1)}, u32[]{:S(2)}, u32[]{:S(2)}) collective-permute-start(bf16[128,256]{1,0:T(8,128)(2,1)S(1)} %slice.211), channel_id=1, source_target_pairs={{0,16},{4,20},{8,24},{12,28},{16,0},{20,4},{24,8},{28,12},{1,17},{... | collective-permute-start | bytes 196616 | tf_op jit(solution)/shard_map/ppermute | solution.py:14
  47.3 1.8 %fusion.77 = bf16[768,256]{1,0:T(8,128)(2,1)S(1)} fusion(bf16[768,4096]{1,0:T(8,128)(2,1)S(1)} %bitcast.28, bf16[48,4096]{1,0:T(8,128)(2,1)S(1)} %collective-permute-done.9, bf16[80,4096]{1,0:T(8,128)(2,1)S(1)} %collective-permute-done.8, bf16[48,4096]{1,0:T(8,128)(2,1)S(1)} %collective-permute-done.7, bf16[80,4096]{1,0:T(8,128)(2,1)S(1)} %collective-permute-done.6, ...), kind=kOutput, calls=%fused_computation.49 | convolution fusion | flops 1619787776 | bytes 8785920 | tf_op jit(solution)/shard_map/dot_general | solution.py:68
  50.5 1.6 %collective-permute-start.10 = (bf16[128,256]{1,0:T(8,128)(2,1)S(1)}, bf16[128,256]{1,0:T(8,128)(2,1)S(1)}, u32[]{:S(2)}, u32[]{:S(2)}) collective-permute-start(bf16[128,256]{1,0:T(8,128)(2,1)S(1)} %slice.207), channel_id=1, source_target_pairs={{0,16},{4,20},{8,24},{12,28},{16,0},{20,4},{24,8},{28,12},{1,17},{... | collective-permute-start | bytes 196616 | tf_op jit(solution)/shard_map/ppermute | solution.py:14
  52.2 2.6 %collective-permute-done.10 = bf16[128,256]{1,0:T(8,128)(2,1)S(1)} collective-permute-done((bf16[128,256]{1,0:T(8,128)(2,1)S(1)}, bf16[128,256]{1,0:T(8,128)(2,1)S(1)}, u32[]{:S(2)}, u32[]{:S(2)}) %collective-permute-start.10) | collective-permute-done | bytes 65568 | tf_op jit(solution)/shard_map/ppermute | solution.py:14
  56.4 1.6 %collective-permute-start.13 = (bf16[128,2048]{1,0:T(8,128)(2,1)S(1)}, bf16[128,2048]{1,0:T(8,128)(2,1)S(1)}, u32[]{:S(2)}, u32[]{:S(2)}) collective-permute-start(bf16[128,2048]{1,0:T(8,128)(2,1)S(1)} %pad_maximum_fusion), channel_id=1, source_target_pairs={{0,1},{1,0},{2,3},{3,2},{4,5},{5,4},{6,7},{7,6},{8,9},{9,8},{10,11... | collective-permute-start | bytes 1572872 | tf_op jit(solution)/shard_map/ppermute | solution.py:14
  61.7 2.8 %collective-permute-done.15 = bf16[256,256]{1,0:T(8,128)(2,1)S(1)} collective-permute-done((bf16[256,256]{1,0:T(8,128)(2,1)S(1)}, bf16[256,256]{1,0:T(8,128)(2,1)S(1)}, u32[]{:S(2)}, u32[]{:S(2)}) %collective-permute-start.15) | collective-permute-done | bytes 131104 | tf_op jit(solution)/shard_map/ppermute | solution.py:14
  70.1 2.7 %collective-permute-start.14 = (bf16[128,1024]{1,0:T(8,128)(2,1)S(1)}, bf16[128,1024]{1,0:T(8,128)(2,1)S(1)}, u32[]{:S(2)}, u32[]{:S(2)}) collective-permute-start(bf16[128,1024]{1,0:T(8,128)(2,1)S(1)} %dynamic-slice_convert_fusion), channel_id=1, source_target_pairs={{0,2},{1,3},{2,0},{3,1},{4,6},{5,7},{6,4},{7,5},{8,10},{9,11},{10,... | collective-permute-start | bytes 786440 | tf_op jit(solution)/shard_map/ppermute | solution.py:14
  72.8 1.6 %convolution_multiply_fusion.2 = f32[80,4096]{1,0:T(8,128)S(1)} fusion(bf16[80,1024]{1,0:T(8,128)(2,1)S(1)} %pad_maximum_fusion.6, bf16[1024,4096]{1,0:T(8,128)(2,1)S(1)} %constant_dynamic-update-slice_fusion), kind=kOutput, calls=%fused_computation.6 | convolution fusion | flops 671416320 | bytes 9863168 | tf_op jit(solution)/shard_map/dot_general | solution.py:127
  74.5 1.6 %collective-permute-start.20 = (bf16[80,2048]{1,0:T(8,128)(2,1)S(1)}, bf16[80,2048]{1,0:T(8,128)(2,1)S(1)}, u32[]{:S(2)}, u32[]{:S(2)}) collective-permute-start(bf16[80,2048]{1,0:T(8,128)(2,1)S(1)} %pad_maximum_fusion.2), channel_id=1, source_target_pairs={{0,1},{1,0},{2,3},{3,2},{4,5},{5,4},{6,7},{7,6},{8,9},{9,8},{10,11... | collective-permute-start | bytes 983048 | tf_op jit(solution)/shard_map/ppermute | solution.py:14
  76.2 9.0 %collective-permute-done.18 = bf16[96,2048]{1,0:T(8,128)(2,1)S(1)} collective-permute-done((bf16[96,2048]{1,0:T(8,128)(2,1)S(1)}, bf16[96,2048]{1,0:T(8,128)(2,1)S(1)}, u32[]{:S(2)}, u32[]{:S(2)}) %collective-permute-start.18) | collective-permute-done | bytes 393248 | tf_op jit(solution)/shard_map/ppermute | solution.py:14
  86.7 1.6 %convolution_multiply_fusion.3 = f32[48,4096]{1,0:T(8,128)S(1)} fusion(bf16[48,1024]{1,0:T(8,128)(2,1)S(1)} %pad_maximum_fusion.8, bf16[1024,4096]{1,0:T(8,128)(2,1)S(1)} %constant_dynamic-update-slice_fusion), kind=kOutput, calls=%fused_computation.7 | convolution fusion | flops 402849792 | bytes 9273344 | tf_op jit(solution)/shard_map/dot_general | solution.py:127
  88.3 3.0 %collective-permute-start.22 = (bf16[48,2048]{1,0:T(8,128)(2,1)S(1)}, bf16[48,2048]{1,0:T(8,128)(2,1)S(1)}, u32[]{:S(2)}, u32[]{:S(2)}) collective-permute-start(bf16[48,2048]{1,0:T(8,128)(2,1)S(1)} %pad_maximum_fusion.5), channel_id=1, source_target_pairs={{0,1},{1,0},{2,3},{3,2},{4,5},{5,4},{6,7},{7,6},{8,9},{9,8},{10,11... | collective-permute-start | bytes 589832 | tf_op jit(solution)/shard_map/ppermute | solution.py:14
  91.4 1.5 %convolution_multiply_fusion.4 = f32[32,4096]{1,0:T(8,128)S(1)} fusion(bf16[32,1024]{1,0:T(8,128)(2,1)S(1)} %pad_maximum_fusion.9, bf16[1024,4096]{1,0:T(8,128)(2,1)S(1)} %constant_dynamic-update-slice_fusion), kind=kOutput, calls=%fused_computation.8 | convolution fusion | flops 268566528 | bytes 8978432 | tf_op jit(solution)/shard_map/dot_general | solution.py:127
  93.2 1.6 %collective-permute-start.26 = (bf16[128,1024]{1,0:T(8,128)(2,1)S(1)}, bf16[128,1024]{1,0:T(8,128)(2,1)S(1)}, u32[]{:S(2)}, u32[]{:S(2)}) collective-permute-start(bf16[128,1024]{1,0:T(8,128)(2,1)S(1)} %get-tuple-element.71), channel_id=1, source_target_pairs={{0,16},{4,20},{8,24},{12,28},{16,0},{20,4},{24,8},{28,12},{1,17},{... | collective-permute-start | bytes 786440 | tf_op jit(solution)/shard_map/ppermute | solution.py:14
  94.8 3.1 %collective-permute-done.20 = bf16[80,2048]{1,0:T(8,128)(2,1)S(1)} collective-permute-done((bf16[80,2048]{1,0:T(8,128)(2,1)S(1)}, bf16[80,2048]{1,0:T(8,128)(2,1)S(1)}, u32[]{:S(2)}, u32[]{:S(2)}) %collective-permute-start.20) | collective-permute-done | bytes 327712 | tf_op jit(solution)/shard_map/ppermute | solution.py:14
  98.0 1.8 %collective-permute-start.21 = (bf16[80,1024]{1,0:T(8,128)(2,1)S(1)}, bf16[80,1024]{1,0:T(8,128)(2,1)S(1)}, u32[]{:S(2)}, u32[]{:S(2)}) collective-permute-start(bf16[80,1024]{1,0:T(8,128)(2,1)S(1)} %dynamic-slice_convert_fusion.6), channel_id=1, source_target_pairs={{0,2},{1,3},{2,0},{3,1},{4,6},{5,7},{6,4},{7,5},{8,10},{9,11},{10,... | collective-permute-start | bytes 491528 | tf_op jit(solution)/shard_map/ppermute | solution.py:14
  99.8 1.7 %collective-permute-done.22 = bf16[48,2048]{1,0:T(8,128)(2,1)S(1)} collective-permute-done((bf16[48,2048]{1,0:T(8,128)(2,1)S(1)}, bf16[48,2048]{1,0:T(8,128)(2,1)S(1)}, u32[]{:S(2)}, u32[]{:S(2)}) %collective-permute-start.22) | collective-permute-done | bytes 196640 | tf_op jit(solution)/shard_map/ppermute | solution.py:14
  101.6 3.2 %collective-permute-start.23 = (bf16[48,1024]{1,0:T(8,128)(2,1)S(1)}, bf16[48,1024]{1,0:T(8,128)(2,1)S(1)}, u32[]{:S(2)}, u32[]{:S(2)}) collective-permute-start(bf16[48,1024]{1,0:T(8,128)(2,1)S(1)} %dynamic-slice_convert_fusion.9), channel_id=1, source_target_pairs={{0,2},{1,3},{2,0},{3,1},{4,6},{5,7},{6,4},{7,5},{8,10},{9,11},{10,... | collective-permute-start | bytes 294920 | tf_op jit(solution)/shard_map/ppermute | solution.py:14
  104.9 2.3 %collective-permute-start.25 = (bf16[32,1024]{1,0:T(8,128)(2,1)S(1)}, bf16[32,1024]{1,0:T(8,128)(2,1)S(1)}, u32[]{:S(2)}, u32[]{:S(2)}) collective-permute-start(bf16[32,1024]{1,0:T(8,128)(2,1)S(1)} %dynamic-slice_convert_fusion.12), channel_id=1, source_target_pairs={{0,2},{1,3},{2,0},{3,1},{4,6},{5,7},{6,4},{7,5},{8,10},{9,11},{10,... | collective-permute-start | bytes 196616 | tf_op jit(solution)/shard_map/ppermute | solution.py:14
  107.3 1.6 %collective-permute-start.27 = (bf16[96,1024]{1,0:T(8,128)(2,1)S(1)}, bf16[96,1024]{1,0:T(8,128)(2,1)S(1)}, u32[]{:S(2)}, u32[]{:S(2)}) collective-permute-start(bf16[96,1024]{1,0:T(8,128)(2,1)S(1)} %get-tuple-element.73), channel_id=1, source_target_pairs={{0,16},{4,20},{8,24},{12,28},{16,0},{20,4},{24,8},{28,12},{1,17},{... | collective-permute-start | bytes 589832 | tf_op jit(solution)/shard_map/ppermute | solution.py:14
  108.8 2.4 %collective-permute-done.21 = bf16[80,1024]{1,0:T(8,128)(2,1)S(1)} collective-permute-done((bf16[80,1024]{1,0:T(8,128)(2,1)S(1)}, bf16[80,1024]{1,0:T(8,128)(2,1)S(1)}, u32[]{:S(2)}, u32[]{:S(2)}) %collective-permute-start.21) | collective-permute-done | bytes 163872 | tf_op jit(solution)/shard_map/ppermute | solution.py:14
  111.2 1.6 %collective-permute-start.28 = (bf16[80,1024]{1,0:T(8,128)(2,1)S(1)}, bf16[80,1024]{1,0:T(8,128)(2,1)S(1)}, u32[]{:S(2)}, u32[]{:S(2)}) collective-permute-start(bf16[80,1024]{1,0:T(8,128)(2,1)S(1)} %get-tuple-element.75), channel_id=1, source_target_pairs={{0,16},{4,20},{8,24},{12,28},{16,0},{20,4},{24,8},{28,12},{1,17},{... | collective-permute-start | bytes 491528 | tf_op jit(solution)/shard_map/ppermute | solution.py:14
  118.4 3.6 %gather_fusion.1 = f32[768,1024]{1,0:T(8,128)} fusion(f32[768,1024]{1,0:T(8,128)S(1)} %convert_dynamic-update-slice_fusion.4, s32[1024]{0:T(1024)S(1)} %pad_clamp_fusion), kind=kCustom, calls=%fused_computation.1 | custom fusion | bytes 6294528 | tf_op jit(solution)/shard_map/gather | solution.py:146
  (136 shorter events, 28.3 us)
Async XLA Ops:
  0.0 15.1 %copy-start = (s32[1024]{0:T(1024)S(1)}, s32[1024]{0:T(1024)}, u32[]{:S(2)}) copy-start(s32[1024]{0:T(1024)} %param.5) | copy-start | bytes 12292
  0.0 26.3 %collective-permute-start.1 = (bf16[128,4096]{1,0:T(8,128)(2,1)}, bf16[128,4096]{1,0:T(8,128)(2,1)S(1)}, u32[]{:S(2)}, u32[]{:S(2)}) collective-permute-start(bf16[128,4096]{1,0:T(8,128)(2,1)} %param.4), channel_id=1, source_target_pairs={{0,16},{4,20},{8,24},{12,28},{16,0},{20,4},{24,8},{28,12},{1,17},{... | collective-permute-start | bytes 3145736 | tf_op jit(solution)/shard_map/ppermute | solution.py:14
  3.0 12.7 %collective-permute-start = (bf16[128,4096]{1,0:T(8,128)(2,1)}, bf16[128,4096]{1,0:T(8,128)(2,1)}, u32[]{:S(2)}, u32[]{:S(2)}) collective-permute-start(bf16[128,4096]{1,0:T(8,128)(2,1)} %param.4), channel_id=1, source_target_pairs={{0,4},{4,0},{8,12},{12,8},{16,20},{20,16},{24,28},{28,24},{1,5},{5... | collective-permute-start | bytes 3145736 | tf_op jit(solution)/shard_map/ppermute | solution.py:14
  3.0 26.6 %collective-permute-start.3 = (bf16[128,4096]{1,0:T(8,128)(2,1)}, bf16[128,4096]{1,0:T(8,128)(2,1)S(1)}, u32[]{:S(2)}, u32[]{:S(2)}) collective-permute-start(bf16[128,4096]{1,0:T(8,128)(2,1)} %param.4), channel_id=1, source_target_pairs={{0,8},{4,12},{8,0},{12,4},{16,24},{20,28},{24,16},{28,20},{1,9},{5... | collective-permute-start | bytes 3145736 | tf_op jit(solution)/shard_map/ppermute | solution.py:14
  26.3 3.3 %collective-permute-start.2 = (bf16[128,4096]{1,0:T(8,128)(2,1)S(1)}, bf16[128,4096]{1,0:T(8,128)(2,1)S(1)}, u32[]{:S(2)}, u32[]{:S(2)}) collective-permute-start(bf16[128,4096]{1,0:T(8,128)(2,1)S(1)} %collective-permute-done.1), channel_id=1, source_target_pairs={{0,4},{4,0},{8,12},{12,8},{16,20},{20,16},{24,28},{28,24},{1,5},{5... | collective-permute-start | bytes 3145736 | tf_op jit(solution)/shard_map/ppermute | solution.py:14
  26.5 17.6 %collective-permute-start.6 = (bf16[80,4096]{1,0:T(8,128)(2,1)S(1)}, bf16[80,4096]{1,0:T(8,128)(2,1)S(1)}, u32[]{:S(2)}, u32[]{:S(2)}) collective-permute-start(bf16[80,4096]{1,0:T(8,128)(2,1)S(1)} %slice.154), channel_id=1, source_target_pairs={{0,8},{4,12},{8,0},{12,4},{16,24},{20,28},{24,16},{28,20},{1,9},{5... | collective-permute-start | bytes 1966088 | tf_op jit(solution)/shard_map/ppermute | solution.py:14
  29.6 4.1 %collective-permute-start.4 = (bf16[128,4096]{1,0:T(8,128)(2,1)S(1)}, bf16[128,4096]{1,0:T(8,128)(2,1)S(1)}, u32[]{:S(2)}, u32[]{:S(2)}) collective-permute-start(bf16[128,4096]{1,0:T(8,128)(2,1)S(1)} %collective-permute-done.3), channel_id=1, source_target_pairs={{0,4},{4,0},{8,12},{12,8},{16,20},{20,16},{24,28},{28,24},{1,5},{5... | collective-permute-start | bytes 3145736 | tf_op jit(solution)/shard_map/ppermute | solution.py:14
  32.1 12.0 %collective-permute-start.7 = (bf16[48,4096]{1,0:T(8,128)(2,1)S(1)}, bf16[48,4096]{1,0:T(8,128)(2,1)S(1)}, u32[]{:S(2)}, u32[]{:S(2)}) collective-permute-start(bf16[48,4096]{1,0:T(8,128)(2,1)S(1)} %slice.156), channel_id=1, source_target_pairs={{0,16},{4,20},{8,24},{12,28},{16,0},{20,4},{24,8},{28,12},{1,17},{... | collective-permute-start | bytes 1179656 | tf_op jit(solution)/shard_map/ppermute | solution.py:14
  35.7 14.8 %collective-permute-start.5 = (bf16[128,256]{1,0:T(8,128)(2,1)S(1)}, bf16[128,256]{1,0:T(8,128)(2,1)S(1)}, u32[]{:S(2)}, u32[]{:S(2)}) collective-permute-start(bf16[128,256]{1,0:T(8,128)(2,1)S(1)} %slice.205), channel_id=1, source_target_pairs={{0,16},{4,20},{8,24},{12,28},{16,0},{20,4},{24,8},{28,12},{1,17},{... | collective-permute-start | bytes 196616 | tf_op jit(solution)/shard_map/ppermute | solution.py:14
  36.3 13.3 %collective-permute-start.11 = (bf16[384,256]{1,0:T(8,128)(2,1)S(1)}, bf16[384,256]{1,0:T(8,128)(2,1)S(1)}, u32[]{:S(2)}, u32[]{:S(2)}) collective-permute-start(bf16[384,256]{1,0:T(8,128)(2,1)S(1)} %slice.209), channel_id=1, source_target_pairs={{0,16},{4,20},{8,24},{12,28},{16,0},{20,4},{24,8},{28,12},{1,17},{... | collective-permute-start | bytes 589832 | tf_op jit(solution)/shard_map/ppermute | solution.py:14
  44.1 1.7 %collective-permute-start.9 = (bf16[48,4096]{1,0:T(8,128)(2,1)S(1)}, bf16[48,4096]{1,0:T(8,128)(2,1)S(1)}, u32[]{:S(2)}, u32[]{:S(2)}) collective-permute-start(bf16[48,4096]{1,0:T(8,128)(2,1)S(1)} %collective-permute-done.7), channel_id=1, source_target_pairs={{0,4},{4,0},{8,12},{12,8},{16,20},{20,16},{24,28},{28,24},{1,5},{5... | collective-permute-start | bytes 1179656 | tf_op jit(solution)/shard_map/ppermute | solution.py:14
  44.1 3.2 %collective-permute-start.8 = (bf16[80,4096]{1,0:T(8,128)(2,1)S(1)}, bf16[80,4096]{1,0:T(8,128)(2,1)S(1)}, u32[]{:S(2)}, u32[]{:S(2)}) collective-permute-start(bf16[80,4096]{1,0:T(8,128)(2,1)S(1)} %collective-permute-done.6), channel_id=1, source_target_pairs={{0,4},{4,0},{8,12},{12,8},{16,20},{20,16},{24,28},{28,24},{1,5},{5... | collective-permute-start | bytes 1966088 | tf_op jit(solution)/shard_map/ppermute | solution.py:14
  45.8 4.7 %collective-permute-start.12 = (bf16[128,256]{1,0:T(8,128)(2,1)S(1)}, bf16[128,256]{1,0:T(8,128)(2,1)S(1)}, u32[]{:S(2)}, u32[]{:S(2)}) collective-permute-start(bf16[128,256]{1,0:T(8,128)(2,1)S(1)} %slice.211), channel_id=1, source_target_pairs={{0,16},{4,20},{8,24},{12,28},{16,0},{20,4},{24,8},{28,12},{1,17},{... | collective-permute-start | bytes 196616 | tf_op jit(solution)/shard_map/ppermute | solution.py:14
  50.5 4.3 %collective-permute-start.10 = (bf16[128,256]{1,0:T(8,128)(2,1)S(1)}, bf16[128,256]{1,0:T(8,128)(2,1)S(1)}, u32[]{:S(2)}, u32[]{:S(2)}) collective-permute-start(bf16[128,256]{1,0:T(8,128)(2,1)S(1)} %slice.207), channel_id=1, source_target_pairs={{0,16},{4,20},{8,24},{12,28},{16,0},{20,4},{24,8},{28,12},{1,17},{... | collective-permute-start | bytes 196616 | tf_op jit(solution)/shard_map/ppermute | solution.py:14
  56.4 13.6 %collective-permute-start.13 = (bf16[128,2048]{1,0:T(8,128)(2,1)S(1)}, bf16[128,2048]{1,0:T(8,128)(2,1)S(1)}, u32[]{:S(2)}, u32[]{:S(2)}) collective-permute-start(bf16[128,2048]{1,0:T(8,128)(2,1)S(1)} %pad_maximum_fusion), channel_id=1, source_target_pairs={{0,1},{1,0},{2,3},{3,2},{4,5},{5,4},{6,7},{7,6},{8,9},{9,8},{10,11... | collective-permute-start | bytes 1572872 | tf_op jit(solution)/shard_map/ppermute | solution.py:14
  58.0 6.4 %collective-permute-start.15 = (bf16[256,256]{1,0:T(8,128)(2,1)S(1)}, bf16[256,256]{1,0:T(8,128)(2,1)S(1)}, u32[]{:S(2)}, u32[]{:S(2)}) collective-permute-start(bf16[256,256]{1,0:T(8,128)(2,1)S(1)} %slice.213), channel_id=1, source_target_pairs={{0,16},{4,20},{8,24},{12,28},{16,0},{20,4},{24,8},{28,12},{1,17},{... | collective-permute-start | bytes 393224 | tf_op jit(solution)/shard_map/ppermute | solution.py:14
  59.6 6.3 %collective-permute-start.16 = (bf16[256,256]{1,0:T(8,128)(2,1)S(1)}, bf16[256,256]{1,0:T(8,128)(2,1)S(1)}, u32[]{:S(2)}, u32[]{:S(2)}) collective-permute-start(bf16[256,256]{1,0:T(8,128)(2,1)S(1)} %slice.216), channel_id=1, source_target_pairs={{0,16},{4,20},{8,24},{12,28},{16,0},{20,4},{24,8},{28,12},{1,17},{... | collective-permute-start | bytes 393224 | tf_op jit(solution)/shard_map/ppermute | solution.py:14
  60.1 7.2 %collective-permute-start.17 = (bf16[256,256]{1,0:T(8,128)(2,1)S(1)}, bf16[256,256]{1,0:T(8,128)(2,1)S(1)}, u32[]{:S(2)}, u32[]{:S(2)}) collective-permute-start(bf16[256,256]{1,0:T(8,128)(2,1)S(1)} %slice.220), channel_id=1, source_target_pairs={{0,16},{4,20},{8,24},{12,28},{16,0},{20,4},{24,8},{28,12},{1,17},{... | collective-permute-start | bytes 393224 | tf_op jit(solution)/shard_map/ppermute | solution.py:14
  68.9 16.2 %collective-permute-start.18 = (bf16[96,2048]{1,0:T(8,128)(2,1)S(1)}, bf16[96,2048]{1,0:T(8,128)(2,1)S(1)}, u32[]{:S(2)}, u32[]{:S(2)}) collective-permute-start(bf16[96,2048]{1,0:T(8,128)(2,1)S(1)} %pad_maximum_fusion.1), channel_id=1, source_target_pairs={{0,1},{1,0},{2,3},{3,2},{4,5},{5,4},{6,7},{7,6},{8,9},{9,8},{10,11... | collective-permute-start | bytes 1179656 | tf_op jit(solution)/shard_map/ppermute | solution.py:14
  70.1 23.0 %collective-permute-start.14 = (bf16[128,1024]{1,0:T(8,128)(2,1)S(1)}, bf16[128,1024]{1,0:T(8,128)(2,1)S(1)}, u32[]{:S(2)}, u32[]{:S(2)}) collective-permute-start(bf16[128,1024]{1,0:T(8,128)(2,1)S(1)} %dynamic-slice_convert_fusion), channel_id=1, source_target_pairs={{0,2},{1,3},{2,0},{3,1},{4,6},{5,7},{6,4},{7,5},{8,10},{9,11},{10,... | collective-permute-start | bytes 786440 | tf_op jit(solution)/shard_map/ppermute | solution.py:14
  74.5 23.4 %collective-permute-start.20 = (bf16[80,2048]{1,0:T(8,128)(2,1)S(1)}, bf16[80,2048]{1,0:T(8,128)(2,1)S(1)}, u32[]{:S(2)}, u32[]{:S(2)}) collective-permute-start(bf16[80,2048]{1,0:T(8,128)(2,1)S(1)} %pad_maximum_fusion.2), channel_id=1, source_target_pairs={{0,1},{1,0},{2,3},{3,2},{4,5},{5,4},{6,7},{7,6},{8,9},{9,8},{10,11... | collective-permute-start | bytes 983048 | tf_op jit(solution)/shard_map/ppermute | solution.py:14
  85.3 21.9 %collective-permute-start.19 = (bf16[96,1024]{1,0:T(8,128)(2,1)S(1)}, bf16[96,1024]{1,0:T(8,128)(2,1)S(1)}, u32[]{:S(2)}, u32[]{:S(2)}) collective-permute-start(bf16[96,1024]{1,0:T(8,128)(2,1)S(1)} %dynamic-slice_convert_fusion.3), channel_id=1, source_target_pairs={{0,2},{1,3},{2,0},{3,1},{4,6},{5,7},{6,4},{7,5},{8,10},{9,11},{10,... | collective-permute-start | bytes 589832 | tf_op jit(solution)/shard_map/ppermute | solution.py:14
  88.3 13.2 %collective-permute-start.22 = (bf16[48,2048]{1,0:T(8,128)(2,1)S(1)}, bf16[48,2048]{1,0:T(8,128)(2,1)S(1)}, u32[]{:S(2)}, u32[]{:S(2)}) collective-permute-start(bf16[48,2048]{1,0:T(8,128)(2,1)S(1)} %pad_maximum_fusion.5), channel_id=1, source_target_pairs={{0,1},{1,0},{2,3},{3,2},{4,5},{5,4},{6,7},{7,6},{8,9},{9,8},{10,11... | collective-permute-start | bytes 589832 | tf_op jit(solution)/shard_map/ppermute | solution.py:14
  93.0 11.9 %collective-permute-start.24 = (bf16[32,2048]{1,0:T(8,128)(2,1)S(1)}, bf16[32,2048]{1,0:T(8,128)(2,1)S(1)}, u32[]{:S(2)}, u32[]{:S(2)}) collective-permute-start(bf16[32,2048]{1,0:T(8,128)(2,1)S(1)} %pad_maximum_fusion.7), channel_id=1, source_target_pairs={{0,1},{1,0},{2,3},{3,2},{4,5},{5,4},{6,7},{7,6},{8,9},{9,8},{10,11... | collective-permute-start | bytes 393224 | tf_op jit(solution)/shard_map/ppermute | solution.py:14
  93.2 21.8 %collective-permute-start.26 = (bf16[128,1024]{1,0:T(8,128)(2,1)S(1)}, bf16[128,1024]{1,0:T(8,128)(2,1)S(1)}, u32[]{:S(2)}, u32[]{:S(2)}) collective-permute-start(bf16[128,1024]{1,0:T(8,128)(2,1)S(1)} %get-tuple-element.71), channel_id=1, source_target_pairs={{0,16},{4,20},{8,24},{12,28},{16,0},{20,4},{24,8},{28,12},{1,17},{... | collective-permute-start | bytes 786440 | tf_op jit(solution)/shard_map/ppermute | solution.py:14
  98.0 13.2 %collective-permute-start.21 = (bf16[80,1024]{1,0:T(8,128)(2,1)S(1)}, bf16[80,1024]{1,0:T(8,128)(2,1)S(1)}, u32[]{:S(2)}, u32[]{:S(2)}) collective-permute-start(bf16[80,1024]{1,0:T(8,128)(2,1)S(1)} %dynamic-slice_convert_fusion.6), channel_id=1, source_target_pairs={{0,2},{1,3},{2,0},{3,1},{4,6},{5,7},{6,4},{7,5},{8,10},{9,11},{10,... | collective-permute-start | bytes 491528 | tf_op jit(solution)/shard_map/ppermute | solution.py:14
  101.6 11.2 %collective-permute-start.23 = (bf16[48,1024]{1,0:T(8,128)(2,1)S(1)}, bf16[48,1024]{1,0:T(8,128)(2,1)S(1)}, u32[]{:S(2)}, u32[]{:S(2)}) collective-permute-start(bf16[48,1024]{1,0:T(8,128)(2,1)S(1)} %dynamic-slice_convert_fusion.9), channel_id=1, source_target_pairs={{0,2},{1,3},{2,0},{3,1},{4,6},{5,7},{6,4},{7,5},{8,10},{9,11},{10,... | collective-permute-start | bytes 294920 | tf_op jit(solution)/shard_map/ppermute | solution.py:14
  104.9 9.0 %collective-permute-start.25 = (bf16[32,1024]{1,0:T(8,128)(2,1)S(1)}, bf16[32,1024]{1,0:T(8,128)(2,1)S(1)}, u32[]{:S(2)}, u32[]{:S(2)}) collective-permute-start(bf16[32,1024]{1,0:T(8,128)(2,1)S(1)} %dynamic-slice_convert_fusion.12), channel_id=1, source_target_pairs={{0,2},{1,3},{2,0},{3,1},{4,6},{5,7},{6,4},{7,5},{8,10},{9,11},{10,... | collective-permute-start | bytes 196616 | tf_op jit(solution)/shard_map/ppermute | solution.py:14
  107.3 7.8 %collective-permute-start.27 = (bf16[96,1024]{1,0:T(8,128)(2,1)S(1)}, bf16[96,1024]{1,0:T(8,128)(2,1)S(1)}, u32[]{:S(2)}, u32[]{:S(2)}) collective-permute-start(bf16[96,1024]{1,0:T(8,128)(2,1)S(1)} %get-tuple-element.73), channel_id=1, source_target_pairs={{0,16},{4,20},{8,24},{12,28},{16,0},{20,4},{24,8},{28,12},{1,17},{... | collective-permute-start | bytes 589832 | tf_op jit(solution)/shard_map/ppermute | solution.py:14
  111.2 5.4 %collective-permute-start.28 = (bf16[80,1024]{1,0:T(8,128)(2,1)S(1)}, bf16[80,1024]{1,0:T(8,128)(2,1)S(1)}, u32[]{:S(2)}, u32[]{:S(2)}) collective-permute-start(bf16[80,1024]{1,0:T(8,128)(2,1)S(1)} %get-tuple-element.75), channel_id=1, source_target_pairs={{0,16},{4,20},{8,24},{12,28},{16,0},{20,4},{24,8},{28,12},{1,17},{... | collective-permute-start | bytes 491528 | tf_op jit(solution)/shard_map/ppermute | solution.py:14
  112.8 4.8 %collective-permute-start.29 = (bf16[48,1024]{1,0:T(8,128)(2,1)S(1)}, bf16[48,1024]{1,0:T(8,128)(2,1)S(1)}, u32[]{:S(2)}, u32[]{:S(2)}) collective-permute-start(bf16[48,1024]{1,0:T(8,128)(2,1)S(1)} %get-tuple-element.85), channel_id=1, source_target_pairs={{0,16},{4,20},{8,24},{12,28},{16,0},{20,4},{24,8},{28,12},{1,17},{... | collective-permute-start | bytes 294920 | tf_op jit(solution)/shard_map/ppermute | solution.py:14
  113.9 4.5 %collective-permute-start.30 = (bf16[32,1024]{1,0:T(8,128)(2,1)S(1)}, bf16[32,1024]{1,0:T(8,128)(2,1)S(1)}, u32[]{:S(2)}, u32[]{:S(2)}) collective-permute-start(bf16[32,1024]{1,0:T(8,128)(2,1)S(1)} %get-tuple-element.87), channel_id=1, source_target_pairs={{0,16},{4,20},{8,24},{12,28},{16,0},{20,4},{24,8},{28,12},{1,17},{... | collective-permute-start | bytes 196616 | tf_op jit(solution)/shard_map/ppermute | solution.py:14
  (3 other events, 38.9 us)

commit v2 on v1

--- a/solution.py
+++ b/solution.py
@@ -120,26 +120,41 @@
         total = pair[0] + after(block, *before).astype(F32)
         return halves(total, "img", bit) if bit < lax.axis_size("img") else (total, total.astype(BF16))
 
-    first, came, pairs = [], [], []
+    def gives(*cut):
+        return [give for keep, give in cut]
+
+    first, pairs, second = [], [], []
+    came, came_second = [], []
+
+    def begin_second(c):
+        before = gives(*pairs[-1:]) + (gives(second[c - 2]) if 2 < c < len(chunks) - 1 else [])
+        pairs.append(onward(first[c], came[c], 2, before))
+        came_second.append(swap(pairs[c][1], "img", 2))
+        if c:
+            end_second(c - 1)
+
+    def end_second(c):
+        before = gives(*second[-1:], *pairs[c + 1 : c + 2])
+        second.append(onward(pairs[c], came_second[c], 4, before))
+
     for c, at in enumerate(chunks):
         w = jnp.concatenate([mean(m, at) for m in order], axis=1)
-        w = after(w, *[give for keep, give in first[-1:] + (pairs[-1:] if 1 < c < len(chunks) - 1 else [])])
+        w = after(w, *gives(*first[-1:], *(pairs[-1:] if 1 < c < len(chunks) - 1 else [])))
         first.append(halves(jnp.dot(w, every_image, preferred_element_type=F32) * scale, "img", 1))
         came.append(swap(first[c][1], "img", 1))
         if c == 0:
             for m in parted:
                 send(m ^ apart, early, half, first[0][1])
         if c:
-            pairs.append(onward(first[c - 1], came[c - 1], 2, [give for keep, give in pairs[-1:]]))
-    pairs.append(onward(first[-1], came[-1], 2, [pairs[-1][1]]))
-    bit = 2
+            begin_second(c - 1)
+    begin_second(len(chunks) - 1)
+    end_second(len(chunks) - 1)
+    pairs = second
+    bit = 4
     while bit < lax.axis_size("img"):
         came = [swap(give, "img", bit) for keep, give in pairs]
         bit *= 2
-        after_it = []
-        for c, (pair, block) in enumerate(zip(pairs, came)):
-            after_it.append(onward(pair, block, bit, [give for keep, give in after_it[-1:] + pairs[c + 1 : c + 2]]))
-        pairs = after_it
+        pairs = [onward(pair, block, bit, []) for pair, block in zip(pairs, came)]
     done = [keep for keep, give in pairs]
     gone = [give for keep, give in pairs]
     other = [swap(block, "ref", top).astype(F32) for block in gone]

time: 122 us -> 122 us (level)
  no operation moved by 1% of the time
where the time goes in v2:
time: 122 us
  starting transfers between devices  42.5 us (35%)
  waiting for transfers between devices  41.5 us (34%)
  matrix products  28.3 us (23%)
  local copies, waits for them, and re-layouts  6.8 us (6%)
  other arithmetic  2.17 us (2%)
    ppermute x31, starting transfers between devices, swap(): return lax.ppermute(block, axis, [(i, i ^ bit) for i in range(count)])  42.5 us
    ppermute x31, waiting for transfers between devices, swap(): return lax.ppermute(block, axis, [(i, i ^ bit) for i in range(count)])  41.5 us
    dot_general x4, matrix products, score(): lax.dot_general(refs, images_of([m]), (((1,), (1,)), ((), ())), preferred...  10.9 us
    dot_general x1, matrix products, body(): refs = jnp.dot(one_hot, references, preferred_element_type=F32).astype(BF16)  9.89 us
    dot_general x5, matrix products, body(): jnp.dot(w, every_image, preferred_element_type=F32) * scale  7.48 us
    gather x1, local copies, waits for them, and re-layouts, body(): jnp.concatenate(done + other, axis=0).at[place]  3.61 us
  transfers between devices with their start and end apart: 31, of which 16 were waited for; matrix products, arithmetic and copies ran while one was open for 26% of the time, Pallas kernels for 0%

profile of v2, /device:TPU:0, one launch (start us, length us, event | category | flops | bytes accessed | tf_op | source)
XLA Modules:
  0.0 122.0 jit_solution(9260559255340675432)
XLA Ops:
  0.0 3.0 %collective-permute-start.1 = (bf16[128,4096]{1,0:T(8,128)(2,1)}, bf16[128,4096]{1,0:T(8,128)(2,1)S(1)}, u32[]{:S(2)}, u32[]{:S(2)}) collective-permute-start(bf16[128,4096]{1,0:T(8,128)(2,1)} %param.4), channel_id=1, source_target_pairs={{0,16},{4,20},{8,24},{12,28},{16,0},{20,4},{24,8},{28,12},{1,17},{... | collective-permute-start | bytes 3145736 | tf_op jit(solution)/shard_map/ppermute | solution.py:14
  5.2 9.9 %multiply_reduce_fusion = (f32[768]{0:T(1024)S(1)}, bf16[768,4096]{1,0:T(8,128)(2,1)}) fusion(bf16[768,4096]{1,0:T(8,128)(2,1)} %param.6, s32[768]{0:T(1024)S(1)} %get-tuple-element.58), kind=kOutput, calls=%fused_computation.2 | convolution fusion | flops 4845009920 | bytes 12589056 | tf_op jit(solution)/shard_map/dot_general | solution.py:54
  15.7 5.0 %fusion.74 = bf16[768,256]{1,0:T(8,128)(2,1)S(1)} fusion(bf16[768,4096]{1,0:T(8,128)(2,1)} %get-tuple-element.94, bf16[128,4096]{1,0:T(8,128)(2,1)} %collective-permute-done, bf16[128,4096]{1,0:T(8,128)(2,1)S(1)} %copy-done.1, f32[256]{0:T(256)S(1)} %get-tuple-element.92, f32[768]{0:T(1024)S(1)} %broadcast_multiply_fusion), kind=kOutput, calls=%fused_computation.48 | convolution fusion | flops 1615593472 | bytes 8785920 | tf_op jit(solution)/shard_map/dot_general | solution.py:68
  20.8 5.6 %collective-permute-done.1 = bf16[128,4096]{1,0:T(8,128)(2,1)S(1)} collective-permute-done((bf16[128,4096]{1,0:T(8,128)(2,1)}, bf16[128,4096]{1,0:T(8,128)(2,1)S(1)}, u32[]{:S(2)}, u32[]{:S(2)}) %collective-permute-start.1) | collective-permute-done | bytes 1048608 | tf_op jit(solution)/shard_map/ppermute | solution.py:14
  26.5 1.8 %collective-permute-start.6 = (bf16[80,4096]{1,0:T(8,128)(2,1)S(1)}, bf16[80,4096]{1,0:T(8,128)(2,1)S(1)}, u32[]{:S(2)}, u32[]{:S(2)}) collective-permute-start(bf16[80,4096]{1,0:T(8,128)(2,1)S(1)} %slice.154), channel_id=1, source_target_pairs={{0,8},{4,12},{8,0},{12,4},{16,24},{20,28},{24,16},{28,20},{1,9},{5... | collective-permute-start | bytes 1966088 | tf_op jit(solution)/shard_map/ppermute | solution.py:14
  29.9 2.0 %fusion.71 = bf16[768,256]{1,0:T(8,128)(2,1)S(1)} fusion(bf16[768,4096]{1,0:T(8,128)(2,1)S(1)} %bitcast.28, bf16[128,4096]{1,0:T(8,128)(2,1)S(1)} %collective-permute-done.2, bf16[128,4096]{1,0:T(8,128)(2,1)S(1)} %collective-permute-done.1, f32[256]{0:T(256)S(1)} %get-tuple-element.91, f32[768]{0:T(1024)S(1)} %broadcast_multiply_fusion), kind=kOutput, calls=%fused_computation.47 | convolution fusion | flops 1615593472 | bytes 8785920 | tf_op jit(solution)/shard_map/dot_general | solution.py:68
  32.1 1.6 %collective-permute-start.7 = (bf16[48,4096]{1,0:T(8,128)(2,1)S(1)}, bf16[48,4096]{1,0:T(8,128)(2,1)S(1)}, u32[]{:S(2)}, u32[]{:S(2)}) collective-permute-start(bf16[48,4096]{1,0:T(8,128)(2,1)S(1)} %slice.156), channel_id=1, source_target_pairs={{0,16},{4,20},{8,24},{12,28},{16,0},{20,4},{24,8},{28,12},{1,17},{... | collective-permute-start | bytes 1179656 | tf_op jit(solution)/shard_map/ppermute | solution.py:14
  33.7 2.0 %fusion.68 = bf16[768,256]{1,0:T(8,128)(2,1)S(1)} fusion(bf16[768,4096]{1,0:T(8,128)(2,1)S(1)} %bitcast.28, bf16[128,4096]{1,0:T(8,128)(2,1)S(1)} %collective-permute-done.4, bf16[128,4096]{1,0:T(8,128)(2,1)S(1)} %collective-permute-done.3, f32[256]{0:T(256)S(1)} %get-tuple-element.90, f32[768]{0:T(1024)S(1)} %broadcast_multiply_fusion), kind=kOutput, calls=%fused_computation.46 | convolution fusion | flops 1615593472 | bytes 8785920 | tf_op jit(solution)/shard_map/dot_general | solution.py:68
  36.3 1.5 %collective-permute-start.11 = (bf16[384,256]{1,0:T(8,128)(2,1)S(1)}, bf16[384,256]{1,0:T(8,128)(2,1)S(1)}, u32[]{:S(2)}, u32[]{:S(2)}) collective-permute-start(bf16[384,256]{1,0:T(8,128)(2,1)S(1)} %slice.209), channel_id=1, source_target_pairs={{0,16},{4,20},{8,24},{12,28},{16,0},{20,4},{24,8},{28,12},{1,17},{... | collective-permute-start | bytes 589832 | tf_op jit(solution)/shard_map/ppermute | solution.py:14
  37.8 6.3 %collective-permute-done.7 = bf16[48,4096]{1,0:T(8,128)(2,1)S(1)} collective-permute-done((bf16[48,4096]{1,0:T(8,128)(2,1)S(1)}, bf16[48,4096]{1,0:T(8,128)(2,1)S(1)}, u32[]{:S(2)}, u32[]{:S(2)}) %collective-permute-start.7) | collective-permute-done | bytes 393248 | tf_op jit(solution)/shard_map/ppermute | solution.py:14
  45.8 1.5 %collective-permute-start.12 = (bf16[128,256]{1,0:T(8,128)(2,1)S(1)}, bf16[128,256]{1,0:T(8,128)(2,1)S(1)}, u32[]{:S(2)}, u32[]{:S(2)}) collective-permute-start(bf16[128,256]{1,0:T(8,128)(2,1)S(1)} %slice.211), channel_id=1, source_target_pairs={{0,16},{4,20},{8,24},{12,28},{16,0},{20,4},{24,8},{28,12},{1,17},{... | collective-permute-start | bytes 196616 | tf_op jit(solution)/shard_map/ppermute | solution.py:14
  47.3 1.8 %fusion.77 = bf16[768,256]{1,0:T(8,128)(2,1)S(1)} fusion(bf16[768,4096]{1,0:T(8,128)(2,1)S(1)} %bitcast.28, bf16[48,4096]{1,0:T(8,128)(2,1)S(1)} %collective-permute-done.9, bf16[80,4096]{1,0:T(8,128)(2,1)S(1)} %collective-permute-done.8, bf16[48,4096]{1,0:T(8,128)(2,1)S(1)} %collective-permute-done.7, bf16[80,4096]{1,0:T(8,128)(2,1)S(1)} %collective-permute-done.6, ...), kind=kOutput, calls=%fused_computation.49 | convolution fusion | flops 1619787776 | bytes 8785920 | tf_op jit(solution)/shard_map/dot_general | solution.py:68
  50.5 1.6 %collective-permute-start.10 = (bf16[128,256]{1,0:T(8,128)(2,1)S(1)}, bf16[128,256]{1,0:T(8,128)(2,1)S(1)}, u32[]{:S(2)}, u32[]{:S(2)}) collective-permute-start(bf16[128,256]{1,0:T(8,128)(2,1)S(1)} %slice.207), channel_id=1, source_target_pairs={{0,16},{4,20},{8,24},{12,28},{16,0},{20,4},{24,8},{28,12},{1,17},{... | collective-permute-start | bytes 196616 | tf_op jit(solution)/shard_map/ppermute | solution.py:14
  52.2 2.6 %collective-permute-done.10 = bf16[128,256]{1,0:T(8,128)(2,1)S(1)} collective-permute-done((bf16[128,256]{1,0:T(8,128)(2,1)S(1)}, bf16[128,256]{1,0:T(8,128)(2,1)S(1)}, u32[]{:S(2)}, u32[]{:S(2)}) %collective-permute-start.10) | collective-permute-done | bytes 65568 | tf_op jit(solution)/shard_map/ppermute | solution.py:14
  56.4 1.6 %collective-permute-start.13 = (bf16[128,2048]{1,0:T(8,128)(2,1)S(1)}, bf16[128,2048]{1,0:T(8,128)(2,1)S(1)}, u32[]{:S(2)}, u32[]{:S(2)}) collective-permute-start(bf16[128,2048]{1,0:T(8,128)(2,1)S(1)} %pad_maximum_fusion), channel_id=1, source_target_pairs={{0,1},{1,0},{2,3},{3,2},{4,5},{5,4},{6,7},{7,6},{8,9},{9,8},{10,11... | collective-permute-start | bytes 1572872 | tf_op jit(solution)/shard_map/ppermute | solution.py:14
  61.7 2.8 %collective-permute-done.15 = bf16[256,256]{1,0:T(8,128)(2,1)S(1)} collective-permute-done((bf16[256,256]{1,0:T(8,128)(2,1)S(1)}, bf16[256,256]{1,0:T(8,128)(2,1)S(1)}, u32[]{:S(2)}, u32[]{:S(2)}) %collective-permute-start.15) | collective-permute-done | bytes 131104 | tf_op jit(solution)/shard_map/ppermute | solution.py:14
  70.1 2.7 %collective-permute-start.14 = (bf16[128,1024]{1,0:T(8,128)(2,1)S(1)}, bf16[128,1024]{1,0:T(8,128)(2,1)S(1)}, u32[]{:S(2)}, u32[]{:S(2)}) collective-permute-start(bf16[128,1024]{1,0:T(8,128)(2,1)S(1)} %dynamic-slice_convert_fusion), channel_id=1, source_target_pairs={{0,2},{1,3},{2,0},{3,1},{4,6},{5,7},{6,4},{7,5},{8,10},{9,11},{10,... | collective-permute-start | bytes 786440 | tf_op jit(solution)/shard_map/ppermute | solution.py:14
  72.8 1.6 %convolution_multiply_fusion.2 = f32[80,4096]{1,0:T(8,128)S(1)} fusion(bf16[80,1024]{1,0:T(8,128)(2,1)S(1)} %pad_maximum_fusion.6, bf16[1024,4096]{1,0:T(8,128)(2,1)S(1)} %constant_dynamic-update-slice_fusion), kind=kOutput, calls=%fused_computation.6 | convolution fusion | flops 671416320 | bytes 9863168 | tf_op jit(solution)/shard_map/dot_general | solution.py:143
  74.4 1.7 %collective-permute-start.20 = (bf16[80,2048]{1,0:T(8,128)(2,1)S(1)}, bf16[80,2048]{1,0:T(8,128)(2,1)S(1)}, u32[]{:S(2)}, u32[]{:S(2)}) collective-permute-start(bf16[80,2048]{1,0:T(8,128)(2,1)S(1)} %pad_maximum_fusion.2), channel_id=1, source_target_pairs={{0,1},{1,0},{2,3},{3,2},{4,5},{5,4},{6,7},{7,6},{8,9},{9,8},{10,11... | collective-permute-start | bytes 983048 | tf_op jit(solution)/shard_map/ppermute | solution.py:14
  76.2 9.0 %collective-permute-done.18 = bf16[96,2048]{1,0:T(8,128)(2,1)S(1)} collective-permute-done((bf16[96,2048]{1,0:T(8,128)(2,1)S(1)}, bf16[96,2048]{1,0:T(8,128)(2,1)S(1)}, u32[]{:S(2)}, u32[]{:S(2)}) %collective-permute-start.18) | collective-permute-done | bytes 393248 | tf_op jit(solution)/shard_map/ppermute | solution.py:14
  86.7 1.6 %convolution_multiply_fusion.3 = f32[48,4096]{1,0:T(8,128)S(1)} fusion(bf16[48,1024]{1,0:T(8,128)(2,1)S(1)} %pad_maximum_fusion.8, bf16[1024,4096]{1,0:T(8,128)(2,1)S(1)} %constant_dynamic-update-slice_fusion), kind=kOutput, calls=%fused_computation.7 | convolution fusion | flops 402849792 | bytes 9273344 | tf_op jit(solution)/shard_map/dot_general | solution.py:143
  88.4 3.0 %collective-permute-start.22 = (bf16[48,2048]{1,0:T(8,128)(2,1)S(1)}, bf16[48,2048]{1,0:T(8,128)(2,1)S(1)}, u32[]{:S(2)}, u32[]{:S(2)}) collective-permute-start(bf16[48,2048]{1,0:T(8,128)(2,1)S(1)} %pad_maximum_fusion.5), channel_id=1, source_target_pairs={{0,1},{1,0},{2,3},{3,2},{4,5},{5,4},{6,7},{7,6},{8,9},{9,8},{10,11... | collective-permute-start | bytes 589832 | tf_op jit(solution)/shard_map/ppermute | solution.py:14
  91.4 1.5 %convolution_multiply_fusion.4 = f32[32,4096]{1,0:T(8,128)S(1)} fusion(bf16[32,1024]{1,0:T(8,128)(2,1)S(1)} %pad_maximum_fusion.9, bf16[1024,4096]{1,0:T(8,128)(2,1)S(1)} %constant_dynamic-update-slice_fusion), kind=kOutput, calls=%fused_computation.8 | convolution fusion | flops 268566528 | bytes 8978432 | tf_op jit(solution)/shard_map/dot_general | solution.py:143
  93.2 1.6 %collective-permute-start.26 = (bf16[128,1024]{1,0:T(8,128)(2,1)S(1)}, bf16[128,1024]{1,0:T(8,128)(2,1)S(1)}, u32[]{:S(2)}, u32[]{:S(2)}) collective-permute-start(bf16[128,1024]{1,0:T(8,128)(2,1)S(1)} %get-tuple-element.71), channel_id=1, source_target_pairs={{0,16},{4,20},{8,24},{12,28},{16,0},{20,4},{24,8},{28,12},{1,17},{... | collective-permute-start | bytes 786440 | tf_op jit(solution)/shard_map/ppermute | solution.py:14
  94.8 3.1 %collective-permute-done.20 = bf16[80,2048]{1,0:T(8,128)(2,1)S(1)} collective-permute-done((bf16[80,2048]{1,0:T(8,128)(2,1)S(1)}, bf16[80,2048]{1,0:T(8,128)(2,1)S(1)}, u32[]{:S(2)}, u32[]{:S(2)}) %collective-permute-start.20) | collective-permute-done | bytes 327712 | tf_op jit(solution)/shard_map/ppermute | solution.py:14
  98.0 1.8 %collective-permute-start.21 = (bf16[80,1024]{1,0:T(8,128)(2,1)S(1)}, bf16[80,1024]{1,0:T(8,128)(2,1)S(1)}, u32[]{:S(2)}, u32[]{:S(2)}) collective-permute-start(bf16[80,1024]{1,0:T(8,128)(2,1)S(1)} %dynamic-slice_convert_fusion.6), channel_id=1, source_target_pairs={{0,2},{1,3},{2,0},{3,1},{4,6},{5,7},{6,4},{7,5},{8,10},{9,11},{10,... | collective-permute-start | bytes 491528 | tf_op jit(solution)/shard_map/ppermute | solution.py:14
  99.9 1.6 %collective-permute-start.27 = (bf16[96,1024]{1,0:T(8,128)(2,1)S(1)}, bf16[96,1024]{1,0:T(8,128)(2,1)S(1)}, u32[]{:S(2)}, u32[]{:S(2)}) collective-permute-start(bf16[96,1024]{1,0:T(8,128)(2,1)S(1)} %get-tuple-element.73), channel_id=1, source_target_pairs={{0,16},{4,20},{8,24},{12,28},{16,0},{20,4},{24,8},{28,12},{1,17},{... | collective-permute-start | bytes 589832 | tf_op jit(solution)/shard_map/ppermute | solution.py:14
  101.6 3.2 %collective-permute-start.23 = (bf16[48,1024]{1,0:T(8,128)(2,1)S(1)}, bf16[48,1024]{1,0:T(8,128)(2,1)S(1)}, u32[]{:S(2)}, u32[]{:S(2)}) collective-permute-start(bf16[48,1024]{1,0:T(8,128)(2,1)S(1)} %dynamic-slice_convert_fusion.9), channel_id=1, source_target_pairs={{0,2},{1,3},{2,0},{3,1},{4,6},{5,7},{6,4},{7,5},{8,10},{9,11},{10,... | collective-permute-start | bytes 294920 | tf_op jit(solution)/shard_map/ppermute | solution.py:14
  104.9 2.3 %collective-permute-start.25 = (bf16[32,1024]{1,0:T(8,128)(2,1)S(1)}, bf16[32,1024]{1,0:T(8,128)(2,1)S(1)}, u32[]{:S(2)}, u32[]{:S(2)}) collective-permute-start(bf16[32,1024]{1,0:T(8,128)(2,1)S(1)} %dynamic-slice_convert_fusion.12), channel_id=1, source_target_pairs={{0,2},{1,3},{2,0},{3,1},{4,6},{5,7},{6,4},{7,5},{8,10},{9,11},{10,... | collective-permute-start | bytes 196616 | tf_op jit(solution)/shard_map/ppermute | solution.py:14
  107.2 4.0 %collective-permute-done.21 = bf16[80,1024]{1,0:T(8,128)(2,1)S(1)} collective-permute-done((bf16[80,1024]{1,0:T(8,128)(2,1)S(1)}, bf16[80,1024]{1,0:T(8,128)(2,1)S(1)}, u32[]{:S(2)}, u32[]{:S(2)}) %collective-permute-start.21) | collective-permute-done | bytes 163872 | tf_op jit(solution)/shard_map/ppermute | solution.py:14
  111.2 1.6 %collective-permute-start.28 = (bf16[80,1024]{1,0:T(8,128)(2,1)S(1)}, bf16[80,1024]{1,0:T(8,128)(2,1)S(1)}, u32[]{:S(2)}, u32[]{:S(2)}) collective-permute-start(bf16[80,1024]{1,0:T(8,128)(2,1)S(1)} %get-tuple-element.75), channel_id=1, source_target_pairs={{0,16},{4,20},{8,24},{12,28},{16,0},{20,4},{24,8},{28,12},{1,17},{... | collective-permute-start | bytes 491528 | tf_op jit(solution)/shard_map/ppermute | solution.py:14
  118.4 3.6 %gather_fusion.1 = f32[768,1024]{1,0:T(8,128)} fusion(f32[768,1024]{1,0:T(8,128)S(1)} %convert_dynamic-update-slice_fusion.4, s32[1024]{0:T(1024)S(1)} %pad_clamp_fusion), kind=kCustom, calls=%fused_computation.1 | custom fusion | bytes 6294528 | tf_op jit(solution)/shard_map/gather | solution.py:161
  (136 shorter events, 26.9 us)
Async XLA Ops:
  0.0 15.1 %copy-start = (s32[1024]{0:T(1024)S(1)}, s32[1024]{0:T(1024)}, u32[]{:S(2)}) copy-start(s32[1024]{0:T(1024)} %param.5) | copy-start | bytes 12292
  0.0 26.3 %collective-permute-start.1 = (bf16[128,4096]{1,0:T(8,128)(2,1)}, bf16[128,4096]{1,0:T(8,128)(2,1)S(1)}, u32[]{:S(2)}, u32[]{:S(2)}) collective-permute-start(bf16[128,4096]{1,0:T(8,128)(2,1)} %param.4), channel_id=1, source_target_pairs={{0,16},{4,20},{8,24},{12,28},{16,0},{20,4},{24,8},{28,12},{1,17},{... | collective-permute-start | bytes 3145736 | tf_op jit(solution)/shard_map/ppermute | solution.py:14
  3.0 12.7 %collective-permute-start = (bf16[128,4096]{1,0:T(8,128)(2,1)}, bf16[128,4096]{1,0:T(8,128)(2,1)}, u32[]{:S(2)}, u32[]{:S(2)}) collective-permute-start(bf16[128,4096]{1,0:T(8,128)(2,1)} %param.4), channel_id=1, source_target_pairs={{0,4},{4,0},{8,12},{12,8},{16,20},{20,16},{24,28},{28,24},{1,5},{5... | collective-permute-start | bytes 3145736 | tf_op jit(solution)/shard_map/ppermute | solution.py:14
  3.0 26.6 %collective-permute-start.3 = (bf16[128,4096]{1,0:T(8,128)(2,1)}, bf16[128,4096]{1,0:T(8,128)(2,1)S(1)}, u32[]{:S(2)}, u32[]{:S(2)}) collective-permute-start(bf16[128,4096]{1,0:T(8,128)(2,1)} %param.4), channel_id=1, source_target_pairs={{0,8},{4,12},{8,0},{12,4},{16,24},{20,28},{24,16},{28,20},{1,9},{5... | collective-permute-start | bytes 3145736 | tf_op jit(solution)/shard_map/ppermute | solution.py:14
  26.3 3.3 %collective-permute-start.2 = (bf16[128,4096]{1,0:T(8,128)(2,1)S(1)}, bf16[128,4096]{1,0:T(8,128)(2,1)S(1)}, u32[]{:S(2)}, u32[]{:S(2)}) collective-permute-start(bf16[128,4096]{1,0:T(8,128)(2,1)S(1)} %collective-permute-done.1), channel_id=1, source_target_pairs={{0,4},{4,0},{8,12},{12,8},{16,20},{20,16},{24,28},{28,24},{1,5},{5... | collective-permute-start | bytes 3145736 | tf_op jit(solution)/shard_map/ppermute | solution.py:14
  26.5 17.6 %collective-permute-start.6 = (bf16[80,4096]{1,0:T(8,128)(2,1)S(1)}, bf16[80,4096]{1,0:T(8,128)(2,1)S(1)}, u32[]{:S(2)}, u32[]{:S(2)}) collective-permute-start(bf16[80,4096]{1,0:T(8,128)(2,1)S(1)} %slice.154), channel_id=1, source_target_pairs={{0,8},{4,12},{8,0},{12,4},{16,24},{20,28},{24,16},{28,20},{1,9},{5... | collective-permute-start | bytes 1966088 | tf_op jit(solution)/shard_map/ppermute | solution.py:14
  29.6 4.1 %collective-permute-start.4 = (bf16[128,4096]{1,0:T(8,128)(2,1)S(1)}, bf16[128,4096]{1,0:T(8,128)(2,1)S(1)}, u32[]{:S(2)}, u32[]{:S(2)}) collective-permute-start(bf16[128,4096]{1,0:T(8,128)(2,1)S(1)} %collective-permute-done.3), channel_id=1, source_target_pairs={{0,4},{4,0},{8,12},{12,8},{16,20},{20,16},{24,28},{28,24},{1,5},{5... | collective-permute-start | bytes 3145736 | tf_op jit(solution)/shard_map/ppermute | solution.py:14
  32.1 12.0 %collective-permute-start.7 = (bf16[48,4096]{1,0:T(8,128)(2,1)S(1)}, bf16[48,4096]{1,0:T(8,128)(2,1)S(1)}, u32[]{:S(2)}, u32[]{:S(2)}) collective-permute-start(bf16[48,4096]{1,0:T(8,128)(2,1)S(1)} %slice.156), channel_id=1, source_target_pairs={{0,16},{4,20},{8,24},{12,28},{16,0},{20,4},{24,8},{28,12},{1,17},{... | collective-permute-start | bytes 1179656 | tf_op jit(solution)/shard_map/ppermute | solution.py:14
  35.7 14.8 %collective-permute-start.5 = (bf16[128,256]{1,0:T(8,128)(2,1)S(1)}, bf16[128,256]{1,0:T(8,128)(2,1)S(1)}, u32[]{:S(2)}, u32[]{:S(2)}) collective-permute-start(bf16[128,256]{1,0:T(8,128)(2,1)S(1)} %slice.205), channel_id=1, source_target_pairs={{0,16},{4,20},{8,24},{12,28},{16,0},{20,4},{24,8},{28,12},{1,17},{... | collective-permute-start | bytes 196616 | tf_op jit(solution)/shard_map/ppermute | solution.py:14
  36.3 13.3 %collective-permute-start.11 = (bf16[384,256]{1,0:T(8,128)(2,1)S(1)}, bf16[384,256]{1,0:T(8,128)(2,1)S(1)}, u32[]{:S(2)}, u32[]{:S(2)}) collective-permute-start(bf16[384,256]{1,0:T(8,128)(2,1)S(1)} %slice.209), channel_id=1, source_target_pairs={{0,16},{4,20},{8,24},{12,28},{16,0},{20,4},{24,8},{28,12},{1,17},{... | collective-permute-start | bytes 589832 | tf_op jit(solution)/shard_map/ppermute | solution.py:14
  44.1 1.7 %collective-permute-start.9 = (bf16[48,4096]{1,0:T(8,128)(2,1)S(1)}, bf16[48,4096]{1,0:T(8,128)(2,1)S(1)}, u32[]{:S(2)}, u32[]{:S(2)}) collective-permute-start(bf16[48,4096]{1,0:T(8,128)(2,1)S(1)} %collective-permute-done.7), channel_id=1, source_target_pairs={{0,4},{4,0},{8,12},{12,8},{16,20},{20,16},{24,28},{28,24},{1,5},{5... | collective-permute-start | bytes 1179656 | tf_op jit(solution)/shard_map/ppermute | solution.py:14
  44.1 3.2 %collective-permute-start.8 = (bf16[80,4096]{1,0:T(8,128)(2,1)S(1)}, bf16[80,4096]{1,0:T(8,128)(2,1)S(1)}, u32[]{:S(2)}, u32[]{:S(2)}) collective-permute-start(bf16[80,4096]{1,0:T(8,128)(2,1)S(1)} %collective-permute-done.6), channel_id=1, source_target_pairs={{0,4},{4,0},{8,12},{12,8},{16,20},{20,16},{24,28},{28,24},{1,5},{5... | collective-permute-start | bytes 1966088 | tf_op jit(solution)/shard_map/ppermute | solution.py:14
  45.8 4.7 %collective-permute-start.12 = (bf16[128,256]{1,0:T(8,128)(2,1)S(1)}, bf16[128,256]{1,0:T(8,128)(2,1)S(1)}, u32[]{:S(2)}, u32[]{:S(2)}) collective-permute-start(bf16[128,256]{1,0:T(8,128)(2,1)S(1)} %slice.211), channel_id=1, source_target_pairs={{0,16},{4,20},{8,24},{12,28},{16,0},{20,4},{24,8},{28,12},{1,17},{... | collective-permute-start | bytes 196616 | tf_op jit(solution)/shard_map/ppermute | solution.py:14
  50.5 4.3 %collective-permute-start.10 = (bf16[128,256]{1,0:T(8,128)(2,1)S(1)}, bf16[128,256]{1,0:T(8,128)(2,1)S(1)}, u32[]{:S(2)}, u32[]{:S(2)}) collective-permute-start(bf16[128,256]{1,0:T(8,128)(2,1)S(1)} %slice.207), channel_id=1, source_target_pairs={{0,16},{4,20},{8,24},{12,28},{16,0},{20,4},{24,8},{28,12},{1,17},{... | collective-permute-start | bytes 196616 | tf_op jit(solution)/shard_map/ppermute | solution.py:14
  56.4 13.6 %collective-permute-start.13 = (bf16[128,2048]{1,0:T(8,128)(2,1)S(1)}, bf16[128,2048]{1,0:T(8,128)(2,1)S(1)}, u32[]{:S(2)}, u32[]{:S(2)}) collective-permute-start(bf16[128,2048]{1,0:T(8,128)(2,1)S(1)} %pad_maximum_fusion), channel_id=1, source_target_pairs={{0,1},{1,0},{2,3},{3,2},{4,5},{5,4},{6,7},{7,6},{8,9},{9,8},{10,11... | collective-permute-start | bytes 1572872 | tf_op jit(solution)/shard_map/ppermute | solution.py:14
  58.0 6.4 %collective-permute-start.15 = (bf16[256,256]{1,0:T(8,128)(2,1)S(1)}, bf16[256,256]{1,0:T(8,128)(2,1)S(1)}, u32[]{:S(2)}, u32[]{:S(2)}) collective-permute-start(bf16[256,256]{1,0:T(8,128)(2,1)S(1)} %slice.213), channel_id=1, source_target_pairs={{0,16},{4,20},{8,24},{12,28},{16,0},{20,4},{24,8},{28,12},{1,17},{... | collective-permute-start | bytes 393224 | tf_op jit(solution)/shard_map/ppermute | solution.py:14
  59.5 6.3 %collective-permute-start.16 = (bf16[256,256]{1,0:T(8,128)(2,1)S(1)}, bf16[256,256]{1,0:T(8,128)(2,1)S(1)}, u32[]{:S(2)}, u32[]{:S(2)}) collective-permute-start(bf16[256,256]{1,0:T(8,128)(2,1)S(1)} %slice.216), channel_id=1, source_target_pairs={{0,16},{4,20},{8,24},{12,28},{16,0},{20,4},{24,8},{28,12},{1,17},{... | collective-permute-start | bytes 393224 | tf_op jit(solution)/shard_map/ppermute | solution.py:14
  60.1 7.2 %collective-permute-start.17 = (bf16[256,256]{1,0:T(8,128)(2,1)S(1)}, bf16[256,256]{1,0:T(8,128)(2,1)S(1)}, u32[]{:S(2)}, u32[]{:S(2)}) collective-permute-start(bf16[256,256]{1,0:T(8,128)(2,1)S(1)} %slice.220), channel_id=1, source_target_pairs={{0,16},{4,20},{8,24},{12,28},{16,0},{20,4},{24,8},{28,12},{1,17},{... | collective-permute-start | bytes 393224 | tf_op jit(solution)/shard_map/ppermute | solution.py:14
  68.9 16.3 %collective-permute-start.18 = (bf16[96,2048]{1,0:T(8,128)(2,1)S(1)}, bf16[96,2048]{1,0:T(8,128)(2,1)S(1)}, u32[]{:S(2)}, u32[]{:S(2)}) collective-permute-start(bf16[96,2048]{1,0:T(8,128)(2,1)S(1)} %pad_maximum_fusion.1), channel_id=1, source_target_pairs={{0,1},{1,0},{2,3},{3,2},{4,5},{5,4},{6,7},{7,6},{8,9},{9,8},{10,11... | collective-permute-start | bytes 1179656 | tf_op jit(solution)/shard_map/ppermute | solution.py:14
  70.1 23.0 %collective-permute-start.14 = (bf16[128,1024]{1,0:T(8,128)(2,1)S(1)}, bf16[128,1024]{1,0:T(8,128)(2,1)S(1)}, u32[]{:S(2)}, u32[]{:S(2)}) collective-permute-start(bf16[128,1024]{1,0:T(8,128)(2,1)S(1)} %dynamic-slice_convert_fusion), channel_id=1, source_target_pairs={{0,2},{1,3},{2,0},{3,1},{4,6},{5,7},{6,4},{7,5},{8,10},{9,11},{10,... | collective-permute-start | bytes 786440 | tf_op jit(solution)/shard_map/ppermute | solution.py:14
  74.4 23.4 %collective-permute-start.20 = (bf16[80,2048]{1,0:T(8,128)(2,1)S(1)}, bf16[80,2048]{1,0:T(8,128)(2,1)S(1)}, u32[]{:S(2)}, u32[]{:S(2)}) collective-permute-start(bf16[80,2048]{1,0:T(8,128)(2,1)S(1)} %pad_maximum_fusion.2), channel_id=1, source_target_pairs={{0,1},{1,0},{2,3},{3,2},{4,5},{5,4},{6,7},{7,6},{8,9},{9,8},{10,11... | collective-permute-start | bytes 983048 | tf_op jit(solution)/shard_map/ppermute | solution.py:14
  85.3 14.5 %collective-permute-start.19 = (bf16[96,1024]{1,0:T(8,128)(2,1)S(1)}, bf16[96,1024]{1,0:T(8,128)(2,1)S(1)}, u32[]{:S(2)}, u32[]{:S(2)}) collective-permute-start(bf16[96,1024]{1,0:T(8,128)(2,1)S(1)} %dynamic-slice_convert_fusion.3), channel_id=1, source_target_pairs={{0,2},{1,3},{2,0},{3,1},{4,6},{5,7},{6,4},{7,5},{8,10},{9,11},{10,... | collective-permute-start | bytes 589832 | tf_op jit(solution)/shard_map/ppermute | solution.py:14
  88.4 13.1 %collective-permute-start.22 = (bf16[48,2048]{1,0:T(8,128)(2,1)S(1)}, bf16[48,2048]{1,0:T(8,128)(2,1)S(1)}, u32[]{:S(2)}, u32[]{:S(2)}) collective-permute-start(bf16[48,2048]{1,0:T(8,128)(2,1)S(1)} %pad_maximum_fusion.5), channel_id=1, source_target_pairs={{0,1},{1,0},{2,3},{3,2},{4,5},{5,4},{6,7},{7,6},{8,9},{9,8},{10,11... | collective-permute-start | bytes 589832 | tf_op jit(solution)/shard_map/ppermute | solution.py:14
  93.0 11.8 %collective-permute-start.24 = (bf16[32,2048]{1,0:T(8,128)(2,1)S(1)}, bf16[32,2048]{1,0:T(8,128)(2,1)S(1)}, u32[]{:S(2)}, u32[]{:S(2)}) collective-permute-start(bf16[32,2048]{1,0:T(8,128)(2,1)S(1)} %pad_maximum_fusion.7), channel_id=1, source_target_pairs={{0,1},{1,0},{2,3},{3,2},{4,5},{5,4},{6,7},{7,6},{8,9},{9,8},{10,11... | collective-permute-start | bytes 393224 | tf_op jit(solution)/shard_map/ppermute | solution.py:14
  93.2 21.8 %collective-permute-start.26 = (bf16[128,1024]{1,0:T(8,128)(2,1)S(1)}, bf16[128,1024]{1,0:T(8,128)(2,1)S(1)}, u32[]{:S(2)}, u32[]{:S(2)}) collective-permute-start(bf16[128,1024]{1,0:T(8,128)(2,1)S(1)} %get-tuple-element.71), channel_id=1, source_target_pairs={{0,16},{4,20},{8,24},{12,28},{16,0},{20,4},{24,8},{28,12},{1,17},{... | collective-permute-start | bytes 786440 | tf_op jit(solution)/shard_map/ppermute | solution.py:14
  98.0 13.1 %collective-permute-start.21 = (bf16[80,1024]{1,0:T(8,128)(2,1)S(1)}, bf16[80,1024]{1,0:T(8,128)(2,1)S(1)}, u32[]{:S(2)}, u32[]{:S(2)}) collective-permute-start(bf16[80,1024]{1,0:T(8,128)(2,1)S(1)} %dynamic-slice_convert_fusion.6), channel_id=1, source_target_pairs={{0,2},{1,3},{2,0},{3,1},{4,6},{5,7},{6,4},{7,5},{8,10},{9,11},{10,... | collective-permute-start | bytes 491528 | tf_op jit(solution)/shard_map/ppermute | solution.py:14
  99.9 15.2 %collective-permute-start.27 = (bf16[96,1024]{1,0:T(8,128)(2,1)S(1)}, bf16[96,1024]{1,0:T(8,128)(2,1)S(1)}, u32[]{:S(2)}, u32[]{:S(2)}) collective-permute-start(bf16[96,1024]{1,0:T(8,128)(2,1)S(1)} %get-tuple-element.73), channel_id=1, source_target_pairs={{0,16},{4,20},{8,24},{12,28},{16,0},{20,4},{24,8},{28,12},{1,17},{... | collective-permute-start | bytes 589832 | tf_op jit(solution)/shard_map/ppermute | solution.py:14
  101.6 11.2 %collective-permute-start.23 = (bf16[48,1024]{1,0:T(8,128)(2,1)S(1)}, bf16[48,1024]{1,0:T(8,128)(2,1)S(1)}, u32[]{:S(2)}, u32[]{:S(2)}) collective-permute-start(bf16[48,1024]{1,0:T(8,128)(2,1)S(1)} %dynamic-slice_convert_fusion.9), channel_id=1, source_target_pairs={{0,2},{1,3},{2,0},{3,1},{4,6},{5,7},{6,4},{7,5},{8,10},{9,11},{10,... | collective-permute-start | bytes 294920 | tf_op jit(solution)/shard_map/ppermute | solution.py:14
  104.9 9.0 %collective-permute-start.25 = (bf16[32,1024]{1,0:T(8,128)(2,1)S(1)}, bf16[32,1024]{1,0:T(8,128)(2,1)S(1)}, u32[]{:S(2)}, u32[]{:S(2)}) collective-permute-start(bf16[32,1024]{1,0:T(8,128)(2,1)S(1)} %dynamic-slice_convert_fusion.12), channel_id=1, source_target_pairs={{0,2},{1,3},{2,0},{3,1},{4,6},{5,7},{6,4},{7,5},{8,10},{9,11},{10,... | collective-permute-start | bytes 196616 | tf_op jit(solution)/shard_map/ppermute | solution.py:14
  111.2 5.4 %collective-permute-start.28 = (bf16[80,1024]{1,0:T(8,128)(2,1)S(1)}, bf16[80,1024]{1,0:T(8,128)(2,1)S(1)}, u32[]{:S(2)}, u32[]{:S(2)}) collective-permute-start(bf16[80,1024]{1,0:T(8,128)(2,1)S(1)} %get-tuple-element.75), channel_id=1, source_target_pairs={{0,16},{4,20},{8,24},{12,28},{16,0},{20,4},{24,8},{28,12},{1,17},{... | collective-permute-start | bytes 491528 | tf_op jit(solution)/shard_map/ppermute | solution.py:14
  112.8 4.8 %collective-permute-start.29 = (bf16[48,1024]{1,0:T(8,128)(2,1)S(1)}, bf16[48,1024]{1,0:T(8,128)(2,1)S(1)}, u32[]{:S(2)}, u32[]{:S(2)}) collective-permute-start(bf16[48,1024]{1,0:T(8,128)(2,1)S(1)} %get-tuple-element.85), channel_id=1, source_target_pairs={{0,16},{4,20},{8,24},{12,28},{16,0},{20,4},{24,8},{28,12},{1,17},{... | collective-permute-start | bytes 294920 | tf_op jit(solution)/shard_map/ppermute | solution.py:14
  113.8 4.5 %collective-permute-start.30 = (bf16[32,1024]{1,0:T(8,128)(2,1)S(1)}, bf16[32,1024]{1,0:T(8,128)(2,1)S(1)}, u32[]{:S(2)}, u32[]{:S(2)}) collective-permute-start(bf16[32,1024]{1,0:T(8,128)(2,1)S(1)} %get-tuple-element.87), channel_id=1, source_target_pairs={{0,16},{4,20},{8,24},{12,28},{16,0},{20,4},{24,8},{28,12},{1,17},{... | collective-permute-start | bytes 196616 | tf_op jit(solution)/shard_map/ppermute | solution.py:14
  (3 other events, 38.9 us)

commit v3 on v2

--- a/solution.py
+++ b/solution.py
@@ -5,7 +5,7 @@
 
 F32 = jnp.float32
 BF16 = jnp.bfloat16
-ROW_CHUNKS = (8, 6, 5, 3, 2)
+ROW_CHUNKS = (8, 7, 4, 3, 2)
 FORWARD_LOW = 10
 
 

time: 122 us -> 121 us (level)
  starting transfers between devices: 42.5 us -> 40.8 us
    ppermute x31, starting transfers between devices: 42.5 us -> 40.8 us  [swap(): return lax.ppermute(block, axis, [(i, i ^ bit) for i in range(count)])]
where the time goes in v3:
time: 121 us
  waiting for transfers between devices  42.6 us (35%)
  starting transfers between devices  40.8 us (34%)
  matrix products  28.2 us (23%)
  local copies, waits for them, and re-layouts  6.81 us (6%)
  other arithmetic  2.14 us (2%)
    ppermute x31, waiting for transfers between devices, swap(): return lax.ppermute(block, axis, [(i, i ^ bit) for i in range(count)])  42.6 us
    ppermute x31, starting transfers between devices, swap(): return lax.ppermute(block, axis, [(i, i ^ bit) for i in range(count)])  40.8 us
    dot_general x4, matrix products, score(): lax.dot_general(refs, images_of([m]), (((1,), (1,)), ((), ())), preferred...  10.9 us
    dot_general x1, matrix products, body(): refs = jnp.dot(one_hot, references, preferred_element_type=F32).astype(BF16)  9.89 us
    dot_general x5, matrix products, body(): jnp.dot(w, every_image, preferred_element_type=F32) * scale  7.43 us
    gather x1, local copies, waits for them, and re-layouts, body(): jnp.concatenate(done + other, axis=0).at[place]  3.61 us
  transfers between devices with their start and end apart: 31, of which 16 were waited for; matrix products, arithmetic and copies ran while one was open for 26% of the time, Pallas kernels for 0%

profile of v3, /device:TPU:0, one launch (start us, length us, event | category | flops | bytes accessed | tf_op | source)
XLA Modules:
  0.0 121.3 jit_solution(15302352650181506364)
XLA Ops:
  0.0 3.0 %collective-permute-start.1 = (bf16[128,4096]{1,0:T(8,128)(2,1)}, bf16[128,4096]{1,0:T(8,128)(2,1)S(1)}, u32[]{:S(2)}, u32[]{:S(2)}) collective-permute-start(bf16[128,4096]{1,0:T(8,128)(2,1)} %param.4), channel_id=1, source_target_pairs={{0,16},{4,20},{8,24},{12,28},{16,0},{20,4},{24,8},{28,12},{1,17},{... | collective-permute-start | bytes 3145736 | tf_op jit(solution)/shard_map/ppermute | solution.py:14
  5.2 9.9 %multiply_reduce_fusion = (f32[768]{0:T(1024)S(1)}, bf16[768,4096]{1,0:T(8,128)(2,1)}) fusion(bf16[768,4096]{1,0:T(8,128)(2,1)} %param.6, s32[768]{0:T(1024)S(1)} %get-tuple-element.58), kind=kOutput, calls=%fused_computation.2 | convolution fusion | flops 4845009920 | bytes 12589056 | tf_op jit(solution)/shard_map/dot_general | solution.py:54
  15.7 5.0 %fusion.74 = bf16[768,256]{1,0:T(8,128)(2,1)S(1)} fusion(bf16[768,4096]{1,0:T(8,128)(2,1)} %get-tuple-element.94, bf16[128,4096]{1,0:T(8,128)(2,1)} %collective-permute-done, bf16[128,4096]{1,0:T(8,128)(2,1)S(1)} %copy-done.1, f32[256]{0:T(256)S(1)} %get-tuple-element.92, f32[768]{0:T(1024)S(1)} %broadcast_multiply_fusion), kind=kOutput, calls=%fused_computation.48 | convolution fusion | flops 1615593472 | bytes 8785920 | tf_op jit(solution)/shard_map/dot_general | solution.py:68
  20.8 5.6 %collective-permute-done.1 = bf16[128,4096]{1,0:T(8,128)(2,1)S(1)} collective-permute-done((bf16[128,4096]{1,0:T(8,128)(2,1)}, bf16[128,4096]{1,0:T(8,128)(2,1)S(1)}, u32[]{:S(2)}, u32[]{:S(2)}) %collective-permute-start.1) | collective-permute-done | bytes 1048608 | tf_op jit(solution)/shard_map/ppermute | solution.py:14
  26.5 1.8 %collective-permute-start.6 = (bf16[80,4096]{1,0:T(8,128)(2,1)S(1)}, bf16[80,4096]{1,0:T(8,128)(2,1)S(1)}, u32[]{:S(2)}, u32[]{:S(2)}) collective-permute-start(bf16[80,4096]{1,0:T(8,128)(2,1)S(1)} %slice.154), channel_id=1, source_target_pairs={{0,8},{4,12},{8,0},{12,4},{16,24},{20,28},{24,16},{28,20},{1,9},{5... | collective-permute-start | bytes 1966088 | tf_op jit(solution)/shard_map/ppermute | solution.py:14
  29.9 2.0 %fusion.71 = bf16[768,256]{1,0:T(8,128)(2,1)S(1)} fusion(bf16[768,4096]{1,0:T(8,128)(2,1)S(1)} %bitcast.28, bf16[128,4096]{1,0:T(8,128)(2,1)S(1)} %collective-permute-done.2, bf16[128,4096]{1,0:T(8,128)(2,1)S(1)} %collective-permute-done.1, f32[256]{0:T(256)S(1)} %get-tuple-element.91, f32[768]{0:T(1024)S(1)} %broadcast_multiply_fusion), kind=kOutput, calls=%fused_computation.47 | convolution fusion | flops 1615593472 | bytes 8785920 | tf_op jit(solution)/shard_map/dot_general | solution.py:68
  32.1 1.6 %collective-permute-start.7 = (bf16[48,4096]{1,0:T(8,128)(2,1)S(1)}, bf16[48,4096]{1,0:T(8,128)(2,1)S(1)}, u32[]{:S(2)}, u32[]{:S(2)}) collective-permute-start(bf16[48,4096]{1,0:T(8,128)(2,1)S(1)} %slice.156), channel_id=1, source_target_pairs={{0,16},{4,20},{8,24},{12,28},{16,0},{20,4},{24,8},{28,12},{1,17},{... | collective-permute-start | bytes 1179656 | tf_op jit(solution)/shard_map/ppermute | solution.py:14
  33.7 2.0 %fusion.68 = bf16[768,256]{1,0:T(8,128)(2,1)S(1)} fusion(bf16[768,4096]{1,0:T(8,128)(2,1)S(1)} %bitcast.28, bf16[128,4096]{1,0:T(8,128)(2,1)S(1)} %collective-permute-done.4, bf16[128,4096]{1,0:T(8,128)(2,1)S(1)} %collective-permute-done.3, f32[256]{0:T(256)S(1)} %get-tuple-element.90, f32[768]{0:T(1024)S(1)} %broadcast_multiply_fusion), kind=kOutput, calls=%fused_computation.46 | convolution fusion | flops 1615593472 | bytes 8785920 | tf_op jit(solution)/shard_map/dot_general | solution.py:68
  36.3 1.5 %collective-permute-start.11 = (bf16[384,256]{1,0:T(8,128)(2,1)S(1)}, bf16[384,256]{1,0:T(8,128)(2,1)S(1)}, u32[]{:S(2)}, u32[]{:S(2)}) collective-permute-start(bf16[384,256]{1,0:T(8,128)(2,1)S(1)} %slice.209), channel_id=1, source_target_pairs={{0,16},{4,20},{8,24},{12,28},{16,0},{20,4},{24,8},{28,12},{1,17},{... | collective-permute-start | bytes 589832 | tf_op jit(solution)/shard_map/ppermute | solution.py:14
  37.8 6.3 %collective-permute-done.7 = bf16[48,4096]{1,0:T(8,128)(2,1)S(1)} collective-permute-done((bf16[48,4096]{1,0:T(8,128)(2,1)S(1)}, bf16[48,4096]{1,0:T(8,128)(2,1)S(1)}, u32[]{:S(2)}, u32[]{:S(2)}) %collective-permute-start.7) | collective-permute-done | bytes 393248 | tf_op jit(solution)/shard_map/ppermute | solution.py:14
  45.8 1.5 %collective-permute-start.12 = (bf16[128,256]{1,0:T(8,128)(2,1)S(1)}, bf16[128,256]{1,0:T(8,128)(2,1)S(1)}, u32[]{:S(2)}, u32[]{:S(2)}) collective-permute-start(bf16[128,256]{1,0:T(8,128)(2,1)S(1)} %slice.211), channel_id=1, source_target_pairs={{0,16},{4,20},{8,24},{12,28},{16,0},{20,4},{24,8},{28,12},{1,17},{... | collective-permute-start | bytes 196616 | tf_op jit(solution)/shard_map/ppermute | solution.py:14
  47.3 1.8 %fusion.77 = bf16[768,256]{1,0:T(8,128)(2,1)S(1)} fusion(bf16[768,4096]{1,0:T(8,128)(2,1)S(1)} %bitcast.28, bf16[48,4096]{1,0:T(8,128)(2,1)S(1)} %collective-permute-done.9, bf16[80,4096]{1,0:T(8,128)(2,1)S(1)} %collective-permute-done.8, bf16[48,4096]{1,0:T(8,128)(2,1)S(1)} %collective-permute-done.7, bf16[80,4096]{1,0:T(8,128)(2,1)S(1)} %collective-permute-done.6, ...), kind=kOutput, calls=%fused_computation.49 | convolution fusion | flops 1619787776 | bytes 8785920 | tf_op jit(solution)/shard_map/dot_general | solution.py:68
  50.5 1.6 %collective-permute-start.10 = (bf16[128,256]{1,0:T(8,128)(2,1)S(1)}, bf16[128,256]{1,0:T(8,128)(2,1)S(1)}, u32[]{:S(2)}, u32[]{:S(2)}) collective-permute-start(bf16[128,256]{1,0:T(8,128)(2,1)S(1)} %slice.207), channel_id=1, source_target_pairs={{0,16},{4,20},{8,24},{12,28},{16,0},{20,4},{24,8},{28,12},{1,17},{... | collective-permute-start | bytes 196616 | tf_op jit(solution)/shard_map/ppermute | solution.py:14
  52.2 2.6 %collective-permute-done.10 = bf16[128,256]{1,0:T(8,128)(2,1)S(1)} collective-permute-done((bf16[128,256]{1,0:T(8,128)(2,1)S(1)}, bf16[128,256]{1,0:T(8,128)(2,1)S(1)}, u32[]{:S(2)}, u32[]{:S(2)}) %collective-permute-start.10) | collective-permute-done | bytes 65568 | tf_op jit(solution)/shard_map/ppermute | solution.py:14
  56.4 1.6 %collective-permute-start.13 = (bf16[128,2048]{1,0:T(8,128)(2,1)S(1)}, bf16[128,2048]{1,0:T(8,128)(2,1)S(1)}, u32[]{:S(2)}, u32[]{:S(2)}) collective-permute-start(bf16[128,2048]{1,0:T(8,128)(2,1)S(1)} %pad_maximum_fusion), channel_id=1, source_target_pairs={{0,1},{1,0},{2,3},{3,2},{4,5},{5,4},{6,7},{7,6},{8,9},{9,8},{10,11... | collective-permute-start | bytes 1572872 | tf_op jit(solution)/shard_map/ppermute | solution.py:14
  58.0 1.5 %collective-permute-start.15 = (bf16[256,256]{1,0:T(8,128)(2,1)S(1)}, bf16[256,256]{1,0:T(8,128)(2,1)S(1)}, u32[]{:S(2)}, u32[]{:S(2)}) collective-permute-start(bf16[256,256]{1,0:T(8,128)(2,1)S(1)} %slice.213), channel_id=1, source_target_pairs={{0,16},{4,20},{8,24},{12,28},{16,0},{20,4},{24,8},{28,12},{1,17},{... | collective-permute-start | bytes 393224 | tf_op jit(solution)/shard_map/ppermute | solution.py:14
  61.7 2.8 %collective-permute-done.15 = bf16[256,256]{1,0:T(8,128)(2,1)S(1)} collective-permute-done((bf16[256,256]{1,0:T(8,128)(2,1)S(1)}, bf16[256,256]{1,0:T(8,128)(2,1)S(1)}, u32[]{:S(2)}, u32[]{:S(2)}) %collective-permute-start.15) | collective-permute-done | bytes 131104 | tf_op jit(solution)/shard_map/ppermute | solution.py:14
  70.1 2.7 %collective-permute-start.14 = (bf16[128,1024]{1,0:T(8,128)(2,1)S(1)}, bf16[128,1024]{1,0:T(8,128)(2,1)S(1)}, u32[]{:S(2)}, u32[]{:S(2)}) collective-permute-start(bf16[128,1024]{1,0:T(8,128)(2,1)S(1)} %dynamic-slice_convert_fusion), channel_id=1, source_target_pairs={{0,2},{1,3},{2,0},{3,1},{4,6},{5,7},{6,4},{7,5},{8,10},{9,11},{10,... | collective-permute-start | bytes 786440 | tf_op jit(solution)/shard_map/ppermute | solution.py:14
  72.8 1.6 %convolution_multiply_fusion.2 = f32[64,4096]{1,0:T(8,128)S(1)} fusion(bf16[64,1024]{1,0:T(8,128)(2,1)S(1)} %pad_maximum_fusion.6, bf16[1024,4096]{1,0:T(8,128)(2,1)S(1)} %constant_dynamic-update-slice_fusion), kind=kOutput, calls=%fused_computation.6 | convolution fusion | flops 537133056 | bytes 9568256 | tf_op jit(solution)/shard_map/dot_general | solution.py:143
  74.4 1.6 %collective-permute-start.20 = (bf16[64,2048]{1,0:T(8,128)(2,1)S(1)}, bf16[64,2048]{1,0:T(8,128)(2,1)S(1)}, u32[]{:S(2)}, u32[]{:S(2)}) collective-permute-start(bf16[64,2048]{1,0:T(8,128)(2,1)S(1)} %pad_maximum_fusion.3), channel_id=1, source_target_pairs={{0,1},{1,0},{2,3},{3,2},{4,5},{5,4},{6,7},{7,6},{8,9},{9,8},{10,11... | collective-permute-start | bytes 786440 | tf_op jit(solution)/shard_map/ppermute | solution.py:14
  76.1 10.4 %collective-permute-done.18 = bf16[112,2048]{1,0:T(8,128)(2,1)S(1)} collective-permute-done((bf16[112,2048]{1,0:T(8,128)(2,1)S(1)}, bf16[112,2048]{1,0:T(8,128)(2,1)S(1)}, u32[]{:S(2)}, u32[]{:S(2)}) %collective-permute-start.18) | collective-permute-done | bytes 458784 | tf_op jit(solution)/shard_map/ppermute | solution.py:14
  88.1 1.6 %convolution_multiply_fusion.3 = f32[48,4096]{1,0:T(8,128)S(1)} fusion(bf16[48,1024]{1,0:T(8,128)(2,1)S(1)} %pad_maximum_fusion.8, bf16[1024,4096]{1,0:T(8,128)(2,1)S(1)} %constant_dynamic-update-slice_fusion), kind=kOutput, calls=%fused_computation.7 | convolution fusion | flops 402849792 | bytes 9273344 | tf_op jit(solution)/shard_map/dot_general | solution.py:143
  89.7 3.0 %collective-permute-start.22 = (bf16[48,2048]{1,0:T(8,128)(2,1)S(1)}, bf16[48,2048]{1,0:T(8,128)(2,1)S(1)}, u32[]{:S(2)}, u32[]{:S(2)}) collective-permute-start(bf16[48,2048]{1,0:T(8,128)(2,1)S(1)} %pad_maximum_fusion.5), channel_id=1, source_target_pairs={{0,1},{1,0},{2,3},{3,2},{4,5},{5,4},{6,7},{7,6},{8,9},{9,8},{10,11... | collective-permute-start | bytes 589832 | tf_op jit(solution)/shard_map/ppermute | solution.py:14
  92.8 1.5 %convolution_multiply_fusion.4 = f32[32,4096]{1,0:T(8,128)S(1)} fusion(bf16[32,1024]{1,0:T(8,128)(2,1)S(1)} %pad_maximum_fusion.9, bf16[1024,4096]{1,0:T(8,128)(2,1)S(1)} %constant_dynamic-update-slice_fusion), kind=kOutput, calls=%fused_computation.8 | convolution fusion | flops 268566528 | bytes 8978432 | tf_op jit(solution)/shard_map/dot_general | solution.py:143
  94.5 3.7 %collective-permute-done.20 = bf16[64,2048]{1,0:T(8,128)(2,1)S(1)} collective-permute-done((bf16[64,2048]{1,0:T(8,128)(2,1)S(1)}, bf16[64,2048]{1,0:T(8,128)(2,1)S(1)}, u32[]{:S(2)}, u32[]{:S(2)}) %collective-permute-start.20) | collective-permute-done | bytes 262176 | tf_op jit(solution)/shard_map/ppermute | solution.py:14
  99.3 1.6 %collective-permute-start.26 = (bf16[128,1024]{1,0:T(8,128)(2,1)S(1)}, bf16[128,1024]{1,0:T(8,128)(2,1)S(1)}, u32[]{:S(2)}, u32[]{:S(2)}) collective-permute-start(bf16[128,1024]{1,0:T(8,128)(2,1)S(1)} %get-tuple-element.67), channel_id=1, source_target_pairs={{0,16},{4,20},{8,24},{12,28},{16,0},{20,4},{24,8},{28,12},{1,17},{... | collective-permute-start | bytes 786440 | tf_op jit(solution)/shard_map/ppermute | solution.py:14
  101.9 3.6 %collective-permute-start.23 = (bf16[48,1024]{1,0:T(8,128)(2,1)S(1)}, bf16[48,1024]{1,0:T(8,128)(2,1)S(1)}, u32[]{:S(2)}, u32[]{:S(2)}) collective-permute-start(bf16[48,1024]{1,0:T(8,128)(2,1)S(1)} %dynamic-slice_convert_fusion.9), channel_id=1, source_target_pairs={{0,2},{1,3},{2,0},{3,1},{4,6},{5,7},{6,4},{7,5},{8,10},{9,11},{10,... | collective-permute-start | bytes 294920 | tf_op jit(solution)/shard_map/ppermute | solution.py:14
  105.5 2.0 %collective-permute-start.25 = (bf16[32,1024]{1,0:T(8,128)(2,1)S(1)}, bf16[32,1024]{1,0:T(8,128)(2,1)S(1)}, u32[]{:S(2)}, u32[]{:S(2)}) collective-permute-start(bf16[32,1024]{1,0:T(8,128)(2,1)S(1)} %dynamic-slice_convert_fusion.12), channel_id=1, source_target_pairs={{0,2},{1,3},{2,0},{3,1},{4,6},{5,7},{6,4},{7,5},{8,10},{9,11},{10,... | collective-permute-start | bytes 196616 | tf_op jit(solution)/shard_map/ppermute | solution.py:14
  108.9 1.6 %collective-permute-start.28 = (bf16[64,1024]{1,0:T(8,128)(2,1)S(1)}, bf16[64,1024]{1,0:T(8,128)(2,1)S(1)}, u32[]{:S(2)}, u32[]{:S(2)}) collective-permute-start(bf16[64,1024]{1,0:T(8,128)(2,1)S(1)} %get-tuple-element.79), channel_id=1, source_target_pairs={{0,16},{4,20},{8,24},{12,28},{16,0},{20,4},{24,8},{28,12},{1,17},{... | collective-permute-start | bytes 393224 | tf_op jit(solution)/shard_map/ppermute | solution.py:14
  111.7 1.6 %collective-permute-start.29 = (bf16[48,1024]{1,0:T(8,128)(2,1)S(1)}, bf16[48,1024]{1,0:T(8,128)(2,1)S(1)}, u32[]{:S(2)}, u32[]{:S(2)}) collective-permute-start(bf16[48,1024]{1,0:T(8,128)(2,1)S(1)} %get-tuple-element.85), channel_id=1, source_target_pairs={{0,16},{4,20},{8,24},{12,28},{16,0},{20,4},{24,8},{28,12},{1,17},{... | collective-permute-start | bytes 294920 | tf_op jit(solution)/shard_map/ppermute | solution.py:14
  114.1 2.3 %collective-permute-done.29 = bf16[48,1024]{1,0:T(8,128)(2,1)S(1)} collective-permute-done((bf16[48,1024]{1,0:T(8,128)(2,1)S(1)}, bf16[48,1024]{1,0:T(8,128)(2,1)S(1)}, u32[]{:S(2)}, u32[]{:S(2)}) %collective-permute-start.29) | collective-permute-done | bytes 98336 | tf_op jit(solution)/shard_map/ppermute | solution.py:14
  117.7 3.6 %gather_fusion.1 = f32[768,1024]{1,0:T(8,128)} fusion(f32[768,1024]{1,0:T(8,128)S(1)} %convert_dynamic-update-slice_fusion.4, s32[1024]{0:T(1024)S(1)} %pad_clamp_fusion), kind=kCustom, calls=%fused_computation.1 | custom fusion | bytes 6294528 | tf_op jit(solution)/shard_map/gather | solution.py:161
  (136 shorter events, 26.0 us)
Async XLA Ops:
  0.0 15.1 %copy-start = (s32[1024]{0:T(1024)S(1)}, s32[1024]{0:T(1024)}, u32[]{:S(2)}) copy-start(s32[1024]{0:T(1024)} %param.5) | copy-start | bytes 12292
  0.0 26.3 %collective-permute-start.1 = (bf16[128,4096]{1,0:T(8,128)(2,1)}, bf16[128,4096]{1,0:T(8,128)(2,1)S(1)}, u32[]{:S(2)}, u32[]{:S(2)}) collective-permute-start(bf16[128,4096]{1,0:T(8,128)(2,1)} %param.4), channel_id=1, source_target_pairs={{0,16},{4,20},{8,24},{12,28},{16,0},{20,4},{24,8},{28,12},{1,17},{... | collective-permute-start | bytes 3145736 | tf_op jit(solution)/shard_map/ppermute | solution.py:14
  3.0 12.7 %collective-permute-start = (bf16[128,4096]{1,0:T(8,128)(2,1)}, bf16[128,4096]{1,0:T(8,128)(2,1)}, u32[]{:S(2)}, u32[]{:S(2)}) collective-permute-start(bf16[128,4096]{1,0:T(8,128)(2,1)} %param.4), channel_id=1, source_target_pairs={{0,4},{4,0},{8,12},{12,8},{16,20},{20,16},{24,28},{28,24},{1,5},{5... | collective-permute-start | bytes 3145736 | tf_op jit(solution)/shard_map/ppermute | solution.py:14
  3.0 26.6 %collective-permute-start.3 = (bf16[128,4096]{1,0:T(8,128)(2,1)}, bf16[128,4096]{1,0:T(8,128)(2,1)S(1)}, u32[]{:S(2)}, u32[]{:S(2)}) collective-permute-start(bf16[128,4096]{1,0:T(8,128)(2,1)} %param.4), channel_id=1, source_target_pairs={{0,8},{4,12},{8,0},{12,4},{16,24},{20,28},{24,16},{28,20},{1,9},{5... | collective-permute-start | bytes 3145736 | tf_op jit(solution)/shard_map/ppermute | solution.py:14
  26.3 3.3 %collective-permute-start.2 = (bf16[128,4096]{1,0:T(8,128)(2,1)S(1)}, bf16[128,4096]{1,0:T(8,128)(2,1)S(1)}, u32[]{:S(2)}, u32[]{:S(2)}) collective-permute-start(bf16[128,4096]{1,0:T(8,128)(2,1)S(1)} %collective-permute-done.1), channel_id=1, source_target_pairs={{0,4},{4,0},{8,12},{12,8},{16,20},{20,16},{24,28},{28,24},{1,5},{5... | collective-permute-start | bytes 3145736 | tf_op jit(solution)/shard_map/ppermute | solution.py:14
  26.5 17.6 %collective-permute-start.6 = (bf16[80,4096]{1,0:T(8,128)(2,1)S(1)}, bf16[80,4096]{1,0:T(8,128)(2,1)S(1)}, u32[]{:S(2)}, u32[]{:S(2)}) collective-permute-start(bf16[80,4096]{1,0:T(8,128)(2,1)S(1)} %slice.154), channel_id=1, source_target_pairs={{0,8},{4,12},{8,0},{12,4},{16,24},{20,28},{24,16},{28,20},{1,9},{5... | collective-permute-start | bytes 1966088 | tf_op jit(solution)/shard_map/ppermute | solution.py:14
  29.6 4.1 %collective-permute-start.4 = (bf16[128,4096]{1,0:T(8,128)(2,1)S(1)}, bf16[128,4096]{1,0:T(8,128)(2,1)S(1)}, u32[]{:S(2)}, u32[]{:S(2)}) collective-permute-start(bf16[128,4096]{1,0:T(8,128)(2,1)S(1)} %collective-permute-done.3), channel_id=1, source_target_pairs={{0,4},{4,0},{8,12},{12,8},{16,20},{20,16},{24,28},{28,24},{1,5},{5... | collective-permute-start | bytes 3145736 | tf_op jit(solution)/shard_map/ppermute | solution.py:14
  32.1 12.0 %collective-permute-start.7 = (bf16[48,4096]{1,0:T(8,128)(2,1)S(1)}, bf16[48,4096]{1,0:T(8,128)(2,1)S(1)}, u32[]{:S(2)}, u32[]{:S(2)}) collective-permute-start(bf16[48,4096]{1,0:T(8,128)(2,1)S(1)} %slice.156), channel_id=1, source_target_pairs={{0,16},{4,20},{8,24},{12,28},{16,0},{20,4},{24,8},{28,12},{1,17},{... | collective-permute-start | bytes 1179656 | tf_op jit(solution)/shard_map/ppermute | solution.py:14
  35.7 14.8 %collective-permute-start.5 = (bf16[128,256]{1,0:T(8,128)(2,1)S(1)}, bf16[128,256]{1,0:T(8,128)(2,1)S(1)}, u32[]{:S(2)}, u32[]{:S(2)}) collective-permute-start(bf16[128,256]{1,0:T(8,128)(2,1)S(1)} %slice.205), channel_id=1, source_target_pairs={{0,16},{4,20},{8,24},{12,28},{16,0},{20,4},{24,8},{28,12},{1,17},{... | collective-permute-start | bytes 196616 | tf_op jit(solution)/shard_map/ppermute | solution.py:14
  36.3 13.3 %collective-permute-start.11 = (bf16[384,256]{1,0:T(8,128)(2,1)S(1)}, bf16[384,256]{1,0:T(8,128)(2,1)S(1)}, u32[]{:S(2)}, u32[]{:S(2)}) collective-permute-start(bf16[384,256]{1,0:T(8,128)(2,1)S(1)} %slice.209), channel_id=1, source_target_pairs={{0,16},{4,20},{8,24},{12,28},{16,0},{20,4},{24,8},{28,12},{1,17},{... | collective-permute-start | bytes 589832 | tf_op jit(solution)/shard_map/ppermute | solution.py:14
  44.1 1.7 %collective-permute-start.9 = (bf16[48,4096]{1,0:T(8,128)(2,1)S(1)}, bf16[48,4096]{1,0:T(8,128)(2,1)S(1)}, u32[]{:S(2)}, u32[]{:S(2)}) collective-permute-start(bf16[48,4096]{1,0:T(8,128)(2,1)S(1)} %collective-permute-done.7), channel_id=1, source_target_pairs={{0,4},{4,0},{8,12},{12,8},{16,20},{20,16},{24,28},{28,24},{1,5},{5... | collective-permute-start | bytes 1179656 | tf_op jit(solution)/shard_map/ppermute | solution.py:14
  44.1 3.2 %collective-permute-start.8 = (bf16[80,4096]{1,0:T(8,128)(2,1)S(1)}, bf16[80,4096]{1,0:T(8,128)(2,1)S(1)}, u32[]{:S(2)}, u32[]{:S(2)}) collective-permute-start(bf16[80,4096]{1,0:T(8,128)(2,1)S(1)} %collective-permute-done.6), channel_id=1, source_target_pairs={{0,4},{4,0},{8,12},{12,8},{16,20},{20,16},{24,28},{28,24},{1,5},{5... | collective-permute-start | bytes 1966088 | tf_op jit(solution)/shard_map/ppermute | solution.py:14
  45.8 4.7 %collective-permute-start.12 = (bf16[128,256]{1,0:T(8,128)(2,1)S(1)}, bf16[128,256]{1,0:T(8,128)(2,1)S(1)}, u32[]{:S(2)}, u32[]{:S(2)}) collective-permute-start(bf16[128,256]{1,0:T(8,128)(2,1)S(1)} %slice.211), channel_id=1, source_target_pairs={{0,16},{4,20},{8,24},{12,28},{16,0},{20,4},{24,8},{28,12},{1,17},{... | collective-permute-start | bytes 196616 | tf_op jit(solution)/shard_map/ppermute | solution.py:14
  50.5 4.3 %collective-permute-start.10 = (bf16[128,256]{1,0:T(8,128)(2,1)S(1)}, bf16[128,256]{1,0:T(8,128)(2,1)S(1)}, u32[]{:S(2)}, u32[]{:S(2)}) collective-permute-start(bf16[128,256]{1,0:T(8,128)(2,1)S(1)} %slice.207), channel_id=1, source_target_pairs={{0,16},{4,20},{8,24},{12,28},{16,0},{20,4},{24,8},{28,12},{1,17},{... | collective-permute-start | bytes 196616 | tf_op jit(solution)/shard_map/ppermute | solution.py:14
  56.4 13.5 %collective-permute-start.13 = (bf16[128,2048]{1,0:T(8,128)(2,1)S(1)}, bf16[128,2048]{1,0:T(8,128)(2,1)S(1)}, u32[]{:S(2)}, u32[]{:S(2)}) collective-permute-start(bf16[128,2048]{1,0:T(8,128)(2,1)S(1)} %pad_maximum_fusion), channel_id=1, source_target_pairs={{0,1},{1,0},{2,3},{3,2},{4,5},{5,4},{6,7},{7,6},{8,9},{9,8},{10,11... | collective-permute-start | bytes 1572872 | tf_op jit(solution)/shard_map/ppermute | solution.py:14
  58.0 6.4 %collective-permute-start.15 = (bf16[256,256]{1,0:T(8,128)(2,1)S(1)}, bf16[256,256]{1,0:T(8,128)(2,1)S(1)}, u32[]{:S(2)}, u32[]{:S(2)}) collective-permute-start(bf16[256,256]{1,0:T(8,128)(2,1)S(1)} %slice.213), channel_id=1, source_target_pairs={{0,16},{4,20},{8,24},{12,28},{16,0},{20,4},{24,8},{28,12},{1,17},{... | collective-permute-start | bytes 393224 | tf_op jit(solution)/shard_map/ppermute | solution.py:14
  59.6 6.3 %collective-permute-start.16 = (bf16[256,256]{1,0:T(8,128)(2,1)S(1)}, bf16[256,256]{1,0:T(8,128)(2,1)S(1)}, u32[]{:S(2)}, u32[]{:S(2)}) collective-permute-start(bf16[256,256]{1,0:T(8,128)(2,1)S(1)} %slice.216), channel_id=1, source_target_pairs={{0,16},{4,20},{8,24},{12,28},{16,0},{20,4},{24,8},{28,12},{1,17},{... | collective-permute-start | bytes 393224 | tf_op jit(solution)/shard_map/ppermute | solution.py:14
  60.1 7.2 %collective-permute-start.17 = (bf16[256,256]{1,0:T(8,128)(2,1)S(1)}, bf16[256,256]{1,0:T(8,128)(2,1)S(1)}, u32[]{:S(2)}, u32[]{:S(2)}) collective-permute-start(bf16[256,256]{1,0:T(8,128)(2,1)S(1)} %slice.220), channel_id=1, source_target_pairs={{0,16},{4,20},{8,24},{12,28},{16,0},{20,4},{24,8},{28,12},{1,17},{... | collective-permute-start | bytes 393224 | tf_op jit(solution)/shard_map/ppermute | solution.py:14
  68.9 17.7 %collective-permute-start.18 = (bf16[112,2048]{1,0:T(8,128)(2,1)S(1)}, bf16[112,2048]{1,0:T(8,128)(2,1)S(1)}, u32[]{:S(2)}, u32[]{:S(2)}) collective-permute-start(bf16[112,2048]{1,0:T(8,128)(2,1)S(1)} %pad_maximum_fusion.1), channel_id=1, source_target_pairs={{0,1},{1,0},{2,3},{3,2},{4,5},{5,4},{6,7},{7,6},{8,9},{9,8},{10,11... | collective-permute-start | bytes 1376264 | tf_op jit(solution)/shard_map/ppermute | solution.py:14
  70.1 24.4 %collective-permute-start.14 = (bf16[128,1024]{1,0:T(8,128)(2,1)S(1)}, bf16[128,1024]{1,0:T(8,128)(2,1)S(1)}, u32[]{:S(2)}, u32[]{:S(2)}) collective-permute-start(bf16[128,1024]{1,0:T(8,128)(2,1)S(1)} %dynamic-slice_convert_fusion), channel_id=1, source_target_pairs={{0,2},{1,3},{2,0},{3,1},{4,6},{5,7},{6,4},{7,5},{8,10},{9,11},{10,... | collective-permute-start | bytes 786440 | tf_op jit(solution)/shard_map/ppermute | solution.py:14
  74.4 23.8 %collective-permute-start.20 = (bf16[64,2048]{1,0:T(8,128)(2,1)S(1)}, bf16[64,2048]{1,0:T(8,128)(2,1)S(1)}, u32[]{:S(2)}, u32[]{:S(2)}) collective-permute-start(bf16[64,2048]{1,0:T(8,128)(2,1)S(1)} %pad_maximum_fusion.3), channel_id=1, source_target_pairs={{0,1},{1,0},{2,3},{3,2},{4,5},{5,4},{6,7},{7,6},{8,9},{9,8},{10,11... | collective-permute-start | bytes 786440 | tf_op jit(solution)/shard_map/ppermute | solution.py:14
  86.7 14.2 %collective-permute-start.19 = (bf16[112,1024]{1,0:T(8,128)(2,1)S(1)}, bf16[112,1024]{1,0:T(8,128)(2,1)S(1)}, u32[]{:S(2)}, u32[]{:S(2)}) collective-permute-start(bf16[112,1024]{1,0:T(8,128)(2,1)S(1)} %dynamic-slice_convert_fusion.3), channel_id=1, source_target_pairs={{0,2},{1,3},{2,0},{3,1},{4,6},{5,7},{6,4},{7,5},{8,10},{9,11},{10,... | collective-permute-start | bytes 688136 | tf_op jit(solution)/shard_map/ppermute | solution.py:14
  89.7 12.1 %collective-permute-start.22 = (bf16[48,2048]{1,0:T(8,128)(2,1)S(1)}, bf16[48,2048]{1,0:T(8,128)(2,1)S(1)}, u32[]{:S(2)}, u32[]{:S(2)}) collective-permute-start(bf16[48,2048]{1,0:T(8,128)(2,1)S(1)} %pad_maximum_fusion.5), channel_id=1, source_target_pairs={{0,1},{1,0},{2,3},{3,2},{4,5},{5,4},{6,7},{7,6},{8,9},{9,8},{10,11... | collective-permute-start | bytes 589832 | tf_op jit(solution)/shard_map/ppermute | solution.py:14
  94.4 11.1 %collective-permute-start.24 = (bf16[32,2048]{1,0:T(8,128)(2,1)S(1)}, bf16[32,2048]{1,0:T(8,128)(2,1)S(1)}, u32[]{:S(2)}, u32[]{:S(2)}) collective-permute-start(bf16[32,2048]{1,0:T(8,128)(2,1)S(1)} %pad_maximum_fusion.7), channel_id=1, source_target_pairs={{0,1},{1,0},{2,3},{3,2},{4,5},{5,4},{6,7},{7,6},{8,9},{9,8},{10,11... | collective-permute-start | bytes 393224 | tf_op jit(solution)/shard_map/ppermute | solution.py:14
  98.3 10.5 %collective-permute-start.21 = (bf16[64,1024]{1,0:T(8,128)(2,1)S(1)}, bf16[64,1024]{1,0:T(8,128)(2,1)S(1)}, u32[]{:S(2)}, u32[]{:S(2)}) collective-permute-start(bf16[64,1024]{1,0:T(8,128)(2,1)S(1)} %dynamic-slice_convert_fusion.6), channel_id=1, source_target_pairs={{0,2},{1,3},{2,0},{3,1},{4,6},{5,7},{6,4},{7,5},{8,10},{9,11},{10,... | collective-permute-start | bytes 393224 | tf_op jit(solution)/shard_map/ppermute | solution.py:14
  99.3 14.7 %collective-permute-start.26 = (bf16[128,1024]{1,0:T(8,128)(2,1)S(1)}, bf16[128,1024]{1,0:T(8,128)(2,1)S(1)}, u32[]{:S(2)}, u32[]{:S(2)}) collective-permute-start(bf16[128,1024]{1,0:T(8,128)(2,1)S(1)} %get-tuple-element.67), channel_id=1, source_target_pairs={{0,16},{4,20},{8,24},{12,28},{16,0},{20,4},{24,8},{28,12},{1,17},{... | collective-permute-start | bytes 786440 | tf_op jit(solution)/shard_map/ppermute | solution.py:14
  100.9 13.1 %collective-permute-start.27 = (bf16[112,1024]{1,0:T(8,128)(2,1)S(1)}, bf16[112,1024]{1,0:T(8,128)(2,1)S(1)}, u32[]{:S(2)}, u32[]{:S(2)}) collective-permute-start(bf16[112,1024]{1,0:T(8,128)(2,1)S(1)} %get-tuple-element.69), channel_id=1, source_target_pairs={{0,16},{4,20},{8,24},{12,28},{16,0},{20,4},{24,8},{28,12},{1,17},{... | collective-permute-start | bytes 688136 | tf_op jit(solution)/shard_map/ppermute | solution.py:14
  101.9 9.8 %collective-permute-start.23 = (bf16[48,1024]{1,0:T(8,128)(2,1)S(1)}, bf16[48,1024]{1,0:T(8,128)(2,1)S(1)}, u32[]{:S(2)}, u32[]{:S(2)}) collective-permute-start(bf16[48,1024]{1,0:T(8,128)(2,1)S(1)} %dynamic-slice_convert_fusion.9), channel_id=1, source_target_pairs={{0,2},{1,3},{2,0},{3,1},{4,6},{5,7},{6,4},{7,5},{8,10},{9,11},{10,... | collective-permute-start | bytes 294920 | tf_op jit(solution)/shard_map/ppermute | solution.py:14
  105.5 7.8 %collective-permute-start.25 = (bf16[32,1024]{1,0:T(8,128)(2,1)S(1)}, bf16[32,1024]{1,0:T(8,128)(2,1)S(1)}, u32[]{:S(2)}, u32[]{:S(2)}) collective-permute-start(bf16[32,1024]{1,0:T(8,128)(2,1)S(1)} %dynamic-slice_convert_fusion.12), channel_id=1, source_target_pairs={{0,2},{1,3},{2,0},{3,1},{4,6},{5,7},{6,4},{7,5},{8,10},{9,11},{10,... | collective-permute-start | bytes 196616 | tf_op jit(solution)/shard_map/ppermute | solution.py:14
  108.9 5.2 %collective-permute-start.28 = (bf16[64,1024]{1,0:T(8,128)(2,1)S(1)}, bf16[64,1024]{1,0:T(8,128)(2,1)S(1)}, u32[]{:S(2)}, u32[]{:S(2)}) collective-permute-start(bf16[64,1024]{1,0:T(8,128)(2,1)S(1)} %get-tuple-element.79), channel_id=1, source_target_pairs={{0,16},{4,20},{8,24},{12,28},{16,0},{20,4},{24,8},{28,12},{1,17},{... | collective-permute-start | bytes 393224 | tf_op jit(solution)/shard_map/ppermute | solution.py:14
  111.7 4.7 %collective-permute-start.29 = (bf16[48,1024]{1,0:T(8,128)(2,1)S(1)}, bf16[48,1024]{1,0:T(8,128)(2,1)S(1)}, u32[]{:S(2)}, u32[]{:S(2)}) collective-permute-start(bf16[48,1024]{1,0:T(8,128)(2,1)S(1)} %get-tuple-element.85), channel_id=1, source_target_pairs={{0,16},{4,20},{8,24},{12,28},{16,0},{20,4},{24,8},{28,12},{1,17},{... | collective-permute-start | bytes 294920 | tf_op jit(solution)/shard_map/ppermute | solution.py:14
  113.3 4.3 %collective-permute-start.30 = (bf16[32,1024]{1,0:T(8,128)(2,1)S(1)}, bf16[32,1024]{1,0:T(8,128)(2,1)S(1)}, u32[]{:S(2)}, u32[]{:S(2)}) collective-permute-start(bf16[32,1024]{1,0:T(8,128)(2,1)S(1)} %get-tuple-element.87), channel_id=1, source_target_pairs={{0,16},{4,20},{8,24},{12,28},{16,0},{20,4},{24,8},{28,12},{1,17},{... | collective-permute-start | bytes 196616 | tf_op jit(solution)/shard_map/ppermute | solution.py:14
  (3 other events, 38.9 us)

commit v4 on v3

--- a/solution.py
+++ b/solution.py
@@ -5,7 +5,7 @@
 
 F32 = jnp.float32
 BF16 = jnp.bfloat16
-ROW_CHUNKS = (8, 7, 4, 3, 2)
+ROW_CHUNKS = (9, 7, 4, 2, 2)
 FORWARD_LOW = 10
 
 

time: 121 us -> 124 us (1.025)
  waiting for transfers between devices: 42.6 us -> 47.6 us
  starting transfers between devices: 40.8 us -> 38.7 us
    ppermute x31, waiting for transfers between devices: 42.6 us -> 47.6 us  [swap(): return lax.ppermute(block, axis, [(i, i ^ bit) for i in range(count)])]
    ppermute x31, starting transfers between devices: 40.8 us -> 38.7 us  [swap(): return lax.ppermute(block, axis, [(i, i ^ bit) for i in range(count)])]
  transfers between devices with their start and end apart: 31 -> 31, of which waited for: 16 -> 15; matrix products, arithmetic and copies ran while one was open for 26% -> 26% of each run, Pallas kernels for 0% -> 0%
where the time goes in v4:
time: 124 us
  waiting for transfers between devices  47.6 us (38%)
  starting transfers between devices  38.7 us (31%)
  matrix products  28.3 us (23%)
  local copies, waits for them, and re-layouts  6.78 us (5%)
  other arithmetic  1.93 us (2%)
    ppermute x31, waiting for transfers between devices, swap(): return lax.ppermute(block, axis, [(i, i ^ bit) for i in range(count)])  47.6 us
    ppermute x31, starting transfers between devices, swap(): return lax.ppermute(block, axis, [(i, i ^ bit) for i in range(count)])  38.7 us
    dot_general x4, matrix products, score(): lax.dot_general(refs, images_of([m]), (((1,), (1,)), ((), ())), preferred...  10.9 us
    dot_general x1, matrix products, body(): refs = jnp.dot(one_hot, references, preferred_element_type=F32).astype(BF16)  9.89 us
    dot_general x5, matrix products, body(): jnp.dot(w, every_image, preferred_element_type=F32) * scale  7.53 us
    gather x1, local copies, waits for them, and re-layouts, body(): jnp.concatenate(done + other, axis=0).at[place]  3.61 us
  transfers between devices with their start and end apart: 31, of which 15 were waited for; matrix products, arithmetic and copies ran while one was open for 26% of the time, Pallas kernels for 0%

profile of v4, /device:TPU:0, one launch (start us, length us, event | category | flops | bytes accessed | tf_op | source)
XLA Modules:
  0.0 124.0 jit_solution(14035734150347222149)
XLA Ops:
  0.0 3.0 %collective-permute-start.1 = (bf16[128,4096]{1,0:T(8,128)(2,1)}, bf16[128,4096]{1,0:T(8,128)(2,1)S(1)}, u32[]{:S(2)}, u32[]{:S(2)}) collective-permute-start(bf16[128,4096]{1,0:T(8,128)(2,1)} %param.4), channel_id=1, source_target_pairs={{0,16},{4,20},{8,24},{12,28},{16,0},{20,4},{24,8},{28,12},{1,17},{... | collective-permute-start | bytes 3145736 | tf_op jit(solution)/shard_map/ppermute | solution.py:14
  5.2 9.9 %multiply_reduce_fusion = (f32[768]{0:T(1024)S(1)}, bf16[768,4096]{1,0:T(8,128)(2,1)}) fusion(bf16[768,4096]{1,0:T(8,128)(2,1)} %param.6, s32[768]{0:T(1024)S(1)} %get-tuple-element.58), kind=kOutput, calls=%fused_computation.2 | convolution fusion | flops 4845009920 | bytes 12589056 | tf_op jit(solution)/shard_map/dot_general | solution.py:54
  15.7 5.0 %fusion.74 = bf16[768,256]{1,0:T(8,128)(2,1)S(1)} fusion(bf16[768,4096]{1,0:T(8,128)(2,1)} %get-tuple-element.102, bf16[128,4096]{1,0:T(8,128)(2,1)} %collective-permute-done, bf16[128,4096]{1,0:T(8,128)(2,1)S(1)} %copy-done.1, f32[256]{0:T(256)S(1)} %get-tuple-element.100, f32[768]{0:T(1024)S(1)} %broadcast_multiply_fusion), kind=kOutput, calls=%fused_computation.48 | convolution fusion | flops 1615593472 | bytes 8785920 | tf_op jit(solution)/shard_map/dot_general | solution.py:68
  20.8 5.6 %collective-permute-done.1 = bf16[128,4096]{1,0:T(8,128)(2,1)S(1)} collective-permute-done((bf16[128,4096]{1,0:T(8,128)(2,1)}, bf16[128,4096]{1,0:T(8,128)(2,1)S(1)}, u32[]{:S(2)}, u32[]{:S(2)}) %collective-permute-start.1) | collective-permute-done | bytes 1048608 | tf_op jit(solution)/shard_map/ppermute | solution.py:14
  26.5 1.8 %collective-permute-start.6 = (bf16[80,4096]{1,0:T(8,128)(2,1)S(1)}, bf16[80,4096]{1,0:T(8,128)(2,1)S(1)}, u32[]{:S(2)}, u32[]{:S(2)}) collective-permute-start(bf16[80,4096]{1,0:T(8,128)(2,1)S(1)} %slice.154), channel_id=1, source_target_pairs={{0,8},{4,12},{8,0},{12,4},{16,24},{20,28},{24,16},{28,20},{1,9},{5... | collective-permute-start | bytes 1966088 | tf_op jit(solution)/shard_map/ppermute | solution.py:14
  29.9 2.0 %fusion.71 = bf16[768,256]{1,0:T(8,128)(2,1)S(1)} fusion(bf16[768,4096]{1,0:T(8,128)(2,1)S(1)} %bitcast.28, bf16[128,4096]{1,0:T(8,128)(2,1)S(1)} %collective-permute-done.2, bf16[128,4096]{1,0:T(8,128)(2,1)S(1)} %collective-permute-done.1, f32[256]{0:T(256)S(1)} %get-tuple-element.99, f32[768]{0:T(1024)S(1)} %broadcast_multiply_fusion), kind=kOutput, calls=%fused_computation.47 | convolution fusion | flops 1615593472 | bytes 8785920 | tf_op jit(solution)/shard_map/dot_general | solution.py:68
  32.1 1.6 %collective-permute-start.7 = (bf16[48,4096]{1,0:T(8,128)(2,1)S(1)}, bf16[48,4096]{1,0:T(8,128)(2,1)S(1)}, u32[]{:S(2)}, u32[]{:S(2)}) collective-permute-start(bf16[48,4096]{1,0:T(8,128)(2,1)S(1)} %slice.156), channel_id=1, source_target_pairs={{0,16},{4,20},{8,24},{12,28},{16,0},{20,4},{24,8},{28,12},{1,17},{... | collective-permute-start | bytes 1179656 | tf_op jit(solution)/shard_map/ppermute | solution.py:14
  33.7 2.0 %fusion.68 = bf16[768,256]{1,0:T(8,128)(2,1)S(1)} fusion(bf16[768,4096]{1,0:T(8,128)(2,1)S(1)} %bitcast.28, bf16[128,4096]{1,0:T(8,128)(2,1)S(1)} %collective-permute-done.4, bf16[128,4096]{1,0:T(8,128)(2,1)S(1)} %collective-permute-done.3, f32[256]{0:T(256)S(1)} %get-tuple-element.98, f32[768]{0:T(1024)S(1)} %broadcast_multiply_fusion), kind=kOutput, calls=%fused_computation.46 | convolution fusion | flops 1615593472 | bytes 8785920 | tf_op jit(solution)/shard_map/dot_general | solution.py:68
  36.3 1.5 %collective-permute-start.11 = (bf16[384,256]{1,0:T(8,128)(2,1)S(1)}, bf16[384,256]{1,0:T(8,128)(2,1)S(1)}, u32[]{:S(2)}, u32[]{:S(2)}) collective-permute-start(bf16[384,256]{1,0:T(8,128)(2,1)S(1)} %slice.209), channel_id=1, source_target_pairs={{0,16},{4,20},{8,24},{12,28},{16,0},{20,4},{24,8},{28,12},{1,17},{... | collective-permute-start | bytes 589832 | tf_op jit(solution)/shard_map/ppermute | solution.py:14
  37.8 6.3 %collective-permute-done.7 = bf16[48,4096]{1,0:T(8,128)(2,1)S(1)} collective-permute-done((bf16[48,4096]{1,0:T(8,128)(2,1)S(1)}, bf16[48,4096]{1,0:T(8,128)(2,1)S(1)}, u32[]{:S(2)}, u32[]{:S(2)}) %collective-permute-start.7) | collective-permute-done | bytes 393248 | tf_op jit(solution)/shard_map/ppermute | solution.py:14
  45.8 1.5 %collective-permute-start.12 = (bf16[144,256]{1,0:T(8,128)(2,1)S(1)}, bf16[144,256]{1,0:T(8,128)(2,1)S(1)}, u32[]{:S(2)}, u32[]{:S(2)}) collective-permute-start(bf16[144,256]{1,0:T(8,128)(2,1)S(1)} %slice.211), channel_id=1, source_target_pairs={{0,16},{4,20},{8,24},{12,28},{16,0},{20,4},{24,8},{28,12},{1,17},{... | collective-permute-start | bytes 221192 | tf_op jit(solution)/shard_map/ppermute | solution.py:14
  47.3 1.8 %fusion.77 = bf16[768,256]{1,0:T(8,128)(2,1)S(1)} fusion(bf16[768,4096]{1,0:T(8,128)(2,1)S(1)} %bitcast.28, bf16[48,4096]{1,0:T(8,128)(2,1)S(1)} %collective-permute-done.9, bf16[80,4096]{1,0:T(8,128)(2,1)S(1)} %collective-permute-done.8, bf16[48,4096]{1,0:T(8,128)(2,1)S(1)} %collective-permute-done.7, bf16[80,4096]{1,0:T(8,128)(2,1)S(1)} %collective-permute-done.6, ...), kind=kOutput, calls=%fused_computation.49 | convolution fusion | flops 1619787776 | bytes 8785920 | tf_op jit(solution)/shard_map/dot_general | solution.py:68
  50.9 1.6 %collective-permute-start.10 = (bf16[144,256]{1,0:T(8,128)(2,1)S(1)}, bf16[144,256]{1,0:T(8,128)(2,1)S(1)}, u32[]{:S(2)}, u32[]{:S(2)}) collective-permute-start(bf16[144,256]{1,0:T(8,128)(2,1)S(1)} %slice.207), channel_id=1, source_target_pairs={{0,16},{4,20},{8,24},{12,28},{16,0},{20,4},{24,8},{28,12},{1,17},{... | collective-permute-start | bytes 221192 | tf_op jit(solution)/shard_map/ppermute | solution.py:14
  52.6 2.7 %collective-permute-done.10 = bf16[144,256]{1,0:T(8,128)(2,1)S(1)} collective-permute-done((bf16[144,256]{1,0:T(8,128)(2,1)S(1)}, bf16[144,256]{1,0:T(8,128)(2,1)S(1)}, u32[]{:S(2)}, u32[]{:S(2)}) %collective-permute-start.10) | collective-permute-done | bytes 73760 | tf_op jit(solution)/shard_map/ppermute | solution.py:14
  57.0 1.6 %collective-permute-start.13 = (bf16[144,2048]{1,0:T(8,128)(2,1)S(1)}, bf16[144,2048]{1,0:T(8,128)(2,1)S(1)}, u32[]{:S(2)}, u32[]{:S(2)}) collective-permute-start(bf16[144,2048]{1,0:T(8,128)(2,1)S(1)} %pad_maximum_fusion), channel_id=1, source_target_pairs={{0,1},{1,0},{2,3},{3,2},{4,5},{5,4},{6,7},{7,6},{8,9},{9,8},{10,11... | collective-permute-start | bytes 1769480 | tf_op jit(solution)/shard_map/ppermute | solution.py:14
  62.3 2.2 %collective-permute-done.15 = bf16[240,256]{1,0:T(8,128)(2,1)S(1)} collective-permute-done((bf16[240,256]{1,0:T(8,128)(2,1)S(1)}, bf16[240,256]{1,0:T(8,128)(2,1)S(1)}, u32[]{:S(2)}, u32[]{:S(2)}) %collective-permute-start.15) | collective-permute-done | bytes 122912 | tf_op jit(solution)/shard_map/ppermute | solution.py:14
  69.6 6.2 %collective-permute-done.13 = bf16[144,2048]{1,0:T(8,128)(2,1)S(1)} collective-permute-done((bf16[144,2048]{1,0:T(8,128)(2,1)S(1)}, bf16[144,2048]{1,0:T(8,128)(2,1)S(1)}, u32[]{:S(2)}, u32[]{:S(2)}) %collective-permute-start.13) | collective-permute-done | bytes 589856 | tf_op jit(solution)/shard_map/ppermute | solution.py:14
  76.0 2.5 %collective-permute-start.14 = (bf16[144,1024]{1,0:T(8,128)(2,1)S(1)}, bf16[144,1024]{1,0:T(8,128)(2,1)S(1)}, u32[]{:S(2)}, u32[]{:S(2)}) collective-permute-start(bf16[144,1024]{1,0:T(8,128)(2,1)S(1)} %dynamic-slice_convert_fusion), channel_id=1, source_target_pairs={{0,2},{1,3},{2,0},{3,1},{4,6},{5,7},{6,4},{7,5},{8,10},{9,11},{10,... | collective-permute-start | bytes 884744 | tf_op jit(solution)/shard_map/ppermute | solution.py:14
  78.4 7.3 %collective-permute-done.18 = bf16[112,2048]{1,0:T(8,128)(2,1)S(1)} collective-permute-done((bf16[112,2048]{1,0:T(8,128)(2,1)S(1)}, bf16[112,2048]{1,0:T(8,128)(2,1)S(1)}, u32[]{:S(2)}, u32[]{:S(2)}) %collective-permute-start.18) | collective-permute-done | bytes 458784 | tf_op jit(solution)/shard_map/ppermute | solution.py:14
  86.4 1.6 %convolution_multiply_fusion.2 = f32[64,4096]{1,0:T(8,128)S(1)} fusion(bf16[64,1024]{1,0:T(8,128)(2,1)S(1)} %pad_maximum_fusion.5, bf16[1024,4096]{1,0:T(8,128)(2,1)S(1)} %constant_dynamic-update-slice_fusion), kind=kOutput, calls=%fused_computation.6 | convolution fusion | flops 537133056 | bytes 9568256 | tf_op jit(solution)/shard_map/dot_general | solution.py:143
  88.1 2.5 %collective-permute-start.20 = (bf16[64,2048]{1,0:T(8,128)(2,1)S(1)}, bf16[64,2048]{1,0:T(8,128)(2,1)S(1)}, u32[]{:S(2)}, u32[]{:S(2)}) collective-permute-start(bf16[64,2048]{1,0:T(8,128)(2,1)S(1)} %pad_maximum_fusion.3), channel_id=1, source_target_pairs={{0,1},{1,0},{2,3},{3,2},{4,5},{5,4},{6,7},{7,6},{8,9},{9,8},{10,11... | collective-permute-start | bytes 786440 | tf_op jit(solution)/shard_map/ppermute | solution.py:14
  90.6 1.5 %convolution_multiply_fusion.4 = f32[32,4096]{1,0:T(8,128)S(1)} fusion(bf16[32,1024]{1,0:T(8,128)(2,1)S(1)} %pad_maximum_fusion.8, bf16[1024,4096]{1,0:T(8,128)(2,1)S(1)} %constant_dynamic-update-slice_fusion), kind=kOutput, calls=%fused_computation.8 | convolution fusion | flops 268566528 | bytes 8978432 | tf_op jit(solution)/shard_map/dot_general | solution.py:143
  92.4 1.5 %convolution_multiply_fusion.3 = f32[32,4096]{1,0:T(8,128)S(1)} fusion(bf16[32,1024]{1,0:T(8,128)(2,1)S(1)} %pad_maximum_fusion.9, bf16[1024,4096]{1,0:T(8,128)(2,1)S(1)} %constant_dynamic-update-slice_fusion), kind=kOutput, calls=%fused_computation.7 | convolution fusion | flops 268566528 | bytes 8978432 | tf_op jit(solution)/shard_map/dot_general | solution.py:143
  93.9 2.1 %collective-permute-start.24 = (bf16[32,2048]{1,0:T(8,128)(2,1)S(1)}, bf16[32,2048]{1,0:T(8,128)(2,1)S(1)}, u32[]{:S(2)}, u32[]{:S(2)}) collective-permute-start(bf16[32,2048]{1,0:T(8,128)(2,1)S(1)} %pad_maximum_fusion.7), channel_id=1, source_target_pairs={{0,1},{1,0},{2,3},{3,2},{4,5},{5,4},{6,7},{7,6},{8,9},{9,8},{10,11... | collective-permute-start | bytes 393224 | tf_op jit(solution)/shard_map/ppermute | solution.py:14
  96.1 7.7 %collective-permute-done.20 = bf16[64,2048]{1,0:T(8,128)(2,1)S(1)} collective-permute-done((bf16[64,2048]{1,0:T(8,128)(2,1)S(1)}, bf16[64,2048]{1,0:T(8,128)(2,1)S(1)}, u32[]{:S(2)}, u32[]{:S(2)}) %collective-permute-start.20) | collective-permute-done | bytes 262176 | tf_op jit(solution)/shard_map/ppermute | solution.py:14
  105.3 1.6 %collective-permute-start.26 = (bf16[144,1024]{1,0:T(8,128)(2,1)S(1)}, bf16[144,1024]{1,0:T(8,128)(2,1)S(1)}, u32[]{:S(2)}, u32[]{:S(2)}) collective-permute-start(bf16[144,1024]{1,0:T(8,128)(2,1)S(1)} %get-tuple-element.67), channel_id=1, source_target_pairs={{0,16},{4,20},{8,24},{12,28},{16,0},{20,4},{24,8},{28,12},{1,17},{... | collective-permute-start | bytes 884744 | tf_op jit(solution)/shard_map/ppermute | solution.py:14
  107.6 1.8 %collective-permute-start.23 = (bf16[32,1024]{1,0:T(8,128)(2,1)S(1)}, bf16[32,1024]{1,0:T(8,128)(2,1)S(1)}, u32[]{:S(2)}, u32[]{:S(2)}) collective-permute-start(bf16[32,1024]{1,0:T(8,128)(2,1)S(1)} %dynamic-slice_convert_fusion.12), channel_id=1, source_target_pairs={{0,2},{1,3},{2,0},{3,1},{4,6},{5,7},{6,4},{7,5},{8,10},{9,11},{10,... | collective-permute-start | bytes 196616 | tf_op jit(solution)/shard_map/ppermute | solution.py:14
  111.3 1.8 %collective-permute-start.28 = (bf16[64,1024]{1,0:T(8,128)(2,1)S(1)}, bf16[64,1024]{1,0:T(8,128)(2,1)S(1)}, u32[]{:S(2)}, u32[]{:S(2)}) collective-permute-start(bf16[64,1024]{1,0:T(8,128)(2,1)S(1)} %get-tuple-element.75), channel_id=1, source_target_pairs={{0,16},{4,20},{8,24},{12,28},{16,0},{20,4},{24,8},{28,12},{1,17},{... | collective-permute-start | bytes 393224 | tf_op jit(solution)/shard_map/ppermute | solution.py:14
  114.5 1.6 %collective-permute-done.25 = bf16[32,1024]{1,0:T(8,128)(2,1)S(1)} collective-permute-done((bf16[32,1024]{1,0:T(8,128)(2,1)S(1)}, bf16[32,1024]{1,0:T(8,128)(2,1)S(1)}, u32[]{:S(2)}, u32[]{:S(2)}) %collective-permute-start.25) | collective-permute-done | bytes 65568 | tf_op jit(solution)/shard_map/ppermute | solution.py:14
  116.1 1.7 %collective-permute-start.30 = (bf16[32,1024]{1,0:T(8,128)(2,1)S(1)}, bf16[32,1024]{1,0:T(8,128)(2,1)S(1)}, u32[]{:S(2)}, u32[]{:S(2)}) collective-permute-start(bf16[32,1024]{1,0:T(8,128)(2,1)S(1)} %get-tuple-element.93), channel_id=1, source_target_pairs={{0,16},{4,20},{8,24},{12,28},{16,0},{20,4},{24,8},{28,12},{1,17},{... | collective-permute-start | bytes 196616 | tf_op jit(solution)/shard_map/ppermute | solution.py:14
  118.0 2.4 %collective-permute-done.30 = bf16[32,1024]{1,0:T(8,128)(2,1)S(1)} collective-permute-done((bf16[32,1024]{1,0:T(8,128)(2,1)S(1)}, bf16[32,1024]{1,0:T(8,128)(2,1)S(1)}, u32[]{:S(2)}, u32[]{:S(2)}) %collective-permute-start.30) | collective-permute-done | bytes 65568 | tf_op jit(solution)/shard_map/ppermute | solution.py:14
  120.4 3.6 %gather_fusion.1 = f32[768,1024]{1,0:T(8,128)} fusion(f32[768,1024]{1,0:T(8,128)S(1)} %convert_dynamic-update-slice_fusion.3, s32[1024]{0:T(1024)S(1)} %pad_clamp_fusion), kind=kCustom, calls=%fused_computation.1 | custom fusion | bytes 6294528 | tf_op jit(solution)/shard_map/gather | solution.py:161
  (132 shorter events, 25.7 us)
Async XLA Ops:
  0.0 15.1 %copy-start = (s32[1024]{0:T(1024)S(1)}, s32[1024]{0:T(1024)}, u32[]{:S(2)}) copy-start(s32[1024]{0:T(1024)} %param.5) | copy-start | bytes 12292
  0.0 26.3 %collective-permute-start.1 = (bf16[128,4096]{1,0:T(8,128)(2,1)}, bf16[128,4096]{1,0:T(8,128)(2,1)S(1)}, u32[]{:S(2)}, u32[]{:S(2)}) collective-permute-start(bf16[128,4096]{1,0:T(8,128)(2,1)} %param.4), channel_id=1, source_target_pairs={{0,16},{4,20},{8,24},{12,28},{16,0},{20,4},{24,8},{28,12},{1,17},{... | collective-permute-start | bytes 3145736 | tf_op jit(solution)/shard_map/ppermute | solution.py:14
  3.0 12.7 %collective-permute-start = (bf16[128,4096]{1,0:T(8,128)(2,1)}, bf16[128,4096]{1,0:T(8,128)(2,1)}, u32[]{:S(2)}, u32[]{:S(2)}) collective-permute-start(bf16[128,4096]{1,0:T(8,128)(2,1)} %param.4), channel_id=1, source_target_pairs={{0,4},{4,0},{8,12},{12,8},{16,20},{20,16},{24,28},{28,24},{1,5},{5... | collective-permute-start | bytes 3145736 | tf_op jit(solution)/shard_map/ppermute | solution.py:14
  3.0 26.6 %collective-permute-start.3 = (bf16[128,4096]{1,0:T(8,128)(2,1)}, bf16[128,4096]{1,0:T(8,128)(2,1)S(1)}, u32[]{:S(2)}, u32[]{:S(2)}) collective-permute-start(bf16[128,4096]{1,0:T(8,128)(2,1)} %param.4), channel_id=1, source_target_pairs={{0,8},{4,12},{8,0},{12,4},{16,24},{20,28},{24,16},{28,20},{1,9},{5... | collective-permute-start | bytes 3145736 | tf_op jit(solution)/shard_map/ppermute | solution.py:14
  26.3 3.3 %collective-permute-start.2 = (bf16[128,4096]{1,0:T(8,128)(2,1)S(1)}, bf16[128,4096]{1,0:T(8,128)(2,1)S(1)}, u32[]{:S(2)}, u32[]{:S(2)}) collective-permute-start(bf16[128,4096]{1,0:T(8,128)(2,1)S(1)} %collective-permute-done.1), channel_id=1, source_target_pairs={{0,4},{4,0},{8,12},{12,8},{16,20},{20,16},{24,28},{28,24},{1,5},{5... | collective-permute-start | bytes 3145736 | tf_op jit(solution)/shard_map/ppermute | solution.py:14
  26.5 17.6 %collective-permute-start.6 = (bf16[80,4096]{1,0:T(8,128)(2,1)S(1)}, bf16[80,4096]{1,0:T(8,128)(2,1)S(1)}, u32[]{:S(2)}, u32[]{:S(2)}) collective-permute-start(bf16[80,4096]{1,0:T(8,128)(2,1)S(1)} %slice.154), channel_id=1, source_target_pairs={{0,8},{4,12},{8,0},{12,4},{16,24},{20,28},{24,16},{28,20},{1,9},{5... | collective-permute-start | bytes 1966088 | tf_op jit(solution)/shard_map/ppermute | solution.py:14
  29.6 4.1 %collective-permute-start.4 = (bf16[128,4096]{1,0:T(8,128)(2,1)S(1)}, bf16[128,4096]{1,0:T(8,128)(2,1)S(1)}, u32[]{:S(2)}, u32[]{:S(2)}) collective-permute-start(bf16[128,4096]{1,0:T(8,128)(2,1)S(1)} %collective-permute-done.3), channel_id=1, source_target_pairs={{0,4},{4,0},{8,12},{12,8},{16,20},{20,16},{24,28},{28,24},{1,5},{5... | collective-permute-start | bytes 3145736 | tf_op jit(solution)/shard_map/ppermute | solution.py:14
  32.1 12.0 %collective-permute-start.7 = (bf16[48,4096]{1,0:T(8,128)(2,1)S(1)}, bf16[48,4096]{1,0:T(8,128)(2,1)S(1)}, u32[]{:S(2)}, u32[]{:S(2)}) collective-permute-start(bf16[48,4096]{1,0:T(8,128)(2,1)S(1)} %slice.156), channel_id=1, source_target_pairs={{0,16},{4,20},{8,24},{12,28},{16,0},{20,4},{24,8},{28,12},{1,17},{... | collective-permute-start | bytes 1179656 | tf_op jit(solution)/shard_map/ppermute | solution.py:14
  35.7 15.1 %collective-permute-start.5 = (bf16[144,256]{1,0:T(8,128)(2,1)S(1)}, bf16[144,256]{1,0:T(8,128)(2,1)S(1)}, u32[]{:S(2)}, u32[]{:S(2)}) collective-permute-start(bf16[144,256]{1,0:T(8,128)(2,1)S(1)} %slice.205), channel_id=1, source_target_pairs={{0,16},{4,20},{8,24},{12,28},{16,0},{20,4},{24,8},{28,12},{1,17},{... | collective-permute-start | bytes 221192 | tf_op jit(solution)/shard_map/ppermute | solution.py:14
  36.3 13.6 %collective-permute-start.11 = (bf16[384,256]{1,0:T(8,128)(2,1)S(1)}, bf16[384,256]{1,0:T(8,128)(2,1)S(1)}, u32[]{:S(2)}, u32[]{:S(2)}) collective-permute-start(bf16[384,256]{1,0:T(8,128)(2,1)S(1)} %slice.209), channel_id=1, source_target_pairs={{0,16},{4,20},{8,24},{12,28},{16,0},{20,4},{24,8},{28,12},{1,17},{... | collective-permute-start | bytes 589832 | tf_op jit(solution)/shard_map/ppermute | solution.py:14
  44.1 1.7 %collective-permute-start.9 = (bf16[48,4096]{1,0:T(8,128)(2,1)S(1)}, bf16[48,4096]{1,0:T(8,128)(2,1)S(1)}, u32[]{:S(2)}, u32[]{:S(2)}) collective-permute-start(bf16[48,4096]{1,0:T(8,128)(2,1)S(1)} %collective-permute-done.7), channel_id=1, source_target_pairs={{0,4},{4,0},{8,12},{12,8},{16,20},{20,16},{24,28},{28,24},{1,5},{5... | collective-permute-start | bytes 1179656 | tf_op jit(solution)/shard_map/ppermute | solution.py:14
  44.1 3.2 %collective-permute-start.8 = (bf16[80,4096]{1,0:T(8,128)(2,1)S(1)}, bf16[80,4096]{1,0:T(8,128)(2,1)S(1)}, u32[]{:S(2)}, u32[]{:S(2)}) collective-permute-start(bf16[80,4096]{1,0:T(8,128)(2,1)S(1)} %collective-permute-done.6), channel_id=1, source_target_pairs={{0,4},{4,0},{8,12},{12,8},{16,20},{20,16},{24,28},{28,24},{1,5},{5... | collective-permute-start | bytes 1966088 | tf_op jit(solution)/shard_map/ppermute | solution.py:14
  45.8 5.0 %collective-permute-start.12 = (bf16[144,256]{1,0:T(8,128)(2,1)S(1)}, bf16[144,256]{1,0:T(8,128)(2,1)S(1)}, u32[]{:S(2)}, u32[]{:S(2)}) collective-permute-start(bf16[144,256]{1,0:T(8,128)(2,1)S(1)} %slice.211), channel_id=1, source_target_pairs={{0,16},{4,20},{8,24},{12,28},{16,0},{20,4},{24,8},{28,12},{1,17},{... | collective-permute-start | bytes 221192 | tf_op jit(solution)/shard_map/ppermute | solution.py:14
  50.9 4.4 %collective-permute-start.10 = (bf16[144,256]{1,0:T(8,128)(2,1)S(1)}, bf16[144,256]{1,0:T(8,128)(2,1)S(1)}, u32[]{:S(2)}, u32[]{:S(2)}) collective-permute-start(bf16[144,256]{1,0:T(8,128)(2,1)S(1)} %slice.207), channel_id=1, source_target_pairs={{0,16},{4,20},{8,24},{12,28},{16,0},{20,4},{24,8},{28,12},{1,17},{... | collective-permute-start | bytes 221192 | tf_op jit(solution)/shard_map/ppermute | solution.py:14
  57.0 18.8 %collective-permute-start.13 = (bf16[144,2048]{1,0:T(8,128)(2,1)S(1)}, bf16[144,2048]{1,0:T(8,128)(2,1)S(1)}, u32[]{:S(2)}, u32[]{:S(2)}) collective-permute-start(bf16[144,2048]{1,0:T(8,128)(2,1)S(1)} %pad_maximum_fusion), channel_id=1, source_target_pairs={{0,1},{1,0},{2,3},{3,2},{4,5},{5,4},{6,7},{7,6},{8,9},{9,8},{10,11... | collective-permute-start | bytes 1769480 | tf_op jit(solution)/shard_map/ppermute | solution.py:14
  58.6 5.9 %collective-permute-start.15 = (bf16[240,256]{1,0:T(8,128)(2,1)S(1)}, bf16[240,256]{1,0:T(8,128)(2,1)S(1)}, u32[]{:S(2)}, u32[]{:S(2)}) collective-permute-start(bf16[240,256]{1,0:T(8,128)(2,1)S(1)} %slice.213), channel_id=1, source_target_pairs={{0,16},{4,20},{8,24},{12,28},{16,0},{20,4},{24,8},{28,12},{1,17},{... | collective-permute-start | bytes 368648 | tf_op jit(solution)/shard_map/ppermute | solution.py:14
  60.1 5.7 %collective-permute-start.16 = (bf16[240,256]{1,0:T(8,128)(2,1)S(1)}, bf16[240,256]{1,0:T(8,128)(2,1)S(1)}, u32[]{:S(2)}, u32[]{:S(2)}) collective-permute-start(bf16[240,256]{1,0:T(8,128)(2,1)S(1)} %slice.216), channel_id=1, source_target_pairs={{0,16},{4,20},{8,24},{12,28},{16,0},{20,4},{24,8},{28,12},{1,17},{... | collective-permute-start | bytes 368648 | tf_op jit(solution)/shard_map/ppermute | solution.py:14
  60.6 6.5 %collective-permute-start.17 = (bf16[240,256]{1,0:T(8,128)(2,1)S(1)}, bf16[240,256]{1,0:T(8,128)(2,1)S(1)}, u32[]{:S(2)}, u32[]{:S(2)}) collective-permute-start(bf16[240,256]{1,0:T(8,128)(2,1)S(1)} %slice.220), channel_id=1, source_target_pairs={{0,16},{4,20},{8,24},{12,28},{16,0},{20,4},{24,8},{28,12},{1,17},{... | collective-permute-start | bytes 368648 | tf_op jit(solution)/shard_map/ppermute | solution.py:14
  68.8 16.9 %collective-permute-start.18 = (bf16[112,2048]{1,0:T(8,128)(2,1)S(1)}, bf16[112,2048]{1,0:T(8,128)(2,1)S(1)}, u32[]{:S(2)}, u32[]{:S(2)}) collective-permute-start(bf16[112,2048]{1,0:T(8,128)(2,1)S(1)} %pad_maximum_fusion.1), channel_id=1, source_target_pairs={{0,1},{1,0},{2,3},{3,2},{4,5},{5,4},{6,7},{7,6},{8,9},{9,8},{10,11... | collective-permute-start | bytes 1376264 | tf_op jit(solution)/shard_map/ppermute | solution.py:14
  76.0 29.3 %collective-permute-start.14 = (bf16[144,1024]{1,0:T(8,128)(2,1)S(1)}, bf16[144,1024]{1,0:T(8,128)(2,1)S(1)}, u32[]{:S(2)}, u32[]{:S(2)}) collective-permute-start(bf16[144,1024]{1,0:T(8,128)(2,1)S(1)} %dynamic-slice_convert_fusion), channel_id=1, source_target_pairs={{0,2},{1,3},{2,0},{3,1},{4,6},{5,7},{6,4},{7,5},{8,10},{9,11},{10,... | collective-permute-start | bytes 884744 | tf_op jit(solution)/shard_map/ppermute | solution.py:14
  85.8 21.1 %collective-permute-start.19 = (bf16[112,1024]{1,0:T(8,128)(2,1)S(1)}, bf16[112,1024]{1,0:T(8,128)(2,1)S(1)}, u32[]{:S(2)}, u32[]{:S(2)}) collective-permute-start(bf16[112,1024]{1,0:T(8,128)(2,1)S(1)} %dynamic-slice_convert_fusion.3), channel_id=1, source_target_pairs={{0,2},{1,3},{2,0},{3,1},{4,6},{5,7},{6,4},{7,5},{8,10},{9,11},{10,... | collective-permute-start | bytes 688136 | tf_op jit(solution)/shard_map/ppermute | solution.py:14
  88.1 15.7 %collective-permute-start.20 = (bf16[64,2048]{1,0:T(8,128)(2,1)S(1)}, bf16[64,2048]{1,0:T(8,128)(2,1)S(1)}, u32[]{:S(2)}, u32[]{:S(2)}) collective-permute-start(bf16[64,2048]{1,0:T(8,128)(2,1)S(1)} %pad_maximum_fusion.3), channel_id=1, source_target_pairs={{0,1},{1,0},{2,3},{3,2},{4,5},{5,4},{6,7},{7,6},{8,9},{9,8},{10,11... | collective-permute-start | bytes 786440 | tf_op jit(solution)/shard_map/ppermute | solution.py:14
  92.3 15.3 %collective-permute-start.22 = (bf16[32,2048]{1,0:T(8,128)(2,1)S(1)}, bf16[32,2048]{1,0:T(8,128)(2,1)S(1)}, u32[]{:S(2)}, u32[]{:S(2)}) collective-permute-start(bf16[32,2048]{1,0:T(8,128)(2,1)S(1)} %pad_maximum_fusion.6), channel_id=1, source_target_pairs={{0,1},{1,0},{2,3},{3,2},{4,5},{5,4},{6,7},{7,6},{8,9},{9,8},{10,11... | collective-permute-start | bytes 393224 | tf_op jit(solution)/shard_map/ppermute | solution.py:14
  93.9 15.4 %collective-permute-start.24 = (bf16[32,2048]{1,0:T(8,128)(2,1)S(1)}, bf16[32,2048]{1,0:T(8,128)(2,1)S(1)}, u32[]{:S(2)}, u32[]{:S(2)}) collective-permute-start(bf16[32,2048]{1,0:T(8,128)(2,1)S(1)} %pad_maximum_fusion.7), channel_id=1, source_target_pairs={{0,1},{1,0},{2,3},{3,2},{4,5},{5,4},{6,7},{7,6},{8,9},{9,8},{10,11... | collective-permute-start | bytes 393224 | tf_op jit(solution)/shard_map/ppermute | solution.py:14
  103.9 7.3 %collective-permute-start.21 = (bf16[64,1024]{1,0:T(8,128)(2,1)S(1)}, bf16[64,1024]{1,0:T(8,128)(2,1)S(1)}, u32[]{:S(2)}, u32[]{:S(2)}) collective-permute-start(bf16[64,1024]{1,0:T(8,128)(2,1)S(1)} %dynamic-slice_convert_fusion.6), channel_id=1, source_target_pairs={{0,2},{1,3},{2,0},{3,1},{4,6},{5,7},{6,4},{7,5},{8,10},{9,11},{10,... | collective-permute-start | bytes 393224 | tf_op jit(solution)/shard_map/ppermute | solution.py:14
  105.3 12.5 %collective-permute-start.26 = (bf16[144,1024]{1,0:T(8,128)(2,1)S(1)}, bf16[144,1024]{1,0:T(8,128)(2,1)S(1)}, u32[]{:S(2)}, u32[]{:S(2)}) collective-permute-start(bf16[144,1024]{1,0:T(8,128)(2,1)S(1)} %get-tuple-element.67), channel_id=1, source_target_pairs={{0,16},{4,20},{8,24},{12,28},{16,0},{20,4},{24,8},{28,12},{1,17},{... | collective-permute-start | bytes 884744 | tf_op jit(solution)/shard_map/ppermute | solution.py:14
  107.0 10.9 %collective-permute-start.27 = (bf16[112,1024]{1,0:T(8,128)(2,1)S(1)}, bf16[112,1024]{1,0:T(8,128)(2,1)S(1)}, u32[]{:S(2)}, u32[]{:S(2)}) collective-permute-start(bf16[112,1024]{1,0:T(8,128)(2,1)S(1)} %get-tuple-element.69), channel_id=1, source_target_pairs={{0,16},{4,20},{8,24},{12,28},{16,0},{20,4},{24,8},{28,12},{1,17},{... | collective-permute-start | bytes 688136 | tf_op jit(solution)/shard_map/ppermute | solution.py:14
  107.6 5.5 %collective-permute-start.23 = (bf16[32,1024]{1,0:T(8,128)(2,1)S(1)}, bf16[32,1024]{1,0:T(8,128)(2,1)S(1)}, u32[]{:S(2)}, u32[]{:S(2)}) collective-permute-start(bf16[32,1024]{1,0:T(8,128)(2,1)S(1)} %dynamic-slice_convert_fusion.12), channel_id=1, source_target_pairs={{0,2},{1,3},{2,0},{3,1},{4,6},{5,7},{6,4},{7,5},{8,10},{9,11},{10,... | collective-permute-start | bytes 196616 | tf_op jit(solution)/shard_map/ppermute | solution.py:14
  109.4 6.6 %collective-permute-start.25 = (bf16[32,1024]{1,0:T(8,128)(2,1)S(1)}, bf16[32,1024]{1,0:T(8,128)(2,1)S(1)}, u32[]{:S(2)}, u32[]{:S(2)}) collective-permute-start(bf16[32,1024]{1,0:T(8,128)(2,1)S(1)} %dynamic-slice_convert_fusion.9), channel_id=1, source_target_pairs={{0,2},{1,3},{2,0},{3,1},{4,6},{5,7},{6,4},{7,5},{8,10},{9,11},{10,... | collective-permute-start | bytes 196616 | tf_op jit(solution)/shard_map/ppermute | solution.py:14
  111.3 6.6 %collective-permute-start.28 = (bf16[64,1024]{1,0:T(8,128)(2,1)S(1)}, bf16[64,1024]{1,0:T(8,128)(2,1)S(1)}, u32[]{:S(2)}, u32[]{:S(2)}) collective-permute-start(bf16[64,1024]{1,0:T(8,128)(2,1)S(1)} %get-tuple-element.75), channel_id=1, source_target_pairs={{0,16},{4,20},{8,24},{12,28},{16,0},{20,4},{24,8},{28,12},{1,17},{... | collective-permute-start | bytes 393224 | tf_op jit(solution)/shard_map/ppermute | solution.py:14
  113.2 4.8 %collective-permute-start.29 = (bf16[32,1024]{1,0:T(8,128)(2,1)S(1)}, bf16[32,1024]{1,0:T(8,128)(2,1)S(1)}, u32[]{:S(2)}, u32[]{:S(2)}) collective-permute-start(bf16[32,1024]{1,0:T(8,128)(2,1)S(1)} %get-tuple-element.95), channel_id=1, source_target_pairs={{0,16},{4,20},{8,24},{12,28},{16,0},{20,4},{24,8},{28,12},{1,17},{... | collective-permute-start | bytes 196616 | tf_op jit(solution)/shard_map/ppermute | solution.py:14
  116.1 4.3 %collective-permute-start.30 = (bf16[32,1024]{1,0:T(8,128)(2,1)S(1)}, bf16[32,1024]{1,0:T(8,128)(2,1)S(1)}, u32[]{:S(2)}, u32[]{:S(2)}) collective-permute-start(bf16[32,1024]{1,0:T(8,128)(2,1)S(1)} %get-tuple-element.93), channel_id=1, source_target_pairs={{0,16},{4,20},{8,24},{12,28},{16,0},{20,4},{24,8},{28,12},{1,17},{... | collective-permute-start | bytes 196616 | tf_op jit(solution)/shard_map/ppermute | solution.py:14
  (3 other events, 38.9 us)

commit v5 on v3

--- a/solution.py
+++ b/solution.py
@@ -108,10 +108,11 @@
             send(m, 0, early, *(pieces[3] if m == apart else []))
     pieces[2 * end] = [after(part, *weights.values()) for part in pieces[2 * end]]
     pieces[2 * end + 1] = [swap(part, "ref", 1) for part in pieces[2 * end]]
-    send(1, 0, early, pieces[2 * end + 1][-1])
     score(end)
     sent = {m: [after(part, weights[end]) for part in parts] for m, parts in sent.items()}
-    send(end, 0, early)
+    joint = swap(jnp.concatenate([weights[m][half : half + early] for m in (end, 1)], axis=1), "ref", top)
+    sent[end ^ apart] = [joint[:, : 2 * img_rows]]
+    sent[1 ^ apart] = [joint[:, 2 * img_rows :]]
 
     order = range(blocks)
     every_image = images_of(order)

time: 121 us -> 122 us (level)
  waiting for transfers between devices: 42.6 us -> 44.1 us
  starting transfers between devices: 40.8 us -> 39.5 us
    ppermute x31 -> x30, waiting for transfers between devices: 42.6 us -> 44.1 us  [swap(): return lax.ppermute(block, axis, [(i, i ^ bit) for i in range(count)])]
    ppermute x31 -> x30, starting transfers between devices: 40.8 us -> 39.5 us  [swap(): return lax.ppermute(block, axis, [(i, i ^ bit) for i in range(count)])]
  transfers between devices with their start and end apart: 31 -> 30, of which waited for: 16 -> 17; matrix products, arithmetic and copies ran while one was open for 26% -> 26% of each run, Pallas kernels for 0% -> 0%
where the time goes in v5:
time: 122 us; the launch traced here: 121 us
  waiting for transfers between devices  44.1 us (36%)
  starting transfers between devices  39.5 us (32%)
  matrix products  28 us (23%)
  local copies, waits for them, and re-layouts  7.02 us (6%)
  other arithmetic  1.94 us (2%)
    ppermute x30, waiting for transfers between devices, swap(): return lax.ppermute(block, axis, [(i, i ^ bit) for i in range(count)])  44.1 us
    ppermute x30, starting transfers between devices, swap(): return lax.ppermute(block, axis, [(i, i ^ bit) for i in range(count)])  39.5 us
    dot_general x4, matrix products, score(): lax.dot_general(refs, images_of([m]), (((1,), (1,)), ((), ())), preferred...  10.7 us
    dot_general x1, matrix products, body(): refs = jnp.dot(one_hot, references, preferred_element_type=F32).astype(BF16)  9.89 us
    dot_general x5, matrix products, body(): jnp.dot(w, every_image, preferred_element_type=F32) * scale  7.43 us
    gather x1, local copies, waits for them, and re-layouts, body(): jnp.concatenate(done + other, axis=0).at[place]  3.61 us
  transfers between devices with their start and end apart: 30, of which 17 were waited for; matrix products, arithmetic and copies ran while one was open for 26% of the time, Pallas kernels for 0%

profile of v5, /device:TPU:0, one launch (start us, length us, event | category | flops | bytes accessed | tf_op | source)
XLA Modules:
  0.0 121.4 jit_solution(11553864533304478180)
XLA Ops:
  0.0 3.0 %collective-permute-start.1 = (bf16[128,4096]{1,0:T(8,128)(2,1)}, bf16[128,4096]{1,0:T(8,128)(2,1)S(1)}, u32[]{:S(2)}, u32[]{:S(2)}) collective-permute-start(bf16[128,4096]{1,0:T(8,128)(2,1)} %param.4), channel_id=1, source_target_pairs={{0,16},{4,20},{8,24},{12,28},{16,0},{20,4},{24,8},{28,12},{1,17},{... | collective-permute-start | bytes 3145736 | tf_op jit(solution)/shard_map/ppermute | solution.py:14
  5.2 9.9 %multiply_reduce_fusion = (f32[768]{0:T(1024)S(1)}, bf16[768,4096]{1,0:T(8,128)(2,1)}) fusion(bf16[768,4096]{1,0:T(8,128)(2,1)} %param.6, s32[768]{0:T(1024)S(1)} %get-tuple-element.54), kind=kOutput, calls=%fused_computation.2 | convolution fusion | flops 4845009920 | bytes 12589056 | tf_op jit(solution)/shard_map/dot_general | solution.py:54
  15.7 5.0 %fusion.74 = bf16[768,256]{1,0:T(8,128)(2,1)S(1)} fusion(bf16[768,4096]{1,0:T(8,128)(2,1)} %get-tuple-element.92, bf16[128,4096]{1,0:T(8,128)(2,1)} %collective-permute-done, bf16[128,4096]{1,0:T(8,128)(2,1)S(1)} %copy-done.1, f32[256]{0:T(256)S(1)} %get-tuple-element.90, f32[768]{0:T(1024)S(1)} %broadcast_multiply_fusion), kind=kOutput, calls=%fused_computation.48 | convolution fusion | flops 1615593472 | bytes 8785920 | tf_op jit(solution)/shard_map/dot_general | solution.py:68
  20.8 5.6 %collective-permute-done.1 = bf16[128,4096]{1,0:T(8,128)(2,1)S(1)} collective-permute-done((bf16[128,4096]{1,0:T(8,128)(2,1)}, bf16[128,4096]{1,0:T(8,128)(2,1)S(1)}, u32[]{:S(2)}, u32[]{:S(2)}) %collective-permute-start.1) | collective-permute-done | bytes 1048608 | tf_op jit(solution)/shard_map/ppermute | solution.py:14
  26.5 1.8 %collective-permute-start.6 = (bf16[80,4096]{1,0:T(8,128)(2,1)S(1)}, bf16[80,4096]{1,0:T(8,128)(2,1)S(1)}, u32[]{:S(2)}, u32[]{:S(2)}) collective-permute-start(bf16[80,4096]{1,0:T(8,128)(2,1)S(1)} %slice.160), channel_id=1, source_target_pairs={{0,8},{4,12},{8,0},{12,4},{16,24},{20,28},{24,16},{28,20},{1,9},{5... | collective-permute-start | bytes 1966088 | tf_op jit(solution)/shard_map/ppermute | solution.py:14
  29.9 1.8 %fusion.71 = bf16[768,256]{1,0:T(8,128)(2,1)S(1)} fusion(bf16[768,4096]{1,0:T(8,128)(2,1)S(1)} %bitcast.28, bf16[128,4096]{1,0:T(8,128)(2,1)S(1)} %collective-permute-done.2, bf16[128,4096]{1,0:T(8,128)(2,1)S(1)} %collective-permute-done.1, f32[256]{0:T(256)S(1)} %get-tuple-element.89, f32[768]{0:T(1024)S(1)} %broadcast_multiply_fusion), kind=kOutput, calls=%fused_computation.47 | convolution fusion | flops 1615593472 | bytes 8785920 | tf_op jit(solution)/shard_map/dot_general | solution.py:68
  31.9 1.6 %collective-permute-start.7 = (bf16[48,4096]{1,0:T(8,128)(2,1)S(1)}, bf16[48,4096]{1,0:T(8,128)(2,1)S(1)}, u32[]{:S(2)}, u32[]{:S(2)}) collective-permute-start(bf16[48,4096]{1,0:T(8,128)(2,1)S(1)} %slice.162), channel_id=1, source_target_pairs={{0,16},{4,20},{8,24},{12,28},{16,0},{20,4},{24,8},{28,12},{1,17},{... | collective-permute-start | bytes 1179656 | tf_op jit(solution)/shard_map/ppermute | solution.py:14
  33.5 1.8 %fusion.68 = bf16[768,256]{1,0:T(8,128)(2,1)S(1)} fusion(bf16[768,4096]{1,0:T(8,128)(2,1)S(1)} %bitcast.28, bf16[128,4096]{1,0:T(8,128)(2,1)S(1)} %collective-permute-done.4, bf16[128,4096]{1,0:T(8,128)(2,1)S(1)} %collective-permute-done.3, f32[256]{0:T(256)S(1)} %get-tuple-element.88, f32[768]{0:T(1024)S(1)} %broadcast_multiply_fusion), kind=kOutput, calls=%fused_computation.46 | convolution fusion | flops 1615593472 | bytes 8785920 | tf_op jit(solution)/shard_map/dot_general | solution.py:68
  37.4 6.5 %collective-permute-done.7 = bf16[48,4096]{1,0:T(8,128)(2,1)S(1)} collective-permute-done((bf16[48,4096]{1,0:T(8,128)(2,1)S(1)}, bf16[48,4096]{1,0:T(8,128)(2,1)S(1)}, u32[]{:S(2)}, u32[]{:S(2)}) %collective-permute-start.7) | collective-permute-done | bytes 393248 | tf_op jit(solution)/shard_map/ppermute | solution.py:14
  46.6 2.0 %fusion.77 = bf16[768,256]{1,0:T(8,128)(2,1)S(1)} fusion(bf16[768,4096]{1,0:T(8,128)(2,1)S(1)} %bitcast.28, bf16[48,4096]{1,0:T(8,128)(2,1)S(1)} %collective-permute-done.9, bf16[80,4096]{1,0:T(8,128)(2,1)S(1)} %collective-permute-done.8, bf16[48,4096]{1,0:T(8,128)(2,1)S(1)} %collective-permute-done.7, bf16[80,4096]{1,0:T(8,128)(2,1)S(1)} %collective-permute-done.6, ...), kind=kOutput, calls=%fused_computation.49 | convolution fusion | flops 1619787776 | bytes 8785920 | tf_op jit(solution)/shard_map/dot_general | solution.py:68
  49.1 1.6 %collective-permute-start.10 = (bf16[128,512]{1,0:T(8,128)(2,1)S(1)}, bf16[128,512]{1,0:T(8,128)(2,1)S(1)}, u32[]{:S(2)}, u32[]{:S(2)}) collective-permute-start(bf16[128,512]{1,0:T(8,128)(2,1)S(1)} %pad_maximum_fusion.6), channel_id=1, source_target_pairs={{0,16},{4,20},{8,24},{12,28},{16,0},{20,4},{24,8},{28,12},{1,17},{... | collective-permute-start | bytes 393224 | tf_op jit(solution)/shard_map/ppermute | solution.py:14
  50.8 3.6 %collective-permute-done.10 = bf16[128,512]{1,0:T(8,128)(2,1)S(1)} collective-permute-done((bf16[128,512]{1,0:T(8,128)(2,1)S(1)}, bf16[128,512]{1,0:T(8,128)(2,1)S(1)}, u32[]{:S(2)}, u32[]{:S(2)}) %collective-permute-start.10) | collective-permute-done | bytes 131104 | tf_op jit(solution)/shard_map/ppermute | solution.py:14
  55.9 1.7 %collective-permute-start.12 = (bf16[128,2048]{1,0:T(8,128)(2,1)S(1)}, bf16[128,2048]{1,0:T(8,128)(2,1)S(1)}, u32[]{:S(2)}, u32[]{:S(2)}) collective-permute-start(bf16[128,2048]{1,0:T(8,128)(2,1)S(1)} %pad_maximum_fusion), channel_id=1, source_target_pairs={{0,1},{1,0},{2,3},{3,2},{4,5},{5,4},{6,7},{7,6},{8,9},{9,8},{10,11... | collective-permute-start | bytes 1572872 | tf_op jit(solution)/shard_map/ppermute | solution.py:14
  57.6 1.5 %collective-permute-start.14 = (bf16[256,256]{1,0:T(8,128)(2,1)S(1)}, bf16[256,256]{1,0:T(8,128)(2,1)S(1)}, u32[]{:S(2)}, u32[]{:S(2)}) collective-permute-start(bf16[256,256]{1,0:T(8,128)(2,1)S(1)} %slice.223), channel_id=1, source_target_pairs={{0,16},{4,20},{8,24},{12,28},{16,0},{20,4},{24,8},{28,12},{1,17},{... | collective-permute-start | bytes 393224 | tf_op jit(solution)/shard_map/ppermute | solution.py:14
  59.6 1.5 %collective-permute-start.16 = (bf16[256,256]{1,0:T(8,128)(2,1)S(1)}, bf16[256,256]{1,0:T(8,128)(2,1)S(1)}, u32[]{:S(2)}, u32[]{:S(2)}) collective-permute-start(bf16[256,256]{1,0:T(8,128)(2,1)S(1)} %slice.230), channel_id=1, source_target_pairs={{0,16},{4,20},{8,24},{12,28},{16,0},{20,4},{24,8},{28,12},{1,17},{... | collective-permute-start | bytes 393224 | tf_op jit(solution)/shard_map/ppermute | solution.py:14
  61.3 2.8 %collective-permute-done.14 = bf16[256,256]{1,0:T(8,128)(2,1)S(1)} collective-permute-done((bf16[256,256]{1,0:T(8,128)(2,1)S(1)}, bf16[256,256]{1,0:T(8,128)(2,1)S(1)}, u32[]{:S(2)}, u32[]{:S(2)}) %collective-permute-start.14) | collective-permute-done | bytes 131104 | tf_op jit(solution)/shard_map/ppermute | solution.py:14
  64.1 1.9 %collective-permute-done.15 = bf16[256,256]{1,0:T(8,128)(2,1)S(1)} collective-permute-done((bf16[256,256]{1,0:T(8,128)(2,1)S(1)}, bf16[256,256]{1,0:T(8,128)(2,1)S(1)}, u32[]{:S(2)}, u32[]{:S(2)}) %collective-permute-start.15) | collective-permute-done | bytes 131104 | tf_op jit(solution)/shard_map/ppermute | solution.py:14
  70.1 2.7 %collective-permute-start.13 = (bf16[128,1024]{1,0:T(8,128)(2,1)S(1)}, bf16[128,1024]{1,0:T(8,128)(2,1)S(1)}, u32[]{:S(2)}, u32[]{:S(2)}) collective-permute-start(bf16[128,1024]{1,0:T(8,128)(2,1)S(1)} %dynamic-slice_convert_fusion), channel_id=1, source_target_pairs={{0,2},{1,3},{2,0},{3,1},{4,6},{5,7},{6,4},{7,5},{8,10},{9,11},{10,... | collective-permute-start | bytes 786440 | tf_op jit(solution)/shard_map/ppermute | solution.py:14
  72.8 1.6 %convolution_multiply_fusion.2 = f32[64,4096]{1,0:T(8,128)S(1)} fusion(bf16[64,1024]{1,0:T(8,128)(2,1)S(1)} %pad_maximum_fusion.7, bf16[1024,4096]{1,0:T(8,128)(2,1)S(1)} %constant_dynamic-update-slice_fusion), kind=kOutput, calls=%fused_computation.6 | convolution fusion | flops 537133056 | bytes 9568256 | tf_op jit(solution)/shard_map/dot_general | solution.py:144
  74.5 1.6 %collective-permute-start.19 = (bf16[64,2048]{1,0:T(8,128)(2,1)S(1)}, bf16[64,2048]{1,0:T(8,128)(2,1)S(1)}, u32[]{:S(2)}, u32[]{:S(2)}) collective-permute-start(bf16[64,2048]{1,0:T(8,128)(2,1)S(1)} %pad_maximum_fusion.3), channel_id=1, source_target_pairs={{0,1},{1,0},{2,3},{3,2},{4,5},{5,4},{6,7},{7,6},{8,9},{9,8},{10,11... | collective-permute-start | bytes 786440 | tf_op jit(solution)/shard_map/ppermute | solution.py:14
  76.2 10.8 %collective-permute-done.17 = bf16[112,2048]{1,0:T(8,128)(2,1)S(1)} collective-permute-done((bf16[112,2048]{1,0:T(8,128)(2,1)S(1)}, bf16[112,2048]{1,0:T(8,128)(2,1)S(1)}, u32[]{:S(2)}, u32[]{:S(2)}) %collective-permute-start.17) | collective-permute-done | bytes 458784 | tf_op jit(solution)/shard_map/ppermute | solution.py:14
  87.1 3.0 %collective-permute-start.18 = (bf16[112,1024]{1,0:T(8,128)(2,1)S(1)}, bf16[112,1024]{1,0:T(8,128)(2,1)S(1)}, u32[]{:S(2)}, u32[]{:S(2)}) collective-permute-start(bf16[112,1024]{1,0:T(8,128)(2,1)S(1)} %dynamic-slice_convert_fusion.3), channel_id=1, source_target_pairs={{0,2},{1,3},{2,0},{3,1},{4,6},{5,7},{6,4},{7,5},{8,10},{9,11},{10,... | collective-permute-start | bytes 688136 | tf_op jit(solution)/shard_map/ppermute | solution.py:14
  90.1 1.6 %convolution_multiply_fusion.3 = f32[48,4096]{1,0:T(8,128)S(1)} fusion(bf16[48,1024]{1,0:T(8,128)(2,1)S(1)} %pad_maximum_fusion.9, bf16[1024,4096]{1,0:T(8,128)(2,1)S(1)} %constant_dynamic-update-slice_fusion), kind=kOutput, calls=%fused_computation.7 | convolution fusion | flops 402849792 | bytes 9273344 | tf_op jit(solution)/shard_map/dot_general | solution.py:144
  91.7 3.0 %collective-permute-start.21 = (bf16[48,2048]{1,0:T(8,128)(2,1)S(1)}, bf16[48,2048]{1,0:T(8,128)(2,1)S(1)}, u32[]{:S(2)}, u32[]{:S(2)}) collective-permute-start(bf16[48,2048]{1,0:T(8,128)(2,1)S(1)} %pad_maximum_fusion.5), channel_id=1, source_target_pairs={{0,1},{1,0},{2,3},{3,2},{4,5},{5,4},{6,7},{7,6},{8,9},{9,8},{10,11... | collective-permute-start | bytes 589832 | tf_op jit(solution)/shard_map/ppermute | solution.py:14
  94.8 1.5 %convolution_multiply_fusion.4 = f32[32,4096]{1,0:T(8,128)S(1)} fusion(bf16[32,1024]{1,0:T(8,128)(2,1)S(1)} %pad_maximum_fusion.10, bf16[1024,4096]{1,0:T(8,128)(2,1)S(1)} %constant_dynamic-update-slice_fusion), kind=kOutput, calls=%fused_computation.8 | convolution fusion | flops 268566528 | bytes 8978432 | tf_op jit(solution)/shard_map/dot_general | solution.py:144
  96.5 2.3 %collective-permute-done.19 = bf16[64,2048]{1,0:T(8,128)(2,1)S(1)} collective-permute-done((bf16[64,2048]{1,0:T(8,128)(2,1)S(1)}, bf16[64,2048]{1,0:T(8,128)(2,1)S(1)}, u32[]{:S(2)}, u32[]{:S(2)}) %collective-permute-start.19) | collective-permute-done | bytes 262176 | tf_op jit(solution)/shard_map/ppermute | solution.py:14
  99.0 1.6 %collective-permute-start.25 = (bf16[128,1024]{1,0:T(8,128)(2,1)S(1)}, bf16[128,1024]{1,0:T(8,128)(2,1)S(1)}, u32[]{:S(2)}, u32[]{:S(2)}) collective-permute-start(bf16[128,1024]{1,0:T(8,128)(2,1)S(1)} %get-tuple-element.63), channel_id=1, source_target_pairs={{0,16},{4,20},{8,24},{12,28},{16,0},{20,4},{24,8},{28,12},{1,17},{... | collective-permute-start | bytes 786440 | tf_op jit(solution)/shard_map/ppermute | solution.py:14
  102.5 3.7 %collective-permute-start.22 = (bf16[48,1024]{1,0:T(8,128)(2,1)S(1)}, bf16[48,1024]{1,0:T(8,128)(2,1)S(1)}, u32[]{:S(2)}, u32[]{:S(2)}) collective-permute-start(bf16[48,1024]{1,0:T(8,128)(2,1)S(1)} %dynamic-slice_convert_fusion.9), channel_id=1, source_target_pairs={{0,2},{1,3},{2,0},{3,1},{4,6},{5,7},{6,4},{7,5},{8,10},{9,11},{10,... | collective-permute-start | bytes 294920 | tf_op jit(solution)/shard_map/ppermute | solution.py:14
  107.6 2.1 %collective-permute-done.20 = bf16[64,1024]{1,0:T(8,128)(2,1)S(1)} collective-permute-done((bf16[64,1024]{1,0:T(8,128)(2,1)S(1)}, bf16[64,1024]{1,0:T(8,128)(2,1)S(1)}, u32[]{:S(2)}, u32[]{:S(2)}) %collective-permute-start.20) | collective-permute-done | bytes 131104 | tf_op jit(solution)/shard_map/ppermute | solution.py:14
  109.8 1.6 %collective-permute-start.27 = (bf16[64,1024]{1,0:T(8,128)(2,1)S(1)}, bf16[64,1024]{1,0:T(8,128)(2,1)S(1)}, u32[]{:S(2)}, u32[]{:S(2)}) collective-permute-start(bf16[64,1024]{1,0:T(8,128)(2,1)S(1)} %get-tuple-element.75), channel_id=1, source_target_pairs={{0,16},{4,20},{8,24},{12,28},{16,0},{20,4},{24,8},{28,12},{1,17},{... | collective-permute-start | bytes 393224 | tf_op jit(solution)/shard_map/ppermute | solution.py:14
  111.9 1.6 %collective-permute-start.28 = (bf16[48,1024]{1,0:T(8,128)(2,1)S(1)}, bf16[48,1024]{1,0:T(8,128)(2,1)S(1)}, u32[]{:S(2)}, u32[]{:S(2)}) collective-permute-start(bf16[48,1024]{1,0:T(8,128)(2,1)S(1)} %get-tuple-element.81), channel_id=1, source_target_pairs={{0,16},{4,20},{8,24},{12,28},{16,0},{20,4},{24,8},{28,12},{1,17},{... | collective-permute-start | bytes 294920 | tf_op jit(solution)/shard_map/ppermute | solution.py:14
  117.8 3.6 %gather_fusion.1 = f32[768,1024]{1,0:T(8,128)} fusion(f32[768,1024]{1,0:T(8,128)S(1)} %convert_dynamic-update-slice_fusion.4, s32[1024]{0:T(1024)S(1)} %pad_clamp_fusion), kind=kCustom, calls=%fused_computation.1 | custom fusion | bytes 6294528 | tf_op jit(solution)/shard_map/gather | solution.py:162
  (139 shorter events, 24.8 us)
Async XLA Ops:
  0.0 15.1 %copy-start = (s32[1024]{0:T(1024)S(1)}, s32[1024]{0:T(1024)}, u32[]{:S(2)}) copy-start(s32[1024]{0:T(1024)} %param.5) | copy-start | bytes 12292
  0.0 26.3 %collective-permute-start.1 = (bf16[128,4096]{1,0:T(8,128)(2,1)}, bf16[128,4096]{1,0:T(8,128)(2,1)S(1)}, u32[]{:S(2)}, u32[]{:S(2)}) collective-permute-start(bf16[128,4096]{1,0:T(8,128)(2,1)} %param.4), channel_id=1, source_target_pairs={{0,16},{4,20},{8,24},{12,28},{16,0},{20,4},{24,8},{28,12},{1,17},{... | collective-permute-start | bytes 3145736 | tf_op jit(solution)/shard_map/ppermute | solution.py:14
  3.0 12.7 %collective-permute-start = (bf16[128,4096]{1,0:T(8,128)(2,1)}, bf16[128,4096]{1,0:T(8,128)(2,1)}, u32[]{:S(2)}, u32[]{:S(2)}) collective-permute-start(bf16[128,4096]{1,0:T(8,128)(2,1)} %param.4), channel_id=1, source_target_pairs={{0,4},{4,0},{8,12},{12,8},{16,20},{20,16},{24,28},{28,24},{1,5},{5... | collective-permute-start | bytes 3145736 | tf_op jit(solution)/shard_map/ppermute | solution.py:14
  3.0 26.6 %collective-permute-start.3 = (bf16[128,4096]{1,0:T(8,128)(2,1)}, bf16[128,4096]{1,0:T(8,128)(2,1)S(1)}, u32[]{:S(2)}, u32[]{:S(2)}) collective-permute-start(bf16[128,4096]{1,0:T(8,128)(2,1)} %param.4), channel_id=1, source_target_pairs={{0,8},{4,12},{8,0},{12,4},{16,24},{20,28},{24,16},{28,20},{1,9},{5... | collective-permute-start | bytes 3145736 | tf_op jit(solution)/shard_map/ppermute | solution.py:14
  15.7 14.2 %slice-start.1 = ((s8[6291456]{0:T(1024)(128)(4,1)}), s8[4194304]{0:T(1024)(128)(4,1)S(1)}, s32[]{:S(2)}) async-start(s8[6291456]{0:T(1024)(128)(4,1)} %bitcast.27), calls=%async_computation.1 | async-start | bytes 8388608
  26.3 3.3 %collective-permute-start.2 = (bf16[128,4096]{1,0:T(8,128)(2,1)S(1)}, bf16[128,4096]{1,0:T(8,128)(2,1)S(1)}, u32[]{:S(2)}, u32[]{:S(2)}) collective-permute-start(bf16[128,4096]{1,0:T(8,128)(2,1)S(1)} %collective-permute-done.1), channel_id=1, source_target_pairs={{0,4},{4,0},{8,12},{12,8},{16,20},{20,16},{24,28},{28,24},{1,5},{5... | collective-permute-start | bytes 3145736 | tf_op jit(solution)/shard_map/ppermute | solution.py:14
  26.5 17.4 %collective-permute-start.6 = (bf16[80,4096]{1,0:T(8,128)(2,1)S(1)}, bf16[80,4096]{1,0:T(8,128)(2,1)S(1)}, u32[]{:S(2)}, u32[]{:S(2)}) collective-permute-start(bf16[80,4096]{1,0:T(8,128)(2,1)S(1)} %slice.160), channel_id=1, source_target_pairs={{0,8},{4,12},{8,0},{12,4},{16,24},{20,28},{24,16},{28,20},{1,9},{5... | collective-permute-start | bytes 1966088 | tf_op jit(solution)/shard_map/ppermute | solution.py:14
  29.6 3.9 %collective-permute-start.4 = (bf16[128,4096]{1,0:T(8,128)(2,1)S(1)}, bf16[128,4096]{1,0:T(8,128)(2,1)S(1)}, u32[]{:S(2)}, u32[]{:S(2)}) collective-permute-start(bf16[128,4096]{1,0:T(8,128)(2,1)S(1)} %collective-permute-done.3), channel_id=1, source_target_pairs={{0,4},{4,0},{8,12},{12,8},{16,20},{20,16},{24,28},{28,24},{1,5},{5... | collective-permute-start | bytes 3145736 | tf_op jit(solution)/shard_map/ppermute | solution.py:14
  31.9 12.0 %collective-permute-start.7 = (bf16[48,4096]{1,0:T(8,128)(2,1)S(1)}, bf16[48,4096]{1,0:T(8,128)(2,1)S(1)}, u32[]{:S(2)}, u32[]{:S(2)}) collective-permute-start(bf16[48,4096]{1,0:T(8,128)(2,1)S(1)} %slice.162), channel_id=1, source_target_pairs={{0,16},{4,20},{8,24},{12,28},{16,0},{20,4},{24,8},{28,12},{1,17},{... | collective-permute-start | bytes 1179656 | tf_op jit(solution)/shard_map/ppermute | solution.py:14
  35.3 13.6 %collective-permute-start.5 = (bf16[128,256]{1,0:T(8,128)(2,1)S(1)}, bf16[128,256]{1,0:T(8,128)(2,1)S(1)}, u32[]{:S(2)}, u32[]{:S(2)}) collective-permute-start(bf16[128,256]{1,0:T(8,128)(2,1)S(1)} %slice.213), channel_id=1, source_target_pairs={{0,16},{4,20},{8,24},{12,28},{16,0},{20,4},{24,8},{28,12},{1,17},{... | collective-permute-start | bytes 196616 | tf_op jit(solution)/shard_map/ppermute | solution.py:14
  35.9 13.0 %collective-permute-start.11 = (bf16[384,256]{1,0:T(8,128)(2,1)S(1)}, bf16[384,256]{1,0:T(8,128)(2,1)S(1)}, u32[]{:S(2)}, u32[]{:S(2)}) collective-permute-start(bf16[384,256]{1,0:T(8,128)(2,1)S(1)} %slice.219), channel_id=1, source_target_pairs={{0,16},{4,20},{8,24},{12,28},{16,0},{20,4},{24,8},{28,12},{1,17},{... | collective-permute-start | bytes 589832 | tf_op jit(solution)/shard_map/ppermute | solution.py:14
  43.9 1.7 %collective-permute-start.9 = (bf16[48,4096]{1,0:T(8,128)(2,1)S(1)}, bf16[48,4096]{1,0:T(8,128)(2,1)S(1)}, u32[]{:S(2)}, u32[]{:S(2)}) collective-permute-start(bf16[48,4096]{1,0:T(8,128)(2,1)S(1)} %collective-permute-done.7), channel_id=1, source_target_pairs={{0,4},{4,0},{8,12},{12,8},{16,20},{20,16},{24,28},{28,24},{1,5},{5... | collective-permute-start | bytes 1179656 | tf_op jit(solution)/shard_map/ppermute | solution.py:14
  43.9 2.7 %collective-permute-start.8 = (bf16[80,4096]{1,0:T(8,128)(2,1)S(1)}, bf16[80,4096]{1,0:T(8,128)(2,1)S(1)}, u32[]{:S(2)}, u32[]{:S(2)}) collective-permute-start(bf16[80,4096]{1,0:T(8,128)(2,1)S(1)} %collective-permute-done.6), channel_id=1, source_target_pairs={{0,4},{4,0},{8,12},{12,8},{16,20},{20,16},{24,28},{28,24},{1,5},{5... | collective-permute-start | bytes 1966088 | tf_op jit(solution)/shard_map/ppermute | solution.py:14
  49.1 5.3 %collective-permute-start.10 = (bf16[128,512]{1,0:T(8,128)(2,1)S(1)}, bf16[128,512]{1,0:T(8,128)(2,1)S(1)}, u32[]{:S(2)}, u32[]{:S(2)}) collective-permute-start(bf16[128,512]{1,0:T(8,128)(2,1)S(1)} %pad_maximum_fusion.6), channel_id=1, source_target_pairs={{0,16},{4,20},{8,24},{12,28},{16,0},{20,4},{24,8},{28,12},{1,17},{... | collective-permute-start | bytes 393224 | tf_op jit(solution)/shard_map/ppermute | solution.py:14
  55.9 14.0 %collective-permute-start.12 = (bf16[128,2048]{1,0:T(8,128)(2,1)S(1)}, bf16[128,2048]{1,0:T(8,128)(2,1)S(1)}, u32[]{:S(2)}, u32[]{:S(2)}) collective-permute-start(bf16[128,2048]{1,0:T(8,128)(2,1)S(1)} %pad_maximum_fusion), channel_id=1, source_target_pairs={{0,1},{1,0},{2,3},{3,2},{4,5},{5,4},{6,7},{7,6},{8,9},{9,8},{10,11... | collective-permute-start | bytes 1572872 | tf_op jit(solution)/shard_map/ppermute | solution.py:14
  57.6 6.4 %collective-permute-start.14 = (bf16[256,256]{1,0:T(8,128)(2,1)S(1)}, bf16[256,256]{1,0:T(8,128)(2,1)S(1)}, u32[]{:S(2)}, u32[]{:S(2)}) collective-permute-start(bf16[256,256]{1,0:T(8,128)(2,1)S(1)} %slice.223), channel_id=1, source_target_pairs={{0,16},{4,20},{8,24},{12,28},{16,0},{20,4},{24,8},{28,12},{1,17},{... | collective-permute-start | bytes 393224 | tf_op jit(solution)/shard_map/ppermute | solution.py:14
  59.1 6.8 %collective-permute-start.15 = (bf16[256,256]{1,0:T(8,128)(2,1)S(1)}, bf16[256,256]{1,0:T(8,128)(2,1)S(1)}, u32[]{:S(2)}, u32[]{:S(2)}) collective-permute-start(bf16[256,256]{1,0:T(8,128)(2,1)S(1)} %slice.226), channel_id=1, source_target_pairs={{0,16},{4,20},{8,24},{12,28},{16,0},{20,4},{24,8},{28,12},{1,17},{... | collective-permute-start | bytes 393224 | tf_op jit(solution)/shard_map/ppermute | solution.py:14
  59.6 7.7 %collective-permute-start.16 = (bf16[256,256]{1,0:T(8,128)(2,1)S(1)}, bf16[256,256]{1,0:T(8,128)(2,1)S(1)}, u32[]{:S(2)}, u32[]{:S(2)}) collective-permute-start(bf16[256,256]{1,0:T(8,128)(2,1)S(1)} %slice.230), channel_id=1, source_target_pairs={{0,16},{4,20},{8,24},{12,28},{16,0},{20,4},{24,8},{28,12},{1,17},{... | collective-permute-start | bytes 393224 | tf_op jit(solution)/shard_map/ppermute | solution.py:14
  69.0 18.0 %collective-permute-start.17 = (bf16[112,2048]{1,0:T(8,128)(2,1)S(1)}, bf16[112,2048]{1,0:T(8,128)(2,1)S(1)}, u32[]{:S(2)}, u32[]{:S(2)}) collective-permute-start(bf16[112,2048]{1,0:T(8,128)(2,1)S(1)} %pad_maximum_fusion.1), channel_id=1, source_target_pairs={{0,1},{1,0},{2,3},{3,2},{4,5},{5,4},{6,7},{7,6},{8,9},{9,8},{10,11... | collective-permute-start | bytes 1376264 | tf_op jit(solution)/shard_map/ppermute | solution.py:14
  70.1 26.4 %collective-permute-start.13 = (bf16[128,1024]{1,0:T(8,128)(2,1)S(1)}, bf16[128,1024]{1,0:T(8,128)(2,1)S(1)}, u32[]{:S(2)}, u32[]{:S(2)}) collective-permute-start(bf16[128,1024]{1,0:T(8,128)(2,1)S(1)} %dynamic-slice_convert_fusion), channel_id=1, source_target_pairs={{0,2},{1,3},{2,0},{3,1},{4,6},{5,7},{6,4},{7,5},{8,10},{9,11},{10,... | collective-permute-start | bytes 786440 | tf_op jit(solution)/shard_map/ppermute | solution.py:14
  74.5 24.3 %collective-permute-start.19 = (bf16[64,2048]{1,0:T(8,128)(2,1)S(1)}, bf16[64,2048]{1,0:T(8,128)(2,1)S(1)}, u32[]{:S(2)}, u32[]{:S(2)}) collective-permute-start(bf16[64,2048]{1,0:T(8,128)(2,1)S(1)} %pad_maximum_fusion.3), channel_id=1, source_target_pairs={{0,1},{1,0},{2,3},{3,2},{4,5},{5,4},{6,7},{7,6},{8,9},{9,8},{10,11... | collective-permute-start | bytes 786440 | tf_op jit(solution)/shard_map/ppermute | solution.py:14
  87.1 13.6 %collective-permute-start.18 = (bf16[112,1024]{1,0:T(8,128)(2,1)S(1)}, bf16[112,1024]{1,0:T(8,128)(2,1)S(1)}, u32[]{:S(2)}, u32[]{:S(2)}) collective-permute-start(bf16[112,1024]{1,0:T(8,128)(2,1)S(1)} %dynamic-slice_convert_fusion.3), channel_id=1, source_target_pairs={{0,2},{1,3},{2,0},{3,1},{4,6},{5,7},{6,4},{7,5},{8,10},{9,11},{10,... | collective-permute-start | bytes 688136 | tf_op jit(solution)/shard_map/ppermute | solution.py:14
  91.7 10.7 %collective-permute-start.21 = (bf16[48,2048]{1,0:T(8,128)(2,1)S(1)}, bf16[48,2048]{1,0:T(8,128)(2,1)S(1)}, u32[]{:S(2)}, u32[]{:S(2)}) collective-permute-start(bf16[48,2048]{1,0:T(8,128)(2,1)S(1)} %pad_maximum_fusion.5), channel_id=1, source_target_pairs={{0,1},{1,0},{2,3},{3,2},{4,5},{5,4},{6,7},{7,6},{8,9},{9,8},{10,11... | collective-permute-start | bytes 589832 | tf_op jit(solution)/shard_map/ppermute | solution.py:14
  96.4 9.8 %collective-permute-start.23 = (bf16[32,2048]{1,0:T(8,128)(2,1)S(1)}, bf16[32,2048]{1,0:T(8,128)(2,1)S(1)}, u32[]{:S(2)}, u32[]{:S(2)}) collective-permute-start(bf16[32,2048]{1,0:T(8,128)(2,1)S(1)} %pad_maximum_fusion.8), channel_id=1, source_target_pairs={{0,1},{1,0},{2,3},{3,2},{4,5},{5,4},{6,7},{7,6},{8,9},{9,8},{10,11... | collective-permute-start | bytes 393224 | tf_op jit(solution)/shard_map/ppermute | solution.py:14
  98.9 10.8 %collective-permute-start.20 = (bf16[64,1024]{1,0:T(8,128)(2,1)S(1)}, bf16[64,1024]{1,0:T(8,128)(2,1)S(1)}, u32[]{:S(2)}, u32[]{:S(2)}) collective-permute-start(bf16[64,1024]{1,0:T(8,128)(2,1)S(1)} %dynamic-slice_convert_fusion.6), channel_id=1, source_target_pairs={{0,2},{1,3},{2,0},{3,1},{4,6},{5,7},{6,4},{7,5},{8,10},{9,11},{10,... | collective-permute-start | bytes 393224 | tf_op jit(solution)/shard_map/ppermute | solution.py:14
  99.0 15.1 %collective-permute-start.25 = (bf16[128,1024]{1,0:T(8,128)(2,1)S(1)}, bf16[128,1024]{1,0:T(8,128)(2,1)S(1)}, u32[]{:S(2)}, u32[]{:S(2)}) collective-permute-start(bf16[128,1024]{1,0:T(8,128)(2,1)S(1)} %get-tuple-element.63), channel_id=1, source_target_pairs={{0,16},{4,20},{8,24},{12,28},{16,0},{20,4},{24,8},{28,12},{1,17},{... | collective-permute-start | bytes 786440 | tf_op jit(solution)/shard_map/ppermute | solution.py:14
  100.8 13.4 %collective-permute-start.26 = (bf16[112,1024]{1,0:T(8,128)(2,1)S(1)}, bf16[112,1024]{1,0:T(8,128)(2,1)S(1)}, u32[]{:S(2)}, u32[]{:S(2)}) collective-permute-start(bf16[112,1024]{1,0:T(8,128)(2,1)S(1)} %get-tuple-element.65), channel_id=1, source_target_pairs={{0,16},{4,20},{8,24},{12,28},{16,0},{20,4},{24,8},{28,12},{1,17},{... | collective-permute-start | bytes 688136 | tf_op jit(solution)/shard_map/ppermute | solution.py:14
  102.5 9.3 %collective-permute-start.22 = (bf16[48,1024]{1,0:T(8,128)(2,1)S(1)}, bf16[48,1024]{1,0:T(8,128)(2,1)S(1)}, u32[]{:S(2)}, u32[]{:S(2)}) collective-permute-start(bf16[48,1024]{1,0:T(8,128)(2,1)S(1)} %dynamic-slice_convert_fusion.9), channel_id=1, source_target_pairs={{0,2},{1,3},{2,0},{3,1},{4,6},{5,7},{6,4},{7,5},{8,10},{9,11},{10,... | collective-permute-start | bytes 294920 | tf_op jit(solution)/shard_map/ppermute | solution.py:14
  106.2 7.2 %collective-permute-start.24 = (bf16[32,1024]{1,0:T(8,128)(2,1)S(1)}, bf16[32,1024]{1,0:T(8,128)(2,1)S(1)}, u32[]{:S(2)}, u32[]{:S(2)}) collective-permute-start(bf16[32,1024]{1,0:T(8,128)(2,1)S(1)} %dynamic-slice_convert_fusion.12), channel_id=1, source_target_pairs={{0,2},{1,3},{2,0},{3,1},{4,6},{5,7},{6,4},{7,5},{8,10},{9,11},{10,... | collective-permute-start | bytes 196616 | tf_op jit(solution)/shard_map/ppermute | solution.py:14
  109.8 5.7 %collective-permute-start.27 = (bf16[64,1024]{1,0:T(8,128)(2,1)S(1)}, bf16[64,1024]{1,0:T(8,128)(2,1)S(1)}, u32[]{:S(2)}, u32[]{:S(2)}) collective-permute-start(bf16[64,1024]{1,0:T(8,128)(2,1)S(1)} %get-tuple-element.75), channel_id=1, source_target_pairs={{0,16},{4,20},{8,24},{12,28},{16,0},{20,4},{24,8},{28,12},{1,17},{... | collective-permute-start | bytes 393224 | tf_op jit(solution)/shard_map/ppermute | solution.py:14
  111.9 4.7 %collective-permute-start.28 = (bf16[48,1024]{1,0:T(8,128)(2,1)S(1)}, bf16[48,1024]{1,0:T(8,128)(2,1)S(1)}, u32[]{:S(2)}, u32[]{:S(2)}) collective-permute-start(bf16[48,1024]{1,0:T(8,128)(2,1)S(1)} %get-tuple-element.81), channel_id=1, source_target_pairs={{0,16},{4,20},{8,24},{12,28},{16,0},{20,4},{24,8},{28,12},{1,17},{... | collective-permute-start | bytes 294920 | tf_op jit(solution)/shard_map/ppermute | solution.py:14
  113.5 4.3 %collective-permute-start.29 = (bf16[32,1024]{1,0:T(8,128)(2,1)S(1)}, bf16[32,1024]{1,0:T(8,128)(2,1)S(1)}, u32[]{:S(2)}, u32[]{:S(2)}) collective-permute-start(bf16[32,1024]{1,0:T(8,128)(2,1)S(1)} %get-tuple-element.83), channel_id=1, source_target_pairs={{0,16},{4,20},{8,24},{12,28},{16,0},{20,4},{24,8},{28,12},{1,17},{... | collective-permute-start | bytes 196616 | tf_op jit(solution)/shard_map/ppermute | solution.py:14
  (5 other events, 44.5 us)
